TPU v7x, 32 devices: a whole 2x2x4 slice. The times are simulated.
32 devices in a mesh: band: 4 (over y, x), slab: 8 (over z, core).
Axes of the slice: x: 2, y: 2, z: 4, core: 2. Of those that a mesh axis runs over, the one named last changes fastest.
Arguments:
- wavefunctions: float32 [4, 128, 128, 128], P('band', 'slab'), may hold values from -6 to 6
Outputs:
- exchange_field: float32 [4, 128, 128, 128], P('band', 'slab')
All inputs are finite; a program needn't handle non-finite values.
Results may differ from a plain program's by a relative error of at most 0.0003.
Values sent between devices are 32-bit elements; how exact they have to be, the bound alone decides.
No kernel may reach another device: no remote copies, remote signals or barrier semaphores. Data moves between devices by JAX's collectives and lax.ppermute only.
A program may use at most 64 MiB of HBM per device.

v0:
```python
import math

import jax
import jax.numpy as jnp
import numpy as np
from jax import lax
from jax.sharding import PartitionSpec as P

HIGHEST_MODE = lax.Precision.HIGHEST


def shifted(value, axis, steps):
    count = lax.axis_size(axis)
    pairs = [(source, (source + steps) % count) for source in range(count)]
    return lax.ppermute(value, axis, pairs)


def dft_tables(length):
    positions = jnp.arange(length, dtype=jnp.int32)
    product = positions[:, None] * positions[None, :] % length
    angles = 2.0 * math.pi / length * product.astype(jnp.float32)
    return (jnp.cos(angles), jnp.sin(angles))


def apply_table(form, field, table):
    return jnp.einsum(form, field, table, precision=HIGHEST_MODE)


def transform(real_part, imag_part, cosine_table, sine_table, form, inverse):
    real_cos = apply_table(form, real_part, cosine_table)
    real_sin = apply_table(form, real_part, sine_table)
    if imag_part is None:
        return (real_cos, -real_sin)
    imag_cos = apply_table(form, imag_part, cosine_table)
    imag_sin = apply_table(form, imag_part, sine_table)
    if inverse:
        return (real_cos - imag_sin, imag_cos + real_sin)
    return (real_cos + imag_sin, imag_cos - real_sin)


def fold_freq(values, length):
    return jnp.where(values < length // 2, values, values - length).astype(jnp.float32)


def coulomb_kernel(length, y_rows, y_start):
    all_freq = fold_freq(jnp.arange(length, dtype=jnp.int32), length)
    local_freq = fold_freq(y_start + jnp.arange(y_rows, dtype=jnp.int32), length)
    squared = (
        all_freq[:, None, None] ** 2 + local_freq[None, :, None] ** 2 + all_freq[None, None, :] ** 2
    )
    kernel_scale = length**1.5 / 4.0 / float(length) ** 3
    return jnp.where(squared > 0, kernel_scale / jnp.maximum(squared, 1.0), 0.0)


def potentials(density):
    length = density.shape[2]
    cosine_table, sine_table = dft_tables(length)
    y_rows = length // lax.axis_size("slab")
    z_form = "pxyn,nk->pxyk"
    y_form = "pxnz,nk->pxkz"
    x_form = "pnyz,nk->pkyz"
    spec_real, spec_imag = transform(density, None, cosine_table, sine_table, z_form, False)
    spec_real, spec_imag = transform(spec_real, spec_imag, cosine_table, sine_table, y_form, False)
    kernel = coulomb_kernel(length, y_rows, lax.axis_index("slab") * y_rows)
    part_real, part_imag = transform(
        lax.all_to_all(spec_real, "slab", split_axis=2, concat_axis=1, tiled=True),
        lax.all_to_all(spec_imag, "slab", split_axis=2, concat_axis=1, tiled=True),
        cosine_table,
        sine_table,
        x_form,
        False,
    )
    part_real = part_real * kernel
    part_imag = part_imag * kernel
    part_real, part_imag = transform(part_real, part_imag, cosine_table, sine_table, x_form, True)
    spec_real = lax.all_to_all(part_real, "slab", split_axis=1, concat_axis=2, tiled=True)
    spec_imag = lax.all_to_all(part_imag, "slab", split_axis=1, concat_axis=2, tiled=True)
    spec_real, spec_imag = transform(spec_real, spec_imag, cosine_table, sine_table, y_form, True)
    real_cos = apply_table(z_form, spec_real, cosine_table)
    imag_sin = apply_table(z_form, spec_imag, sine_table)
    return real_cos - imag_sin


def select_sum(selector, fields):
    return jnp.einsum("pb,pxyz->bxyz", selector, fields, precision=HIGHEST_MODE)


def per_device(wavefunctions):
    band_count = wavefunctions.shape[0]
    columns = lax.axis_size("band")
    half_loop = columns // 2
    left_index, right_index = np.triu_indices(band_count)
    left_select = (left_index[:, None] == np.arange(band_count)[None, :]).astype(np.float32)
    right_select = (
        (right_index[:, None] == np.arange(band_count)[None, :])
        & (left_index != right_index)[:, None]
    ).astype(np.float32)
    local_pots = potentials(wavefunctions[left_index] * wavefunctions[right_index])
    total_sum = select_sum(jnp.asarray(left_select), local_pots * wavefunctions[right_index])
    total_sum = total_sum + select_sum(
        jnp.asarray(right_select), local_pots * wavefunctions[left_index]
    )
    field_shape = wavefunctions.shape[1:]
    visitor = wavefunctions
    carried = jnp.zeros_like(wavefunctions)
    for shift_step in range(1, half_loop + 1):
        visitor, carried = shifted((visitor, carried), "band", 1)
        pair_density = (wavefunctions[:, None] * visitor[None, :]).reshape(
            (band_count * band_count,) + field_shape
        )
        pair_pots = potentials(pair_density).reshape((band_count, band_count) + field_shape)
        total_sum = total_sum + jnp.sum(pair_pots * visitor[None, :], axis=1)
        if shift_step < half_loop:
            contrib = jnp.sum(pair_pots * wavefunctions[:, None], axis=0)
        else:
            contrib = jnp.zeros_like(wavefunctions)
        carried = carried + contrib
    total_sum = total_sum + shifted(carried, "band", -half_loop)
    return -0.25 * total_sum


def solution(mesh):
    in_specs = (P("band", "slab", None, None),)
    out_specs = P("band", "slab", None, None)
    return jax.shard_map(
        per_device, mesh=mesh, in_specs=in_specs, out_specs=out_specs, check_vma=False
    )
```

profile of v0, /device:TPU:0, one launch (start us, length us, event | category | flops | bytes accessed | tf_op | source)
XLA Modules:
  0.0 418.8 jit_solution(9022010832290226636)
XLA Ops:
  7.9 6.3 %all-to-all-start = ((f32[1,16,128,128]{3,1,0,2:T(8,128)}), f32[1,16,128,128]{3,1,0,2:T(8,128)}, u32[]{:S(2)}, u32[]{:S(2)}) async-start(f32[1,16,128,128]{3,1,0,2:T(8,128)} %copy.72), calls=%async_computation | async-start | bytes 2097152 | tf_op jit(solution)/shard_map/all_to_all | solution.py:66
  20.0 21.0 %all-to-all-done = f32[1,16,128,128]{3,1,0,2:T(8,128)} async-done(((f32[1,16,128,128]{3,1,0,2:T(8,128)}), f32[1,16,128,128]{3,1,0,2:T(8,128)}, u32[]{:S(2)}, u32[]{:S(2)}) %all-to-all-start) | async-done | bytes 1048608 | tf_op jit(solution)/shard_map/all_to_all | solution.py:66
  41.0 4.7 %all-to-all-start.1 = ((f32[1,16,128,128]{3,1,0,2:T(8,128)}), f32[1,16,128,128]{3,1,0,2:T(8,128)}, u32[]{:S(2)}, u32[]{:S(2)}) async-start(f32[1,16,128,128]{3,1,0,2:T(8,128)} %copy.77), calls=%async_computation.1 | async-start | bytes 2097152 | tf_op jit(solution)/shard_map/all_to_all | solution.py:67
  54.8 17.5 %all-to-all-done.1 = f32[1,16,128,128]{3,1,0,2:T(8,128)} async-done(((f32[1,16,128,128]{3,1,0,2:T(8,128)}), f32[1,16,128,128]{3,1,0,2:T(8,128)}, u32[]{:S(2)}, u32[]{:S(2)}) %all-to-all-start.1) | async-done | bytes 1048608 | tf_op jit(solution)/shard_map/all_to_all | solution.py:67
  72.3 4.2 %all-to-all-start.4 = ((f32[1,16,128,128]{3,1,0,2:T(8,128)}), f32[1,16,128,128]{3,1,0,2:T(8,128)}, u32[]{:S(2)}, u32[]{:S(2)}) async-start(f32[1,16,128,128]{3,1,0,2:T(8,128)} %copy.96), calls=%async_computation.4 | async-start | bytes 2097152 | tf_op jit(solution)/shard_map/all_to_all | solution.py:66
  80.8 22.3 %all-to-all-done.4 = f32[1,16,128,128]{3,1,0,2:T(8,128)} async-done(((f32[1,16,128,128]{3,1,0,2:T(8,128)}), f32[1,16,128,128]{3,1,0,2:T(8,128)}, u32[]{:S(2)}, u32[]{:S(2)}) %all-to-all-start.4) | async-done | bytes 1048608 | tf_op jit(solution)/shard_map/all_to_all | solution.py:66
  119.3 14.1 %all-to-all-done.5 = f32[1,16,128,128]{3,1,0,2:T(8,128)S(1)} async-done(((f32[1,16,128,128]{3,1,0,2:T(8,128)}), f32[1,16,128,128]{3,1,0,2:T(8,128)S(1)}, u32[]{:S(2)}, u32[]{:S(2)}) %all-to-all-start.5) | async-done | bytes 1048608 | tf_op jit(solution)/shard_map/all_to_all | solution.py:67
  134.4 4.2 %all-to-all-start.2 = ((f32[1,128,16,128]{3,2,0,1:T(8,128)}), f32[1,128,16,128]{3,2,0,1:T(8,128)}, u32[]{:S(2)}, u32[]{:S(2)}) async-start(f32[1,128,16,128]{3,2,0,1:T(8,128)} %copy.84), calls=%async_computation.2 | async-start | bytes 2097152 | tf_op jit(solution)/shard_map/all_to_all | solution.py:76
  145.6 19.6 %all-to-all-done.2 = f32[1,128,16,128]{3,2,0,1:T(8,128)} async-done(((f32[1,128,16,128]{3,2,0,1:T(8,128)}), f32[1,128,16,128]{3,2,0,1:T(8,128)}, u32[]{:S(2)}, u32[]{:S(2)}) %all-to-all-start.2) | async-done | bytes 1048608 | tf_op jit(solution)/shard_map/all_to_all | solution.py:76
  165.2 4.5 %all-to-all-start.3 = ((f32[1,128,16,128]{3,2,0,1:T(8,128)}), f32[1,128,16,128]{3,2,0,1:T(8,128)}, u32[]{:S(2)}, u32[]{:S(2)}) async-start(f32[1,128,16,128]{3,2,0,1:T(8,128)} %copy.89), calls=%async_computation.3 | async-start | bytes 2097152 | tf_op jit(solution)/shard_map/all_to_all | solution.py:77
  177.7 18.6 %all-to-all-done.3 = f32[1,128,16,128]{3,2,0,1:T(8,128)} async-done(((f32[1,128,16,128]{3,2,0,1:T(8,128)}), f32[1,128,16,128]{3,2,0,1:T(8,128)}, u32[]{:S(2)}, u32[]{:S(2)}) %all-to-all-start.3) | async-done | bytes 1048608 | tf_op jit(solution)/shard_map/all_to_all | solution.py:77
  204.7 22.4 %all-to-all-done.8 = f32[1,16,128,128]{3,1,0,2:T(8,128)} async-done(((f32[1,16,128,128]{3,1,0,2:T(8,128)}), f32[1,16,128,128]{3,1,0,2:T(8,128)}, u32[]{:S(2)}, u32[]{:S(2)}) %all-to-all-start.8) | async-done | bytes 1048608 | tf_op jit(solution)/shard_map/all_to_all | solution.py:66
  227.1 4.7 %all-to-all-start.9 = ((f32[1,16,128,128]{3,1,0,2:T(8,128)}), f32[1,16,128,128]{3,1,0,2:T(8,128)}, u32[]{:S(2)}, u32[]{:S(2)}) async-start(f32[1,16,128,128]{3,1,0,2:T(8,128)} %copy.125), calls=%async_computation.9 | async-start | bytes 2097152 | tf_op jit(solution)/shard_map/all_to_all | solution.py:67
  243.2 15.2 %all-to-all-done.9 = f32[1,16,128,128]{3,1,0,2:T(8,128)} async-done(((f32[1,16,128,128]{3,1,0,2:T(8,128)}), f32[1,16,128,128]{3,1,0,2:T(8,128)}, u32[]{:S(2)}, u32[]{:S(2)}) %all-to-all-start.9) | async-done | bytes 1048608 | tf_op jit(solution)/shard_map/all_to_all | solution.py:67
  258.3 4.2 %all-to-all-start.6 = ((f32[1,128,16,128]{3,2,0,1:T(8,128)}), f32[1,128,16,128]{3,2,0,1:T(8,128)}, u32[]{:S(2)}, u32[]{:S(2)}) async-start(f32[1,128,16,128]{3,2,0,1:T(8,128)} %copy.108), calls=%async_computation.6 | async-start | bytes 2097152 | tf_op jit(solution)/shard_map/all_to_all | solution.py:76
  272.0 17.1 %all-to-all-done.6 = f32[1,128,16,128]{3,2,0,1:T(8,128)} async-done(((f32[1,128,16,128]{3,2,0,1:T(8,128)}), f32[1,128,16,128]{3,2,0,1:T(8,128)}, u32[]{:S(2)}, u32[]{:S(2)}) %all-to-all-start.6) | async-done | bytes 1048608 | tf_op jit(solution)/shard_map/all_to_all | solution.py:76
  289.2 4.4 %all-to-all-start.7 = ((f32[1,128,16,128]{3,2,0,1:T(8,128)}), f32[1,128,16,128]{3,2,0,1:T(8,128)}, u32[]{:S(2)}, u32[]{:S(2)}) async-start(f32[1,128,16,128]{3,2,0,1:T(8,128)} %copy.113), calls=%async_computation.7 | async-start | bytes 2097152 | tf_op jit(solution)/shard_map/all_to_all | solution.py:77
  308.3 11.9 %all-to-all-done.7 = f32[1,128,16,128]{3,2,0,1:T(8,128)} async-done(((f32[1,128,16,128]{3,2,0,1:T(8,128)}), f32[1,128,16,128]{3,2,0,1:T(8,128)}, u32[]{:S(2)}, u32[]{:S(2)}) %all-to-all-start.7) | async-done | bytes 1048608 | tf_op jit(solution)/shard_map/all_to_all | solution.py:77
  320.2 4.5 %all-to-all-start.10 = ((f32[1,128,16,128]{3,2,0,1:T(8,128)}), f32[1,128,16,128]{3,2,0,1:T(8,128)}, u32[]{:S(2)}, u32[]{:S(2)}) async-start(f32[1,128,16,128]{3,2,0,1:T(8,128)} %copy.132), calls=%async_computation.10 | async-start | bytes 2097152 | tf_op jit(solution)/shard_map/all_to_all | solution.py:76
  341.1 10.2 %all-to-all-done.10 = f32[1,128,16,128]{3,2,0,1:T(8,128)} async-done(((f32[1,128,16,128]{3,2,0,1:T(8,128)}), f32[1,128,16,128]{3,2,0,1:T(8,128)}, u32[]{:S(2)}, u32[]{:S(2)}) %all-to-all-start.10) | async-done | bytes 1048608 | tf_op jit(solution)/shard_map/all_to_all | solution.py:76
  351.3 4.2 %all-to-all-start.11 = ((f32[1,128,16,128]{3,2,0,1:T(8,128)}), f32[1,128,16,128]{3,2,0,1:T(8,128)}, u32[]{:S(2)}, u32[]{:S(2)}) async-start(f32[1,128,16,128]{3,2,0,1:T(8,128)} %copy.137), calls=%async_computation.11 | async-start | bytes 2097152 | tf_op jit(solution)/shard_map/all_to_all | solution.py:77
  369.8 12.3 %all-to-all-done.11 = f32[1,128,16,128]{3,2,0,1:T(8,128)} async-done(((f32[1,128,16,128]{3,2,0,1:T(8,128)}), f32[1,128,16,128]{3,2,0,1:T(8,128)}, u32[]{:S(2)}, u32[]{:S(2)}) %all-to-all-start.11) | async-done | bytes 1048608 | tf_op jit(solution)/shard_map/all_to_all | solution.py:77
  384.7 5.1 %collective-permute-done.3 = f32[1,16,128,128]{3,2,1,0:T(8,128)} collective-permute-done((f32[1,16,128,128]{3,2,1,0:T(8,128)}, f32[1,16,128,128]{3,2,1,0:T(8,128)}, u32[]{:S(2)}, u32[]{:S(2)}) %collective-permute-start.3) | collective-permute-done | bytes 1048608 | tf_op jit(solution)/shard_map/ppermute | solution.py:15
  396.5 18.2 %collective-permute-done.4 = f32[1,16,128,128]{3,2,1,0:T(8,128)S(1)} collective-permute-done((f32[1,16,128,128]{3,2,1,0:T(8,128)}, f32[1,16,128,128]{3,2,1,0:T(8,128)S(1)}, u32[]{:S(2)}, u32[]{:S(2)}) %collective-permute-start.4) | collective-permute-done | bytes 1048608 | tf_op jit(solution)/shard_map/ppermute | solution.py:15
  (124 shorter events, 146.0 us)
Async XLA Ops:
  0.0 2.5 copy-start
  7.9 33.0 %all-to-all-start = ((f32[1,16,128,128]{3,1,0,2:T(8,128)}), f32[1,16,128,128]{3,1,0,2:T(8,128)}, u32[]{:S(2)}, u32[]{:S(2)}) async-start(f32[1,16,128,128]{3,1,0,2:T(8,128)} %copy.72), calls=%async_computation | async-start | bytes 2097152 | tf_op jit(solution)/shard_map/all_to_all | solution.py:66
  14.3 31.4 %collective-permute-start = (f32[1,16,128,128]{3,2,1,0:T(8,128)S(1)}, f32[1,16,128,128]{3,2,1,0:T(8,128)}, u32[]{:S(2)}, u32[]{:S(2)}) collective-permute-start(f32[1,16,128,128]{3,2,1,0:T(8,128)S(1)} %copy-done), channel_id=1, source_target_pairs={{0,8},{8,16},{16,24},{24,0},{1,9},{9,17},{17,25},{25,1},{2,10},{10... | collective-permute-start | bytes 3145736 | tf_op jit(solution)/shard_map/ppermute | solution.py:15
  41.0 31.3 %all-to-all-start.1 = ((f32[1,16,128,128]{3,1,0,2:T(8,128)}), f32[1,16,128,128]{3,1,0,2:T(8,128)}, u32[]{:S(2)}, u32[]{:S(2)}) async-start(f32[1,16,128,128]{3,1,0,2:T(8,128)} %copy.77), calls=%async_computation.1 | async-start | bytes 2097152 | tf_op jit(solution)/shard_map/all_to_all | solution.py:67
  72.3 30.8 %all-to-all-start.4 = ((f32[1,16,128,128]{3,1,0,2:T(8,128)}), f32[1,16,128,128]{3,1,0,2:T(8,128)}, u32[]{:S(2)}, u32[]{:S(2)}) async-start(f32[1,16,128,128]{3,1,0,2:T(8,128)} %copy.96), calls=%async_computation.4 | async-start | bytes 2097152 | tf_op jit(solution)/shard_map/all_to_all | solution.py:66
  103.1 30.2 %all-to-all-start.5 = ((f32[1,16,128,128]{3,1,0,2:T(8,128)}), f32[1,16,128,128]{3,1,0,2:T(8,128)S(1)}, u32[]{:S(2)}, u32[]{:S(2)}) async-start(f32[1,16,128,128]{3,1,0,2:T(8,128)} %copy.101), calls=%async_computation.5 | async-start | bytes 2097152 | tf_op jit(solution)/shard_map/all_to_all | solution.py:67
  134.4 30.8 %all-to-all-start.2 = ((f32[1,128,16,128]{3,2,0,1:T(8,128)}), f32[1,128,16,128]{3,2,0,1:T(8,128)}, u32[]{:S(2)}, u32[]{:S(2)}) async-start(f32[1,128,16,128]{3,2,0,1:T(8,128)} %copy.84), calls=%async_computation.2 | async-start | bytes 2097152 | tf_op jit(solution)/shard_map/all_to_all | solution.py:76
  138.6 31.1 %collective-permute-start.1 = (f32[1,16,128,128]{3,2,1,0:T(8,128)}, f32[1,16,128,128]{3,2,1,0:T(8,128)S(1)}, u32[]{:S(2)}, u32[]{:S(2)}) collective-permute-start(f32[1,16,128,128]{3,2,1,0:T(8,128)} %collective-permute-done), channel_id=1, source_target_pairs={{0,8},{8,16},{16,24},{24,0},{1,9},{9,17},{17,25},{25,1},{2,10},{10... | collective-permute-start | bytes 3145736 | tf_op jit(solution)/shard_map/ppermute | solution.py:15
  165.2 31.1 %all-to-all-start.3 = ((f32[1,128,16,128]{3,2,0,1:T(8,128)}), f32[1,128,16,128]{3,2,0,1:T(8,128)}, u32[]{:S(2)}, u32[]{:S(2)}) async-start(f32[1,128,16,128]{3,2,0,1:T(8,128)} %copy.89), calls=%async_computation.3 | async-start | bytes 2097152 | tf_op jit(solution)/shard_map/all_to_all | solution.py:77
  196.3 30.8 %all-to-all-start.8 = ((f32[1,16,128,128]{3,1,0,2:T(8,128)}), f32[1,16,128,128]{3,1,0,2:T(8,128)}, u32[]{:S(2)}, u32[]{:S(2)}) async-start(f32[1,16,128,128]{3,1,0,2:T(8,128)} %copy.120), calls=%async_computation.8 | async-start | bytes 2097152 | tf_op jit(solution)/shard_map/all_to_all | solution.py:66
  227.1 31.2 %all-to-all-start.9 = ((f32[1,16,128,128]{3,1,0,2:T(8,128)}), f32[1,16,128,128]{3,1,0,2:T(8,128)}, u32[]{:S(2)}, u32[]{:S(2)}) async-start(f32[1,16,128,128]{3,1,0,2:T(8,128)} %copy.125), calls=%async_computation.9 | async-start | bytes 2097152 | tf_op jit(solution)/shard_map/all_to_all | solution.py:67
  231.7 1.5 copy-start.12
  258.3 30.8 %all-to-all-start.6 = ((f32[1,128,16,128]{3,2,0,1:T(8,128)}), f32[1,128,16,128]{3,2,0,1:T(8,128)}, u32[]{:S(2)}, u32[]{:S(2)}) async-start(f32[1,128,16,128]{3,2,0,1:T(8,128)} %copy.108), calls=%async_computation.6 | async-start | bytes 2097152 | tf_op jit(solution)/shard_map/all_to_all | solution.py:76
  263.7 95.7 %collective-permute-start.2 = (f32[1,16,128,128]{3,2,1,0:T(8,128)}, f32[1,16,128,128]{3,2,1,0:T(8,128)}, u32[]{:S(2)}, u32[]{:S(2)}) collective-permute-start(f32[1,16,128,128]{3,2,1,0:T(8,128)} %broadcast_in_dim.27), channel_id=1, source_target_pairs={{0,8},{8,16},{16,24},{24,0},{1,9},{9,17},{17,25},{25,1},{2,10},{10... | collective-permute-start | bytes 3145736 | tf_op jit(solution)/shard_map/ppermute | solution.py:15
  289.2 31.0 %all-to-all-start.7 = ((f32[1,128,16,128]{3,2,0,1:T(8,128)}), f32[1,128,16,128]{3,2,0,1:T(8,128)}, u32[]{:S(2)}, u32[]{:S(2)}) async-start(f32[1,128,16,128]{3,2,0,1:T(8,128)} %copy.113), calls=%async_computation.7 | async-start | bytes 2097152 | tf_op jit(solution)/shard_map/all_to_all | solution.py:77
  320.2 31.1 %all-to-all-start.10 = ((f32[1,128,16,128]{3,2,0,1:T(8,128)}), f32[1,128,16,128]{3,2,0,1:T(8,128)}, u32[]{:S(2)}, u32[]{:S(2)}) async-start(f32[1,128,16,128]{3,2,0,1:T(8,128)} %copy.132), calls=%async_computation.10 | async-start | bytes 2097152 | tf_op jit(solution)/shard_map/all_to_all | solution.py:76
  326.0 2.3 copy-start.8
  351.3 30.8 %all-to-all-start.11 = ((f32[1,128,16,128]{3,2,0,1:T(8,128)}), f32[1,128,16,128]{3,2,0,1:T(8,128)}, u32[]{:S(2)}, u32[]{:S(2)}) async-start(f32[1,128,16,128]{3,2,0,1:T(8,128)} %copy.137), calls=%async_computation.11 | async-start | bytes 2097152 | tf_op jit(solution)/shard_map/all_to_all | solution.py:77
  355.5 2.6 copy-start.10
  359.4 5.3 %copy-start.4 = (f32[16,128,128]{2,1,0:T(8,128)S(1)}, f32[16,128,128]{2,1,0:T(8,128)}, u32[]{:S(2)}) copy-start(f32[16,128,128]{2,1,0:T(8,128)} %fusion.19) | copy-start | bytes 3145732
  362.9 3.0 copy-start.3
  362.9 26.9 %collective-permute-start.3 = (f32[1,16,128,128]{3,2,1,0:T(8,128)}, f32[1,16,128,128]{3,2,1,0:T(8,128)}, u32[]{:S(2)}, u32[]{:S(2)}) collective-permute-start(f32[1,16,128,128]{3,2,1,0:T(8,128)} %get-tuple-element.5), channel_id=1, source_target_pairs={{0,8},{8,16},{16,24},{24,0},{1,9},{9,17},{17,25},{25,1},{2,10},{10... | collective-permute-start | bytes 3145736 | tf_op jit(solution)/shard_map/ppermute | solution.py:15
  389.8 24.8 %collective-permute-start.4 = (f32[1,16,128,128]{3,2,1,0:T(8,128)}, f32[1,16,128,128]{3,2,1,0:T(8,128)S(1)}, u32[]{:S(2)}, u32[]{:S(2)}) collective-permute-start(f32[1,16,128,128]{3,2,1,0:T(8,128)} %collective-permute-done.3), channel_id=1, source_target_pairs={{0,16},{8,24},{16,0},{24,8},{1,17},{9,25},{17,1},{25,9},{2,18},{10... | collective-permute-start | bytes 3145736 | tf_op jit(solution)/shard_map/ppermute | solution.py:15
  395.2 19.5 %copy-start.2 = (f32[1,16,128,128]{3,2,1,0:T(8,128)S(1)}, f32[1,16,128,128]{3,2,1,0:T(8,128)}, u32[]{:S(2)}) copy-start(f32[1,16,128,128]{3,2,1,0:T(8,128)} %copy-done.1) | copy-start | bytes 3145732
  (6 other events, 7.4 us)
where the time goes:
time: 427 us; the launch traced here: 419 us
  waiting for transfers between devices  225 us (53%)
  matrix products  93.8 us (22%)
  starting transfers between devices  61.7 us (14%)
  local copies, waits for them, and re-layouts  36.4 us (9%)
    dot_general x60, matrix products, apply_table(): return jnp.einsum(form, field, table, precision=HIGHEST_MODE)  93.8 us
    all_to_all x3, waiting for transfers between devices, potentials(): lax.all_to_all(spec_real, 'slab', split_axis=2, concat_axis=1, tiled=True)  65.7 us
    all_to_all x3, waiting for transfers between devices, potentials(): lax.all_to_all(part_real, 'slab', split_axis=1, concat_axis=2, tiled=True)  47 us
    all_to_all x3, waiting for transfers between devices, potentials(): lax.all_to_all(spec_imag, 'slab', split_axis=2, concat_axis=1, tiled=True)  46.7 us
    all_to_all x3, waiting for transfers between devices, potentials(): lax.all_to_all(part_imag, 'slab', split_axis=1, concat_axis=2, tiled=True)  42.8 us
    ppermute x5, waiting for transfers between devices, shifted(): return lax.ppermute(value, axis, pairs)  23.3 us
    all_to_all x3, starting transfers between devices, potentials(): lax.all_to_all(spec_real, 'slab', split_axis=2, concat_axis=1, tiled=True)  14.8 us
    all_to_all x3, starting transfers between devices, potentials(): lax.all_to_all(part_imag, 'slab', split_axis=1, concat_axis=2, tiled=True)  13.1 us
  transfers between devices with their start and end apart: 17, of which 14 were waited for; matrix products, arithmetic and copies ran while one was open for 28% of the time, Pallas kernels for 0%

commit v1 on v0

v1 whole, which is shorter than its diff:
```python
import functools

import jax
import jax.numpy as jnp
import numpy as np
from jax import lax
from jax.experimental import pallas as pl
from jax.experimental.pallas import tpu as pltpu
from jax.sharding import PartitionSpec as P

HIGHEST_MODE = lax.Precision.HIGHEST
VMEM_LIMIT = 32 * 1024 * 1024


def cas_table(length):
    positions = np.arange(length)
    angles = 2.0 * np.pi / length * (positions[:, None] * positions[None, :] % length)
    return (np.cos(angles) + np.sin(angles)).astype(np.float32)


def squared_freqs(length):
    positions = np.arange(length)
    return (np.minimum(positions, length - positions) ** 2).astype(np.float32)


def coulomb(squared, length):
    kernel_scale = -0.25 * length**1.5 / 4.0 / float(length) ** 3
    return jnp.where(squared > 0, kernel_scale / jnp.maximum(squared, 1.0), 0.0)


def shifted(value, axis, steps):
    count = lax.axis_size(axis)
    pairs = [(source, (source + steps) % count) for source in range(count)]
    return lax.ppermute(value, axis, pairs)


def apply_table(form, field, table):
    return jnp.einsum(form, field, table, precision=HIGHEST_MODE)


def potentials(density):
    length = density.shape[2]
    table = jnp.asarray(cas_table(length))
    y_rows = length // lax.axis_size("slab")
    z_form = "pxyn,nk->pxyk"
    y_form = "pxnz,nk->pxkz"
    x_form = "pnyz,nk->pkyz"
    squared = jnp.asarray(squared_freqs(length))
    own_squared = lax.dynamic_slice_in_dim(squared, lax.axis_index("slab") * y_rows, y_rows)
    spec = apply_table(y_form, apply_table(z_form, density, table), table)
    spec = lax.all_to_all(spec, "slab", split_axis=2, concat_axis=1, tiled=True)
    spec = apply_table(x_form, spec, table) * coulomb(
        squared[:, None, None] + own_squared[None, :, None] + squared[None, None, :], length
    )
    spec = apply_table(x_form, spec, table)
    spec = lax.all_to_all(spec, "slab", split_axis=1, concat_axis=2, tiled=True)
    return apply_table(z_form, apply_table(y_form, spec, table), table)


def select_sum(selector, fields):
    return jnp.einsum("pb,pxyz->bxyz", selector, fields, precision=HIGHEST_MODE)


def general_device(wavefunctions):
    band_count = wavefunctions.shape[0]
    columns = lax.axis_size("band")
    half_loop = columns // 2
    left_index, right_index = np.triu_indices(band_count)
    left_select = (left_index[:, None] == np.arange(band_count)[None, :]).astype(np.float32)
    right_select = (
        (right_index[:, None] == np.arange(band_count)[None, :])
        & (left_index != right_index)[:, None]
    ).astype(np.float32)
    local_pots = potentials(wavefunctions[left_index] * wavefunctions[right_index])
    total_sum = select_sum(jnp.asarray(left_select), local_pots * wavefunctions[right_index])
    total_sum = total_sum + select_sum(
        jnp.asarray(right_select), local_pots * wavefunctions[left_index]
    )
    field_shape = wavefunctions.shape[1:]
    visitor = wavefunctions
    carried = jnp.zeros_like(wavefunctions)
    for shift_step in range(1, half_loop + 1):
        visitor, carried = shifted((visitor, carried), "band", 1)
        pair_density = (wavefunctions[:, None] * visitor[None, :]).reshape(
            (band_count * band_count,) + field_shape
        )
        pair_pots = potentials(pair_density).reshape((band_count, band_count) + field_shape)
        total_sum = total_sum + jnp.sum(pair_pots * visitor[None, :], axis=1)
        if shift_step < half_loop:
            contrib = jnp.sum(pair_pots * wavefunctions[:, None], axis=0)
        else:
            contrib = jnp.zeros_like(wavefunctions)
        carried = carried + contrib
    return total_sum + shifted(carried, "band", -half_loop)


def split_parts(value):
    high = value.astype(jnp.bfloat16)
    low = (value - high.astype(jnp.float32)).astype(jnp.bfloat16)
    return high, low


def product(left, right):
    return jnp.dot(left, right, preferred_element_type=jnp.float32)


def left_table(table):
    high, low = split_parts(table)
    if table.shape[1] <= 64:
        return jnp.concatenate([high, high, low], axis=1)
    return jnp.concatenate(
        [
            jnp.concatenate([high, high], axis=1),
            jnp.concatenate([low, jnp.zeros_like(low)], axis=1),
        ],
        axis=0,
    )


def left_apply(parts, value):
    high, low = split_parts(value)
    if value.shape[0] <= 64:
        return product(parts, jnp.concatenate([high, low, high], axis=0))
    both = product(parts, jnp.concatenate([high, low], axis=0))
    rows = parts.shape[0] // 2
    return both[:rows] + both[rows:]


def right_table(table):
    high, low = split_parts(table)
    return jnp.concatenate(
        [
            jnp.concatenate([high, low], axis=1),
            jnp.concatenate([high, jnp.zeros_like(low)], axis=1),
        ],
        axis=0,
    )


def right_apply(value, parts):
    both = product(jnp.concatenate(split_parts(value), axis=1), parts)
    columns = parts.shape[1] // 2
    return both[:, :columns] + both[:, columns:]


def two_planes(ref, first):
    return jnp.concatenate([ref[first], ref[first + 1]], axis=1)


def store_two(ref, first, value):
    length = ref.shape[2]
    ref[first] = value[:, :length]
    ref[first + 1] = value[:, length:]


def partner_masks(slabs):
    far = list(range(slabs - 1, slabs // 2 - 1, -1))
    near = list(range(1, slabs // 2)) + [0]
    return [mask for pair in zip(far, near) for mask in pair] if slabs > 1 else [0]


def own_masks(slabs):
    return [chip + core for chip in range(slabs - 2, -1, -2) for core in range(2)]


def masks_of(fields, slabs):
    return own_masks(slabs) if len(fields) == 1 else partner_masks(slabs)


def partner_rows(table_ref, masks, start, size):
    slab = lax.axis_index("slab")
    return jnp.concatenate(
        [
            table_ref[pl.ds(start + lax.bitwise_xor(slab, mask) * size, size), :]
            for mask in masks
        ],
        axis=0,
    )


def half_groups():
    column = lax.axis_index("band")
    return lax.rem(column, 2), lax.div(column, 2)


def group_starts(fields, length):
    if len(fields) == 1:
        return [0]
    return [group * (length // 2) for group in half_groups()]


def y_tables(fields, slabs, table_ref):
    starts = group_starts(fields, table_ref.shape[0])
    size = table_ref.shape[0] // slabs // (1 if len(fields) == 1 else 2)
    masks = masks_of(fields, slabs)
    return [partner_rows(table_ref, masks, start, size) for start in starts]


def forward_kernel(fields, slabs, bands, table_ref, *rest):
    psi_refs, out_refs, held = rest[:bands], rest[bands:-1], rest[-1]
    planes, length = psi_refs[0].shape[:2]
    per_slab = out_refs[0].shape[1]
    rows = held.shape[1] // planes
    y_parts = [left_table(table) for table in y_tables(fields, slabs, table_ref)]
    z_parts = right_table(table_ref[...])
    piece = per_slab * planes
    for first in range(0, planes, 2):
        psi = [two_planes(ref, first) for ref in psi_refs]
        for f, (a, b, group) in enumerate(fields):
            spec = left_apply(y_parts[group], psi[a] * psi[b])
            for side in range(2):
                held[f, pl.ds(first + side, rows, stride=planes), :] = spec[
                    :, side * length : (side + 1) * length
                ]
    for k, ref in enumerate(out_refs):
        for f in range(len(fields)):
            spec = right_apply(held[f, k * piece : (k + 1) * piece, :], z_parts)
            ref[f] = spec.reshape(per_slab, planes, length)


def folded_square(position, length):
    folded = jnp.minimum(position, length - position)
    return (folded * folded).astype(jnp.float32)


def middle_kernel(fields, slabs, table_ref, *rest):
    if len(fields) == 1:
        *chip_refs, swap_ref, kept_ref, swapped_ref = rest
        per_slab = chip_refs[0].shape[1] // 2
        in_refs, out_refs = [], []
        for n, ref in enumerate(chip_refs):
            half = pl.ds(n * per_slab, per_slab)
            in_refs += [ref.at[:, pl.ds(0, per_slab)], swap_ref.at[:, half]]
            out_refs += [kept_ref.at[:, half], swapped_ref.at[:, half]]
    else:
        in_refs, out_refs = rest[:slabs], rest[slabs:]
    _, per_slab, planes, length = in_refs[0].shape
    back_table = partner_rows(table_ref, masks_of(fields, slabs), 0, planes)
    x_parts, back_parts = left_table(back_table.T), left_table(back_table)
    in_plane = folded_square(
        lax.broadcasted_iota(jnp.int32, (length, length), 0), length
    ) + folded_square(lax.broadcasted_iota(jnp.int32, (length, length), 1), length)
    own_start = lax.axis_index("slab") * per_slab
    starts = [start + own_start for start in group_starts(fields, length)]
    for j in range(0, per_slab, 2):
        factors = [
            jnp.concatenate(
                [
                    coulomb(in_plane + folded_square(start + j + side, length), length)
                    for side in range(2)
                ],
                axis=1,
            )
            for start in starts
        ]
        for f, (_, _, group) in enumerate(fields):
            wide = jnp.concatenate(
                [
                    jnp.concatenate([ref[f, j + side] for ref in in_refs], axis=0)
                    for side in range(2)
                ],
                axis=1,
            )
            back = left_apply(back_parts, left_apply(x_parts, wide) * factors[group])
            for k, ref in enumerate(out_refs):
                for side in range(2):
                    ref[f, j + side] = back[
                        k * planes : (k + 1) * planes, side * length : (side + 1) * length
                    ]


def two_potentials(y_parts, held, f, first, planes):
    rows = held.shape[1] // planes
    spec = jnp.concatenate(
        [held[f, pl.ds(first + side, rows, stride=planes), :] for side in range(2)], axis=1
    )
    return left_apply(y_parts, spec)


def backward_kernel(fields, slabs, arrays, bands, table_ref, *rest):
    spec_refs, psi_refs = rest[:arrays], rest[arrays : arrays + bands]
    term_refs, out_refs, held = rest[arrays + bands : -bands - 1], rest[-bands - 1 : -1], rest[-1]
    _, per_slab, planes, length = spec_refs[0].shape
    z_parts = right_table(table_ref[...])
    y_parts = [left_table(table.T) for table in y_tables(fields, slabs, table_ref)]
    rows = per_slab * planes
    for k, ref in enumerate(spec_refs):
        for f in range(len(fields)):
            held[f, k * rows : (k + 1) * rows, :] = right_apply(
                ref[f].reshape(rows, length), z_parts
            )
    for first in range(0, planes, 2):
        psi = [two_planes(ref, first) for ref in psi_refs]
        sums = [None] * bands
        for ref in term_refs:
            term = two_planes(ref, first)
            sums[0] = term if sums[0] is None else sums[0] + term
        for f, (a, b, group) in enumerate(fields):
            pot = two_potentials(y_parts[group], held, f, first, planes)
            for i, j in ((a, b),) if a == b else ((a, b), (b, a)):
                term = pot * psi[j]
                sums[i] = term if sums[i] is None else sums[i] + term
        for ref, total in zip(out_refs, sums):
            store_two(ref, first, total)


def permuted(value, axis, mask):
    count = lax.axis_size(axis)
    return lax.ppermute(value, axis, [(source, source ^ mask) for source in range(count)])


def exchanged(blocks, masks):
    return [
        permuted(block, "slab", mask) if mask else block for block, mask in zip(blocks, masks)
    ]


def paired_device(wavefunctions):
    _, planes, length, _ = wavefunctions.shape
    slabs = lax.axis_size("slab")
    table = jnp.asarray(cas_table(length))

    def call(body, shape, count, held, *operands):
        return pl.pallas_call(
            body,
            out_shape=[jax.ShapeDtypeStruct(shape, jnp.float32)] * count,
            scratch_shapes=[pltpu.VMEM(held, jnp.float32)] if held else [],
            compiler_params=pltpu.CompilerParams(vmem_limit_bytes=VMEM_LIMIT),
        )(table, *operands)

    own_pair = [(0, 0, 0)]
    cross_pairs = [(0, 1, 0), (0, 2, 1), (1, 2, 1)]
    own_rows, cross_rows = length // slabs, length // 2 // slabs
    own_held = (1, length * planes, length)
    cross_held = (3, length // 2 * planes, length)
    own_chips, cross_masks = own_masks(slabs)[::2], partner_masks(slabs)
    own_block = (1, 2 * own_rows, planes, length)
    cross_block = (3, cross_rows, planes, length)
    swap_block = (1, length // 2, planes, length)

    def forward(fields, block, count, held, *bands):
        body = functools.partial(forward_kernel, fields, slabs, len(bands))
        return call(body, block, count, held, *bands)

    def middle(fields, block, count, *blocks):
        body = functools.partial(middle_kernel, fields, slabs)
        return call(body, block, count, None, *blocks)

    def backward(fields, blocks, bands, terms, held):
        body = functools.partial(backward_kernel, fields, slabs, len(blocks), len(bands))
        shape = (planes, length, length)
        return call(body, shape, len(bands), held, *blocks, *bands, *terms)

    psi = wavefunctions[0]
    bands = [psi, permuted(psi, "band", 1), permuted(psi, "band", 2)]
    chips = exchanged(forward(own_pair, own_block, len(own_chips), own_held, psi), own_chips)
    cross_spec = forward(cross_pairs, cross_block, slabs, cross_held, *bands)
    cross_spec = exchanged(cross_spec, cross_masks)
    chips, cross_spec[0] = lax.optimization_barrier((chips, cross_spec[0]))
    swap = jnp.concatenate([chip[:, own_rows:] for chip in chips], axis=1)
    kept, swap = middle(own_pair, swap_block, 2, *chips, permuted(swap, "slab", 1))
    swap = permuted(swap, "slab", 1)
    chips = [
        jnp.concatenate([part[:, n * own_rows : (n + 1) * own_rows] for part in (kept, swap)], axis=1)
        for n in range(len(own_chips))
    ]
    cross_spec = middle(cross_pairs, cross_block, slabs, *cross_spec)
    cross_spec = exchanged(cross_spec, cross_masks)
    chips, cross_spec = lax.optimization_barrier((chips, cross_spec))
    chips = exchanged(chips, own_chips)
    own_sum, to_x, to_y = backward(cross_pairs, cross_spec, bands, [], cross_held)
    sums = [own_sum, permuted(to_x, "band", 1), permuted(to_y, "band", 2)]
    (total,) = backward(own_pair, chips, [psi], sums, own_held)
    return total[None]


def per_device(wavefunctions):
    length = wavefunctions.shape[2]
    columns, slabs = lax.axis_size("band"), lax.axis_size("slab")
    fits = (
        wavefunctions.shape[0] == 1
        and columns == 4
        and length == 128
        and wavefunctions.shape[1] % 8 == 0
        and slabs & (slabs - 1) == 0
        and slabs > 1
        and length % (4 * slabs) == 0
    )
    return paired_device(wavefunctions) if fits else general_device(wavefunctions)


def solution(mesh):
    in_specs = (P("band", "slab", None, None),)
    out_specs = P("band", "slab", None, None)
    return jax.shard_map(
        per_device, mesh=mesh, in_specs=in_specs, out_specs=out_specs, check_vma=False
    )
```

time: 427 us -> 137 us (0.32); the launches traced: 419 us -> 137 us
  waiting for transfers between devices: 225 us -> 80.2 us
  matrix products: 93.8 us -> 0 us
  local copies, waits for them, and re-layouts: 36.4 us -> 3.14 us
  starting transfers between devices: 61.7 us -> 45.1 us
  Pallas kernels: 0 us -> 8.2 us
    all_to_all x12 -> x0, waiting for transfers between devices: 202 us -> none  [the longest x3 65.7 us: potentials(): lax.all_to_all(spec_real, 'slab', split_axis=2, concat_axis=1, tiled=True)]
    dot_general x60 -> x0, matrix products: 93.8 us -> none  [apply_table(): return jnp.einsum(form, field, table, precision=HIGHEST_MODE)]
    ppermute x5 -> x26, waiting for transfers between devices: 23.3 us -> 80.2 us  [permuted(): lax.ppermute(value, axis, [(source, source ^ mask) for source in range(co...]
    all_to_all x12 -> x0, starting transfers between devices: 54 us -> none  [the longest x3 14.8 us: potentials(): lax.all_to_all(spec_real, 'slab', split_axis=2, concat_axis=1, tiled=True)]
    ppermute x5 -> x26, starting transfers between devices: 7.76 us -> 45.1 us  [permuted(): lax.ppermute(value, axis, [(source, source ^ mask) for source in range(co...]
    all_to_all x12 -> x0, local copies, waits for them, and re-layouts: 14.8 us -> none  [the longest x3 4.07 us: potentials(): lax.all_to_all(spec_real, 'slab', split_axis=2, concat_axis=1, tiled=True)]
    sub x6 -> x0, local copies, waits for them, and re-layouts: 9.73 us -> none  [the longest x3 4.86 us: transform(): return (real_cos - imag_sin, imag_cos + real_sin)]
    add x6 -> x0, local copies, waits for them, and re-layouts: 9.67 us -> none  [the longest x3 4.86 us: transform(): return (real_cos + imag_sin, imag_cos - real_sin)]
  transfers between devices with their start and end apart: 17 -> 26, of which waited for: 14 -> 14; matrix products, arithmetic and copies ran while one was open for 28% -> 0% of each run, Pallas kernels for 0% -> 3%
where the time goes in v1:
time: 137 us
  waiting for transfers between devices  80.2 us (59%)
  starting transfers between devices  45.1 us (33%)
  Pallas kernels  8.2 us (6%)
  local copies, waits for them, and re-layouts  3.14 us (2%)
    ppermute x26, waiting for transfers between devices, permuted(): lax.ppermute(value, axis, [(source, source ^ mask) for source in range(co...  80.2 us
    ppermute x26, starting transfers between devices, permuted(): lax.ppermute(value, axis, [(source, source ^ mask) for source in range(co...  45.1 us
    pallas_call x6, Pallas kernels, call(): pl.pallas_call(body, out_shape=[jax.ShapeDtypeStruct(shape, jnp.float32)]...  8.2 us
  transfers between devices with their start and end apart: 26, of which 14 were waited for; matrix products, arithmetic and copies ran while one was open for 0% of the time, Pallas kernels for 3%

profile of v1, /device:TPU:0, one launch (start us, length us, event | category | flops | bytes accessed | tf_op | source)
XLA Modules:
  0.0 136.8 jit_solution(18117082795589298780)
XLA Ops:
  0.0 3.0 %collective-permute-start.4 = (f32[16,128,128]{2,1,0:T(8,128)}, f32[16,128,128]{2,1,0:T(8,128)S(1)}, u32[]{:S(2)}, u32[]{:S(2)}) collective-permute-start(f32[16,128,128]{2,1,0:T(8,128)} %bitcast.2), channel_id=1, source_target_pairs={{0,16},{8,24},{16,0},{24,8},{1,17},{9,25},{17,1},{25,9},{2,18},{10... | collective-permute-start | bytes 3145736 | tf_op jit(solution)/shard_map/ppermute | solution.py:309
  7.5 3.7 %collective-permute-start = (f32[1,32,16,128]{3,2,1,0:T(8,128)S(1)}, f32[1,32,16,128]{3,2,1,0:T(8,128)S(1)}, u32[]{:S(2)}, u32[]{:S(2)}) collective-permute-start(f32[1,32,16,128]{3,2,1,0:T(8,128)S(1)} %get-tuple-element.47), channel_id=1, source_target_pairs={{0,6},{1,7},{2,4},{3,5},{4,2},{5,3},{6,0},{7,1},{8,14},{9,15},{10,... | collective-permute-start | bytes 786440 | tf_op jit(solution)/shard_map/ppermute | solution.py:309
  11.9 14.4 %collective-permute-done.4.rest_2_.rest_10_ = f32[16,128,128]{2,1,0:T(8,128)S(1)} collective-permute-done((f32[16,128,128]{2,1,0:T(8,128)}, f32[16,128,128]{2,1,0:T(8,128)S(1)}, u32[]{:S(2)}, u32[]{:S(2)}) %collective-permute-start.4) | collective-permute-done | bytes 1048608 | tf_op jit(solution)/shard_map/ppermute | solution.py:309
  29.3 1.9 %collective-permute-start.5 = (f32[3,8,16,128]{3,2,1,0:T(8,128)S(1)}, f32[3,8,16,128]{3,2,1,0:T(8,128)S(1)}, u32[]{:S(2)}, u32[]{:S(2)}) collective-permute-start(f32[3,8,16,128]{3,2,1,0:T(8,128)S(1)} %get-tuple-element.51), channel_id=1, source_target_pairs={{0,7},{1,6},{2,5},{3,4},{4,3},{5,2},{6,1},{7,0},{8,15},{9,14},{10,... | collective-permute-start | bytes 589832 | tf_op jit(solution)/shard_map/ppermute | solution.py:309
  31.3 1.6 %collective-permute-done.1.rest_1_ = f32[1,32,16,128]{3,2,1,0:T(8,128)S(1)} collective-permute-done((f32[1,32,16,128]{3,2,1,0:T(8,128)S(1)}, f32[1,32,16,128]{3,2,1,0:T(8,128)S(1)}, u32[]{:S(2)}, u32[]{:S(2)}) %collective-permute-start.1) | collective-permute-done | bytes 262176 | tf_op jit(solution)/shard_map/ppermute | solution.py:309
  32.9 5.4 %collective-permute-done.5.rest_0_ = f32[3,8,16,128]{3,2,1,0:T(8,128)S(1)} collective-permute-done((f32[3,8,16,128]{3,2,1,0:T(8,128)S(1)}, f32[3,8,16,128]{3,2,1,0:T(8,128)S(1)}, u32[]{:S(2)}, u32[]{:S(2)}) %collective-permute-start.5) | collective-permute-done | bytes 196640 | tf_op jit(solution)/shard_map/ppermute | solution.py:309
  39.9 2.7 %collective-permute-start.9 = (f32[3,8,16,128]{3,2,1,0:T(8,128)S(1)}, f32[3,8,16,128]{3,2,1,0:T(8,128)S(1)}, u32[]{:S(2)}, u32[]{:S(2)}) collective-permute-start(f32[3,8,16,128]{3,2,1,0:T(8,128)S(1)} %get-tuple-element.60), channel_id=1, source_target_pairs={{0,6},{1,7},{2,4},{3,5},{4,2},{5,3},{6,0},{7,1},{8,14},{9,15},{10,... | collective-permute-start | bytes 589832 | tf_op jit(solution)/shard_map/ppermute | solution.py:309
  43.6 2.9 %collective-permute-start.10 = (f32[3,8,16,128]{3,2,1,0:T(8,128)S(1)}, f32[3,8,16,128]{3,2,1,0:T(8,128)S(1)}, u32[]{:S(2)}, u32[]{:S(2)}) collective-permute-start(f32[3,8,16,128]{3,2,1,0:T(8,128)S(1)} %get-tuple-element.61), channel_id=1, source_target_pairs={{0,2},{1,3},{2,0},{3,1},{4,6},{5,7},{6,4},{7,5},{8,10},{9,11},{10,... | collective-permute-start | bytes 589832 | tf_op jit(solution)/shard_map/ppermute | solution.py:309
  47.0 1.8 %collective-permute-start.12 = (f32[3,8,16,128]{3,2,1,0:T(8,128)S(1)}, f32[3,8,16,128]{3,2,1,0:T(8,128)S(1)}, u32[]{:S(2)}, u32[]{:S(2)}) collective-permute-start(f32[3,8,16,128]{3,2,1,0:T(8,128)S(1)} %get-tuple-element.63), channel_id=1, source_target_pairs={{0,3},{1,2},{2,1},{3,0},{4,7},{5,6},{6,5},{7,4},{8,11},{9,10},{10,... | collective-permute-start | bytes 589832 | tf_op jit(solution)/shard_map/ppermute | solution.py:309
  48.8 6.3 %collective-permute-start.13 = (f32[3,8,16,128]{3,2,1,0:T(8,128)S(1)}, f32[3,8,16,128]{3,2,1,0:T(8,128)S(1)}, u32[]{:S(2)}, u32[]{:S(2)}) collective-permute-start(f32[3,8,16,128]{3,2,1,0:T(8,128)S(1)} %get-tuple-element.64), channel_id=1, source_target_pairs={{0,4},{1,5},{2,6},{3,7},{4,0},{5,1},{6,2},{7,3},{8,12},{9,13},{10,... | collective-permute-start | bytes 589832 | tf_op jit(solution)/shard_map/ppermute | solution.py:309
  55.1 6.1 %collective-permute-done.11.rest_4_ = f32[3,8,16,128]{3,2,1,0:T(8,128)S(1)} collective-permute-done((f32[3,8,16,128]{3,2,1,0:T(8,128)S(1)}, f32[3,8,16,128]{3,2,1,0:T(8,128)S(1)}, u32[]{:S(2)}, u32[]{:S(2)}) %collective-permute-start.11) | collective-permute-done | bytes 196640 | tf_op jit(solution)/shard_map/ppermute | solution.py:309
  61.2 8.4 %collective-permute-done.13.rest_6_ = f32[3,8,16,128]{3,2,1,0:T(8,128)S(1)} collective-permute-done((f32[3,8,16,128]{3,2,1,0:T(8,128)S(1)}, f32[3,8,16,128]{3,2,1,0:T(8,128)S(1)}, u32[]{:S(2)}, u32[]{:S(2)}) %collective-permute-start.13) | collective-permute-done | bytes 196640 | tf_op jit(solution)/shard_map/ppermute | solution.py:309
  70.9 2.4 %collective-permute-start.14 = (f32[3,8,16,128]{3,2,1,0:T(8,128)S(1)}, f32[3,8,16,128]{3,2,1,0:T(8,128)S(1)}, u32[]{:S(2)}, u32[]{:S(2)}) collective-permute-start(f32[3,8,16,128]{3,2,1,0:T(8,128)S(1)} %get-tuple-element.66), channel_id=1, source_target_pairs={{0,7},{1,6},{2,5},{3,4},{4,3},{5,2},{6,1},{7,0},{8,15},{9,14},{10,... | collective-permute-start | bytes 589832 | tf_op jit(solution)/shard_map/ppermute | solution.py:309
  74.9 2.4 %collective-permute-start.18 = (f32[3,8,16,128]{3,2,1,0:T(8,128)S(1)}, f32[3,8,16,128]{3,2,1,0:T(8,128)S(1)}, u32[]{:S(2)}, u32[]{:S(2)}) collective-permute-start(f32[3,8,16,128]{3,2,1,0:T(8,128)S(1)} %get-tuple-element.70), channel_id=1, source_target_pairs={{0,5},{1,4},{2,7},{3,6},{4,1},{5,0},{6,3},{7,2},{8,13},{9,12},{10,... | collective-permute-start | bytes 589832 | tf_op jit(solution)/shard_map/ppermute | solution.py:309
  77.4 2.6 %collective-permute-done.14.rest_0_ = f32[3,8,16,128]{3,2,1,0:T(8,128)S(1)} collective-permute-done((f32[3,8,16,128]{3,2,1,0:T(8,128)S(1)}, f32[3,8,16,128]{3,2,1,0:T(8,128)S(1)}, u32[]{:S(2)}, u32[]{:S(2)}) %collective-permute-start.14) | collective-permute-done | bytes 196640 | tf_op jit(solution)/shard_map/ppermute | solution.py:309
  79.9 6.4 %collective-permute-start.19 = (f32[3,8,16,128]{3,2,1,0:T(8,128)S(1)}, f32[3,8,16,128]{3,2,1,0:T(8,128)S(1)}, u32[]{:S(2)}, u32[]{:S(2)}) collective-permute-start(f32[3,8,16,128]{3,2,1,0:T(8,128)S(1)} %get-tuple-element.71), channel_id=1, source_target_pairs={{0,3},{1,2},{2,1},{3,0},{4,7},{5,6},{6,5},{7,4},{8,11},{9,10},{10,... | collective-permute-start | bytes 589832 | tf_op jit(solution)/shard_map/ppermute | solution.py:309
  86.5 2.1 %collective-permute-done.17.rest_3_ = f32[3,8,16,128]{3,2,1,0:T(8,128)S(1)} collective-permute-done((f32[3,8,16,128]{3,2,1,0:T(8,128)S(1)}, f32[3,8,16,128]{3,2,1,0:T(8,128)S(1)}, u32[]{:S(2)}, u32[]{:S(2)}) %collective-permute-start.17) | collective-permute-done | bytes 196640 | tf_op jit(solution)/shard_map/ppermute | solution.py:309
  88.6 14.0 %collective-permute-done.18.rest_4_ = f32[3,8,16,128]{3,2,1,0:T(8,128)S(1)} collective-permute-done((f32[3,8,16,128]{3,2,1,0:T(8,128)S(1)}, f32[3,8,16,128]{3,2,1,0:T(8,128)S(1)}, u32[]{:S(2)}, u32[]{:S(2)}) %collective-permute-start.18) | collective-permute-done | bytes 196640 | tf_op jit(solution)/shard_map/ppermute | solution.py:309
  102.5 4.4 %collective-permute-done.20.rest_6_ = f32[3,8,16,128]{3,2,1,0:T(8,128)S(1)} collective-permute-done((f32[3,8,16,128]{3,2,1,0:T(8,128)S(1)}, f32[3,8,16,128]{3,2,1,0:T(8,128)S(1)}, u32[]{:S(2)}, u32[]{:S(2)}) %collective-permute-start.20) | collective-permute-done | bytes 196640 | tf_op jit(solution)/shard_map/ppermute | solution.py:309
  106.9 1.6 %shard_map.32 = (f32[16,128,128]{2,1,0:T(8,128)S(1)}, f32[16,128,128]{2,1,0:T(8,128)S(1)}, f32[16,128,128]{2,1,0:T(8,128)S(1)}) custom-call(f32[128,128]{1,0:T(8,128)S(1)} %copy-done.2, f32[3,8,16,128]{3,2,1,0:T(8,128)S(1)} %collective-permute-done.14.rest_0_, f32[3,8,16,128]{3,2,1,0:T(8,128)S(1)} %collective-permute-done.15.rest_1_, ...), custom_call_target="tpu_custom_call" | custom-call | tf_op jit(solution)/shard_map/pallas_call | solution.py:324
  111.7 3.3 %collective-permute-start.23 = (f32[1,32,16,128]{3,2,1,0:T(8,128)S(1)}, f32[1,32,16,128]{3,2,1,0:T(8,128)S(1)}, u32[]{:S(2)}, u32[]{:S(2)}) collective-permute-start(f32[1,32,16,128]{3,2,1,0:T(8,128)S(1)} %get-tuple-element.76), channel_id=1, source_target_pairs={{0,2},{1,3},{2,0},{3,1},{4,6},{5,7},{6,4},{7,5},{8,10},{9,11},{10,... | collective-permute-start | bytes 786440 | tf_op jit(solution)/shard_map/ppermute | solution.py:309
  115.1 6.8 %collective-permute-done.21.rest_0_ = f32[1,32,16,128]{3,2,1,0:T(8,128)S(1)} collective-permute-done((f32[1,32,16,128]{3,2,1,0:T(8,128)S(1)}, f32[1,32,16,128]{3,2,1,0:T(8,128)S(1)}, u32[]{:S(2)}, u32[]{:S(2)}) %collective-permute-start.21) | collective-permute-done | bytes 262176 | tf_op jit(solution)/shard_map/ppermute | solution.py:309
  121.8 11.1 %collective-permute-done.22.rest_1_ = f32[1,32,16,128]{3,2,1,0:T(8,128)S(1)} collective-permute-done((f32[1,32,16,128]{3,2,1,0:T(8,128)S(1)}, f32[1,32,16,128]{3,2,1,0:T(8,128)S(1)}, u32[]{:S(2)}, u32[]{:S(2)}) %collective-permute-start.22) | collective-permute-done | bytes 262176 | tf_op jit(solution)/shard_map/ppermute | solution.py:309
  134.8 2.0 %shard_map.33 = f32[16,128,128]{2,1,0:T(8,128)} custom-call(f32[128,128]{1,0:T(8,128)S(1)} %copy-done.2, f32[1,32,16,128]{3,2,1,0:T(8,128)S(1)} %collective-permute-done.21.rest_0_, f32[1,32,16,128]{3,2,1,0:T(8,128)S(1)} %collective-permute-done.22.rest_1_, f32[1,32,16,128]{3,2,1,0:T(8,128)S(1)} %collective-permute-done.23.rest_2_, ...), custom_call_target="tpu_custom_call" | custom-call | tf_op jit(solution)/shard_map/pallas_call | solution.py:324
  (59 shorter events, 19.5 us)
Async XLA Ops:
  0.0 26.3 %collective-permute-start.4 = (f32[16,128,128]{2,1,0:T(8,128)}, f32[16,128,128]{2,1,0:T(8,128)S(1)}, u32[]{:S(2)}, u32[]{:S(2)}) collective-permute-start(f32[16,128,128]{2,1,0:T(8,128)} %bitcast.2), channel_id=1, source_target_pairs={{0,16},{8,24},{16,0},{24,8},{1,17},{9,25},{17,1},{25,9},{2,18},{10... | collective-permute-start | bytes 3145736 | tf_op jit(solution)/shard_map/ppermute | solution.py:309
  3.0 24.8 %collective-permute-start.3 = (f32[16,128,128]{2,1,0:T(8,128)}, f32[16,128,128]{2,1,0:T(8,128)S(1)}, u32[]{:S(2)}, u32[]{:S(2)}) collective-permute-start(f32[16,128,128]{2,1,0:T(8,128)} %bitcast.3), channel_id=1, source_target_pairs={{0,8},{8,0},{16,24},{24,16},{1,9},{9,1},{17,25},{25,17},{2,10},{10... | collective-permute-start | bytes 3145736 | tf_op jit(solution)/shard_map/ppermute | solution.py:309
  7.5 23.8 %collective-permute-start = (f32[1,32,16,128]{3,2,1,0:T(8,128)S(1)}, f32[1,32,16,128]{3,2,1,0:T(8,128)S(1)}, u32[]{:S(2)}, u32[]{:S(2)}) collective-permute-start(f32[1,32,16,128]{3,2,1,0:T(8,128)S(1)} %get-tuple-element.47), channel_id=1, source_target_pairs={{0,6},{1,7},{2,4},{3,5},{4,2},{5,3},{6,0},{7,1},{8,14},{9,15},{10,... | collective-permute-start | bytes 786440 | tf_op jit(solution)/shard_map/ppermute | solution.py:309
  11.1 21.8 %collective-permute-start.1 = (f32[1,32,16,128]{3,2,1,0:T(8,128)S(1)}, f32[1,32,16,128]{3,2,1,0:T(8,128)S(1)}, u32[]{:S(2)}, u32[]{:S(2)}) collective-permute-start(f32[1,32,16,128]{3,2,1,0:T(8,128)S(1)} %get-tuple-element.48), channel_id=1, source_target_pairs={{0,4},{1,5},{2,6},{3,7},{4,0},{5,1},{6,2},{7,3},{8,12},{9,13},{10,... | collective-permute-start | bytes 786440 | tf_op jit(solution)/shard_map/ppermute | solution.py:309
  11.1 21.8 %collective-permute-start.2 = (f32[1,32,16,128]{3,2,1,0:T(8,128)S(1)}, f32[1,32,16,128]{3,2,1,0:T(8,128)S(1)}, u32[]{:S(2)}, u32[]{:S(2)}) collective-permute-start(f32[1,32,16,128]{3,2,1,0:T(8,128)S(1)} %get-tuple-element.49), channel_id=1, source_target_pairs={{0,2},{1,3},{2,0},{3,1},{4,6},{5,7},{6,4},{7,5},{8,10},{9,11},{10,... | collective-permute-start | bytes 786440 | tf_op jit(solution)/shard_map/ppermute | solution.py:309
  29.3 8.9 %collective-permute-start.5 = (f32[3,8,16,128]{3,2,1,0:T(8,128)S(1)}, f32[3,8,16,128]{3,2,1,0:T(8,128)S(1)}, u32[]{:S(2)}, u32[]{:S(2)}) collective-permute-start(f32[3,8,16,128]{3,2,1,0:T(8,128)S(1)} %get-tuple-element.51), channel_id=1, source_target_pairs={{0,7},{1,6},{2,5},{3,4},{4,3},{5,2},{6,1},{7,0},{8,15},{9,14},{10,... | collective-permute-start | bytes 589832 | tf_op jit(solution)/shard_map/ppermute | solution.py:309
  39.9 9.0 %collective-permute-start.9 = (f32[3,8,16,128]{3,2,1,0:T(8,128)S(1)}, f32[3,8,16,128]{3,2,1,0:T(8,128)S(1)}, u32[]{:S(2)}, u32[]{:S(2)}) collective-permute-start(f32[3,8,16,128]{3,2,1,0:T(8,128)S(1)} %get-tuple-element.60), channel_id=1, source_target_pairs={{0,6},{1,7},{2,4},{3,5},{4,2},{5,3},{6,0},{7,1},{8,14},{9,15},{10,... | collective-permute-start | bytes 589832 | tf_op jit(solution)/shard_map/ppermute | solution.py:309
  43.5 31.4 %collective-permute-start.7 = (f32[1,64,16,128]{3,2,1,0:T(8,128)S(1)}, f32[1,64,16,128]{3,2,1,0:T(8,128)S(1)}, u32[]{:S(2)}, u32[]{:S(2)}) collective-permute-start(f32[1,64,16,128]{3,2,1,0:T(8,128)S(1)} %get-tuple-element.57), channel_id=1, source_target_pairs={{0,1},{1,0},{2,3},{3,2},{4,5},{5,4},{6,7},{7,6},{8,9},{9,8},{10,11... | collective-permute-start | bytes 1572872 | tf_op jit(solution)/shard_map/ppermute | solution.py:309
  43.6 11.5 %collective-permute-start.10 = (f32[3,8,16,128]{3,2,1,0:T(8,128)S(1)}, f32[3,8,16,128]{3,2,1,0:T(8,128)S(1)}, u32[]{:S(2)}, u32[]{:S(2)}) collective-permute-start(f32[3,8,16,128]{3,2,1,0:T(8,128)S(1)} %get-tuple-element.61), channel_id=1, source_target_pairs={{0,2},{1,3},{2,0},{3,1},{4,6},{5,7},{6,4},{7,5},{8,10},{9,11},{10,... | collective-permute-start | bytes 589832 | tf_op jit(solution)/shard_map/ppermute | solution.py:309
  46.4 14.8 %collective-permute-start.11 = (f32[3,8,16,128]{3,2,1,0:T(8,128)S(1)}, f32[3,8,16,128]{3,2,1,0:T(8,128)S(1)}, u32[]{:S(2)}, u32[]{:S(2)}) collective-permute-start(f32[3,8,16,128]{3,2,1,0:T(8,128)S(1)} %get-tuple-element.62), channel_id=1, source_target_pairs={{0,5},{1,4},{2,7},{3,6},{4,1},{5,0},{6,3},{7,2},{8,13},{9,12},{10,... | collective-permute-start | bytes 589832 | tf_op jit(solution)/shard_map/ppermute | solution.py:309
  47.0 14.2 %collective-permute-start.12 = (f32[3,8,16,128]{3,2,1,0:T(8,128)S(1)}, f32[3,8,16,128]{3,2,1,0:T(8,128)S(1)}, u32[]{:S(2)}, u32[]{:S(2)}) collective-permute-start(f32[3,8,16,128]{3,2,1,0:T(8,128)S(1)} %get-tuple-element.63), channel_id=1, source_target_pairs={{0,3},{1,2},{2,1},{3,0},{4,7},{5,6},{6,5},{7,4},{8,11},{9,10},{10,... | collective-permute-start | bytes 589832 | tf_op jit(solution)/shard_map/ppermute | solution.py:309
  48.8 20.8 %collective-permute-start.13 = (f32[3,8,16,128]{3,2,1,0:T(8,128)S(1)}, f32[3,8,16,128]{3,2,1,0:T(8,128)S(1)}, u32[]{:S(2)}, u32[]{:S(2)}) collective-permute-start(f32[3,8,16,128]{3,2,1,0:T(8,128)S(1)} %get-tuple-element.64), channel_id=1, source_target_pairs={{0,4},{1,5},{2,6},{3,7},{4,0},{5,1},{6,2},{7,3},{8,12},{9,13},{10,... | collective-permute-start | bytes 589832 | tf_op jit(solution)/shard_map/ppermute | solution.py:309
  70.9 9.1 %collective-permute-start.14 = (f32[3,8,16,128]{3,2,1,0:T(8,128)S(1)}, f32[3,8,16,128]{3,2,1,0:T(8,128)S(1)}, u32[]{:S(2)}, u32[]{:S(2)}) collective-permute-start(f32[3,8,16,128]{3,2,1,0:T(8,128)S(1)} %get-tuple-element.66), channel_id=1, source_target_pairs={{0,7},{1,6},{2,5},{3,4},{4,3},{5,2},{6,1},{7,0},{8,15},{9,14},{10,... | collective-permute-start | bytes 589832 | tf_op jit(solution)/shard_map/ppermute | solution.py:309
  73.3 13.1 %collective-permute-start.15 = (f32[3,8,16,128]{3,2,1,0:T(8,128)S(1)}, f32[3,8,16,128]{3,2,1,0:T(8,128)S(1)}, u32[]{:S(2)}, u32[]{:S(2)}) collective-permute-start(f32[3,8,16,128]{3,2,1,0:T(8,128)S(1)} %get-tuple-element.67), channel_id=1, source_target_pairs={{0,1},{1,0},{2,3},{3,2},{4,5},{5,4},{6,7},{7,6},{8,9},{9,8},{10,11... | collective-permute-start | bytes 589832 | tf_op jit(solution)/shard_map/ppermute | solution.py:309
  73.7 12.7 %collective-permute-start.16 = (f32[3,8,16,128]{3,2,1,0:T(8,128)S(1)}, f32[3,8,16,128]{3,2,1,0:T(8,128)S(1)}, u32[]{:S(2)}, u32[]{:S(2)}) collective-permute-start(f32[3,8,16,128]{3,2,1,0:T(8,128)S(1)} %get-tuple-element.68), channel_id=1, source_target_pairs={{0,6},{1,7},{2,4},{3,5},{4,2},{5,3},{6,0},{7,1},{8,14},{9,15},{10,... | collective-permute-start | bytes 589832 | tf_op jit(solution)/shard_map/ppermute | solution.py:309
  74.9 13.7 %collective-permute-start.17 = (f32[3,8,16,128]{3,2,1,0:T(8,128)S(1)}, f32[3,8,16,128]{3,2,1,0:T(8,128)S(1)}, u32[]{:S(2)}, u32[]{:S(2)}) collective-permute-start(f32[3,8,16,128]{3,2,1,0:T(8,128)S(1)} %get-tuple-element.69), channel_id=1, source_target_pairs={{0,2},{1,3},{2,0},{3,1},{4,6},{5,7},{6,4},{7,5},{8,10},{9,11},{10,... | collective-permute-start | bytes 589832 | tf_op jit(solution)/shard_map/ppermute | solution.py:309
  74.9 27.6 %collective-permute-start.18 = (f32[3,8,16,128]{3,2,1,0:T(8,128)S(1)}, f32[3,8,16,128]{3,2,1,0:T(8,128)S(1)}, u32[]{:S(2)}, u32[]{:S(2)}) collective-permute-start(f32[3,8,16,128]{3,2,1,0:T(8,128)S(1)} %get-tuple-element.70), channel_id=1, source_target_pairs={{0,5},{1,4},{2,7},{3,6},{4,1},{5,0},{6,3},{7,2},{8,13},{9,12},{10,... | collective-permute-start | bytes 589832 | tf_op jit(solution)/shard_map/ppermute | solution.py:309
  79.9 22.6 %collective-permute-start.19 = (f32[3,8,16,128]{3,2,1,0:T(8,128)S(1)}, f32[3,8,16,128]{3,2,1,0:T(8,128)S(1)}, u32[]{:S(2)}, u32[]{:S(2)}) collective-permute-start(f32[3,8,16,128]{3,2,1,0:T(8,128)S(1)} %get-tuple-element.71), channel_id=1, source_target_pairs={{0,3},{1,2},{2,1},{3,0},{4,7},{5,6},{6,5},{7,4},{8,11},{9,10},{10,... | collective-permute-start | bytes 589832 | tf_op jit(solution)/shard_map/ppermute | solution.py:309
  86.4 20.6 %collective-permute-start.20 = (f32[3,8,16,128]{3,2,1,0:T(8,128)S(1)}, f32[3,8,16,128]{3,2,1,0:T(8,128)S(1)}, u32[]{:S(2)}, u32[]{:S(2)}) collective-permute-start(f32[3,8,16,128]{3,2,1,0:T(8,128)S(1)} %get-tuple-element.72), channel_id=1, source_target_pairs={{0,4},{1,5},{2,6},{3,7},{4,0},{5,1},{6,2},{7,3},{8,12},{9,13},{10,... | collective-permute-start | bytes 589832 | tf_op jit(solution)/shard_map/ppermute | solution.py:309
  108.5 25.0 %collective-permute-start.24 = (f32[16,128,128]{2,1,0:T(8,128)S(1)}, f32[16,128,128]{2,1,0:T(8,128)S(1)}, u32[]{:S(2)}, u32[]{:S(2)}) collective-permute-start(f32[16,128,128]{2,1,0:T(8,128)S(1)} %get-tuple-element.87), channel_id=1, source_target_pairs={{0,8},{8,0},{16,24},{24,16},{1,9},{9,1},{17,25},{25,17},{2,10},{10... | collective-permute-start | bytes 3145736 | tf_op jit(solution)/shard_map/ppermute | solution.py:309
  110.1 24.7 %collective-permute-start.25 = (f32[16,128,128]{2,1,0:T(8,128)S(1)}, f32[16,128,128]{2,1,0:T(8,128)S(1)}, u32[]{:S(2)}, u32[]{:S(2)}) collective-permute-start(f32[16,128,128]{2,1,0:T(8,128)S(1)} %get-tuple-element.88), channel_id=1, source_target_pairs={{0,16},{8,24},{16,0},{24,8},{1,17},{9,25},{17,1},{25,9},{2,18},{10... | collective-permute-start | bytes 3145736 | tf_op jit(solution)/shard_map/ppermute | solution.py:309
  110.7 11.1 %collective-permute-start.21 = (f32[1,32,16,128]{3,2,1,0:T(8,128)S(1)}, f32[1,32,16,128]{3,2,1,0:T(8,128)S(1)}, u32[]{:S(2)}, u32[]{:S(2)}) collective-permute-start(f32[1,32,16,128]{3,2,1,0:T(8,128)S(1)} %get-tuple-element.74), channel_id=1, source_target_pairs={{0,6},{1,7},{2,4},{3,5},{4,2},{5,3},{6,0},{7,1},{8,14},{9,15},{10,... | collective-permute-start | bytes 786440 | tf_op jit(solution)/shard_map/ppermute | solution.py:309
  111.7 21.2 %collective-permute-start.22 = (f32[1,32,16,128]{3,2,1,0:T(8,128)S(1)}, f32[1,32,16,128]{3,2,1,0:T(8,128)S(1)}, u32[]{:S(2)}, u32[]{:S(2)}) collective-permute-start(f32[1,32,16,128]{3,2,1,0:T(8,128)S(1)} %get-tuple-element.75), channel_id=1, source_target_pairs={{0,4},{1,5},{2,6},{3,7},{4,0},{5,1},{6,2},{7,3},{8,12},{9,13},{10,... | collective-permute-start | bytes 786440 | tf_op jit(solution)/shard_map/ppermute | solution.py:309
  111.7 21.2 %collective-permute-start.23 = (f32[1,32,16,128]{3,2,1,0:T(8,128)S(1)}, f32[1,32,16,128]{3,2,1,0:T(8,128)S(1)}, u32[]{:S(2)}, u32[]{:S(2)}) collective-permute-start(f32[1,32,16,128]{3,2,1,0:T(8,128)S(1)} %get-tuple-element.76), channel_id=1, source_target_pairs={{0,2},{1,3},{2,0},{3,1},{4,6},{5,7},{6,4},{7,5},{8,10},{9,11},{10,... | collective-permute-start | bytes 786440 | tf_op jit(solution)/shard_map/ppermute | solution.py:309
  (11 other events, 54.4 us)

commit v2 on v1

--- a/solution.py
+++ b/solution.py
@@ -356,7 +356,8 @@
     chips = exchanged(forward(own_pair, own_block, len(own_chips), own_held, psi), own_chips)
     cross_spec = forward(cross_pairs, cross_block, slabs, cross_held, *bands)
     cross_spec = exchanged(cross_spec, cross_masks)
-    chips, cross_spec[0] = lax.optimization_barrier((chips, cross_spec[0]))
+    late = slabs // 2
+    chips, cross_spec[late] = lax.optimization_barrier((chips, cross_spec[late]))
     swap = jnp.concatenate([chip[:, own_rows:] for chip in chips], axis=1)
     kept, swap = middle(own_pair, swap_block, 2, *chips, permuted(swap, "slab", 1))
     swap = permuted(swap, "slab", 1)

time: 137 us -> 137 us (level)
  starting transfers between devices: 45.1 us -> 39.3 us
  waiting for transfers between devices: 80.2 us -> 85.8 us
    ppermute x26, starting transfers between devices: 45.1 us -> 39.3 us  [permuted(): lax.ppermute(value, axis, [(source, source ^ mask) for source in range(co...]
    ppermute x26, waiting for transfers between devices: 80.2 us -> 85.8 us  [permuted(): lax.ppermute(value, axis, [(source, source ^ mask) for source in range(co...]
  transfers between devices with their start and end apart: 26 -> 26, of which waited for: 14 -> 15; matrix products, arithmetic and copies ran while one was open for 0% -> 0% of each run, Pallas kernels for 3% -> 3%
where the time goes in v2:
time: 137 us
  waiting for transfers between devices  85.8 us (63%)
  starting transfers between devices  39.3 us (29%)
  Pallas kernels  8.2 us (6%)
  local copies, waits for them, and re-layouts  3.14 us (2%)
    ppermute x26, waiting for transfers between devices, permuted(): lax.ppermute(value, axis, [(source, source ^ mask) for source in range(co...  85.8 us
    ppermute x26, starting transfers between devices, permuted(): lax.ppermute(value, axis, [(source, source ^ mask) for source in range(co...  39.3 us
    pallas_call x6, Pallas kernels, call(): pl.pallas_call(body, out_shape=[jax.ShapeDtypeStruct(shape, jnp.float32)]...  8.2 us
  transfers between devices with their start and end apart: 26, of which 15 were waited for; matrix products, arithmetic and copies ran while one was open for 0% of the time, Pallas kernels for 3%

profile of v2, /device:TPU:0, one launch (start us, length us, event | category | flops | bytes accessed | tf_op | source)
XLA Modules:
  0.0 136.7 jit_solution(17217944320848737539)
XLA Ops:
  0.0 3.0 %collective-permute-start.4 = (f32[16,128,128]{2,1,0:T(8,128)}, f32[16,128,128]{2,1,0:T(8,128)S(1)}, u32[]{:S(2)}, u32[]{:S(2)}) collective-permute-start(f32[16,128,128]{2,1,0:T(8,128)} %bitcast.2), channel_id=1, source_target_pairs={{0,16},{8,24},{16,0},{24,8},{1,17},{9,25},{17,1},{25,9},{2,18},{10... | collective-permute-start | bytes 3145736 | tf_op jit(solution)/shard_map/ppermute | solution.py:309
  7.5 3.7 %collective-permute-start = (f32[1,32,16,128]{3,2,1,0:T(8,128)S(1)}, f32[1,32,16,128]{3,2,1,0:T(8,128)S(1)}, u32[]{:S(2)}, u32[]{:S(2)}) collective-permute-start(f32[1,32,16,128]{3,2,1,0:T(8,128)S(1)} %get-tuple-element.47), channel_id=1, source_target_pairs={{0,6},{1,7},{2,4},{3,5},{4,2},{5,3},{6,0},{7,1},{8,14},{9,15},{10,... | collective-permute-start | bytes 786440 | tf_op jit(solution)/shard_map/ppermute | solution.py:309
  11.9 14.4 %collective-permute-done.4.rest_2_.rest_10_ = f32[16,128,128]{2,1,0:T(8,128)S(1)} collective-permute-done((f32[16,128,128]{2,1,0:T(8,128)}, f32[16,128,128]{2,1,0:T(8,128)S(1)}, u32[]{:S(2)}, u32[]{:S(2)}) %collective-permute-start.4) | collective-permute-done | bytes 1048608 | tf_op jit(solution)/shard_map/ppermute | solution.py:309
  27.8 1.5 %shard_map.29 = (f32[3,8,16,128]{3,2,1,0:T(8,128)S(1)}, f32[3,8,16,128]{3,2,1,0:T(8,128)S(1)}, f32[3,8,16,128]{3,2,1,0:T(8,128)S(1)}, f32[3,8,16,128]{3,2,1,0:T(...) custom-call(f32[128,128]{1,0:T(8,128)S(1)} %copy-done.2, ...), custom_call_target="tpu_custom_call" | custom-call | tf_op jit(solution)/shard_map/pallas_call | solution.py:324
  30.2 2.6 %collective-permute-done.1.rest_1_ = f32[1,32,16,128]{3,2,1,0:T(8,128)S(1)} collective-permute-done((f32[1,32,16,128]{3,2,1,0:T(8,128)S(1)}, f32[1,32,16,128]{3,2,1,0:T(8,128)S(1)}, u32[]{:S(2)}, u32[]{:S(2)}) %collective-permute-start.1) | collective-permute-done | bytes 262176 | tf_op jit(solution)/shard_map/ppermute | solution.py:309
  32.9 8.6 %collective-permute-done.5.rest_4_ = f32[3,8,16,128]{3,2,1,0:T(8,128)S(1)} collective-permute-done((f32[3,8,16,128]{3,2,1,0:T(8,128)S(1)}, f32[3,8,16,128]{3,2,1,0:T(8,128)S(1)}, u32[]{:S(2)}, u32[]{:S(2)}) %collective-permute-start.5) | collective-permute-done | bytes 196640 | tf_op jit(solution)/shard_map/ppermute | solution.py:309
  42.7 2.6 %collective-permute-start.8 = (f32[3,8,16,128]{3,2,1,0:T(8,128)S(1)}, f32[3,8,16,128]{3,2,1,0:T(8,128)S(1)}, u32[]{:S(2)}, u32[]{:S(2)}) collective-permute-start(f32[3,8,16,128]{3,2,1,0:T(8,128)S(1)} %get-tuple-element.58), channel_id=1, source_target_pairs={{0,7},{1,6},{2,5},{3,4},{4,3},{5,2},{6,1},{7,0},{8,15},{9,14},{10,... | collective-permute-start | bytes 589832 | tf_op jit(solution)/shard_map/ppermute | solution.py:309
  48.2 3.2 %collective-permute-done.8.rest_0_ = f32[3,8,16,128]{3,2,1,0:T(8,128)S(1)} collective-permute-done((f32[3,8,16,128]{3,2,1,0:T(8,128)S(1)}, f32[3,8,16,128]{3,2,1,0:T(8,128)S(1)}, u32[]{:S(2)}, u32[]{:S(2)}) %collective-permute-start.8) | collective-permute-done | bytes 196640 | tf_op jit(solution)/shard_map/ppermute | solution.py:309
  51.4 6.8 %collective-permute-start.12 = (f32[3,8,16,128]{3,2,1,0:T(8,128)S(1)}, f32[3,8,16,128]{3,2,1,0:T(8,128)S(1)}, u32[]{:S(2)}, u32[]{:S(2)}) collective-permute-start(f32[3,8,16,128]{3,2,1,0:T(8,128)S(1)} %get-tuple-element.63), channel_id=1, source_target_pairs={{0,3},{1,2},{2,1},{3,0},{4,7},{5,6},{6,5},{7,4},{8,11},{9,10},{10,... | collective-permute-start | bytes 589832 | tf_op jit(solution)/shard_map/ppermute | solution.py:309
  58.2 2.1 %collective-permute-done.11.rest_3_ = f32[3,8,16,128]{3,2,1,0:T(8,128)S(1)} collective-permute-done((f32[3,8,16,128]{3,2,1,0:T(8,128)S(1)}, f32[3,8,16,128]{3,2,1,0:T(8,128)S(1)}, u32[]{:S(2)}, u32[]{:S(2)}) %collective-permute-start.11) | collective-permute-done | bytes 196640 | tf_op jit(solution)/shard_map/ppermute | solution.py:309
  60.3 6.7 %collective-permute-done.12.rest_5_ = f32[3,8,16,128]{3,2,1,0:T(8,128)S(1)} collective-permute-done((f32[3,8,16,128]{3,2,1,0:T(8,128)S(1)}, f32[3,8,16,128]{3,2,1,0:T(8,128)S(1)}, u32[]{:S(2)}, u32[]{:S(2)}) %collective-permute-start.12) | collective-permute-done | bytes 196640 | tf_op jit(solution)/shard_map/ppermute | solution.py:309
  67.1 3.2 %collective-permute-done.13.rest_6_ = f32[3,8,16,128]{3,2,1,0:T(8,128)S(1)} collective-permute-done((f32[3,8,16,128]{3,2,1,0:T(8,128)S(1)}, f32[3,8,16,128]{3,2,1,0:T(8,128)S(1)}, u32[]{:S(2)}, u32[]{:S(2)}) %collective-permute-start.13) | collective-permute-done | bytes 196640 | tf_op jit(solution)/shard_map/ppermute | solution.py:309
  73.0 2.4 %collective-permute-start.16 = (f32[3,8,16,128]{3,2,1,0:T(8,128)S(1)}, f32[3,8,16,128]{3,2,1,0:T(8,128)S(1)}, u32[]{:S(2)}, u32[]{:S(2)}) collective-permute-start(f32[3,8,16,128]{3,2,1,0:T(8,128)S(1)} %get-tuple-element.68), channel_id=1, source_target_pairs={{0,6},{1,7},{2,4},{3,5},{4,2},{5,3},{6,0},{7,1},{8,14},{9,15},{10,... | collective-permute-start | bytes 589832 | tf_op jit(solution)/shard_map/ppermute | solution.py:309
  76.6 4.1 %collective-permute-done.14.rest_0_ = f32[3,8,16,128]{3,2,1,0:T(8,128)S(1)} collective-permute-done((f32[3,8,16,128]{3,2,1,0:T(8,128)S(1)}, f32[3,8,16,128]{3,2,1,0:T(8,128)S(1)}, u32[]{:S(2)}, u32[]{:S(2)}) %collective-permute-start.14) | collective-permute-done | bytes 196640 | tf_op jit(solution)/shard_map/ppermute | solution.py:309
  80.7 5.4 %collective-permute-start.19 = (f32[3,8,16,128]{3,2,1,0:T(8,128)S(1)}, f32[3,8,16,128]{3,2,1,0:T(8,128)S(1)}, u32[]{:S(2)}, u32[]{:S(2)}) collective-permute-start(f32[3,8,16,128]{3,2,1,0:T(8,128)S(1)} %get-tuple-element.71), channel_id=1, source_target_pairs={{0,3},{1,2},{2,1},{3,0},{4,7},{5,6},{6,5},{7,4},{8,11},{9,10},{10,... | collective-permute-start | bytes 589832 | tf_op jit(solution)/shard_map/ppermute | solution.py:309
  88.6 13.8 %collective-permute-done.18.rest_4_ = f32[3,8,16,128]{3,2,1,0:T(8,128)S(1)} collective-permute-done((f32[3,8,16,128]{3,2,1,0:T(8,128)S(1)}, f32[3,8,16,128]{3,2,1,0:T(8,128)S(1)}, u32[]{:S(2)}, u32[]{:S(2)}) %collective-permute-start.18) | collective-permute-done | bytes 196640 | tf_op jit(solution)/shard_map/ppermute | solution.py:309
  102.4 4.4 %collective-permute-done.20.rest_6_ = f32[3,8,16,128]{3,2,1,0:T(8,128)S(1)} collective-permute-done((f32[3,8,16,128]{3,2,1,0:T(8,128)S(1)}, f32[3,8,16,128]{3,2,1,0:T(8,128)S(1)}, u32[]{:S(2)}, u32[]{:S(2)}) %collective-permute-start.20) | collective-permute-done | bytes 196640 | tf_op jit(solution)/shard_map/ppermute | solution.py:309
  106.7 1.6 %shard_map.32 = (f32[16,128,128]{2,1,0:T(8,128)S(1)}, f32[16,128,128]{2,1,0:T(8,128)S(1)}, f32[16,128,128]{2,1,0:T(8,128)S(1)}) custom-call(f32[128,128]{1,0:T(8,128)S(1)} %copy-done.2, f32[3,8,16,128]{3,2,1,0:T(8,128)S(1)} %collective-permute-done.14.rest_0_, f32[3,8,16,128]{3,2,1,0:T(8,128)S(1)} %collective-permute-done.15.rest_1_, ...), custom_call_target="tpu_custom_call" | custom-call | tf_op jit(solution)/shard_map/pallas_call | solution.py:324
  108.3 1.6 %collective-permute-start.24 = (f32[16,128,128]{2,1,0:T(8,128)S(1)}, f32[16,128,128]{2,1,0:T(8,128)S(1)}, u32[]{:S(2)}, u32[]{:S(2)}) collective-permute-start(f32[16,128,128]{2,1,0:T(8,128)S(1)} %get-tuple-element.87), channel_id=1, source_target_pairs={{0,8},{8,0},{16,24},{24,16},{1,9},{9,1},{17,25},{25,17},{2,10},{10... | collective-permute-start | bytes 3145736 | tf_op jit(solution)/shard_map/ppermute | solution.py:309
  110.4 1.6 %collective-permute-start.21 = (f32[1,32,16,128]{3,2,1,0:T(8,128)S(1)}, f32[1,32,16,128]{3,2,1,0:T(8,128)S(1)}, u32[]{:S(2)}, u32[]{:S(2)}) collective-permute-start(f32[1,32,16,128]{3,2,1,0:T(8,128)S(1)} %get-tuple-element.74), channel_id=1, source_target_pairs={{0,6},{1,7},{2,4},{3,5},{4,2},{5,3},{6,0},{7,1},{8,14},{9,15},{10,... | collective-permute-start | bytes 786440 | tf_op jit(solution)/shard_map/ppermute | solution.py:309
  112.0 2.8 %collective-permute-start.23 = (f32[1,32,16,128]{3,2,1,0:T(8,128)S(1)}, f32[1,32,16,128]{3,2,1,0:T(8,128)S(1)}, u32[]{:S(2)}, u32[]{:S(2)}) collective-permute-start(f32[1,32,16,128]{3,2,1,0:T(8,128)S(1)} %get-tuple-element.76), channel_id=1, source_target_pairs={{0,2},{1,3},{2,0},{3,1},{4,6},{5,7},{6,4},{7,5},{8,10},{9,11},{10,... | collective-permute-start | bytes 786440 | tf_op jit(solution)/shard_map/ppermute | solution.py:309
  114.8 6.8 %collective-permute-done.21.rest_0_ = f32[1,32,16,128]{3,2,1,0:T(8,128)S(1)} collective-permute-done((f32[1,32,16,128]{3,2,1,0:T(8,128)S(1)}, f32[1,32,16,128]{3,2,1,0:T(8,128)S(1)}, u32[]{:S(2)}, u32[]{:S(2)}) %collective-permute-start.21) | collective-permute-done | bytes 262176 | tf_op jit(solution)/shard_map/ppermute | solution.py:309
  121.5 12.1 %collective-permute-done.22.rest_1_ = f32[1,32,16,128]{3,2,1,0:T(8,128)S(1)} collective-permute-done((f32[1,32,16,128]{3,2,1,0:T(8,128)S(1)}, f32[1,32,16,128]{3,2,1,0:T(8,128)S(1)}, u32[]{:S(2)}, u32[]{:S(2)}) %collective-permute-start.22) | collective-permute-done | bytes 262176 | tf_op jit(solution)/shard_map/ppermute | solution.py:309
  134.7 2.0 %shard_map.33 = f32[16,128,128]{2,1,0:T(8,128)} custom-call(f32[128,128]{1,0:T(8,128)S(1)} %copy-done.2, f32[1,32,16,128]{3,2,1,0:T(8,128)S(1)} %collective-permute-done.21.rest_0_, f32[1,32,16,128]{3,2,1,0:T(8,128)S(1)} %collective-permute-done.22.rest_1_, f32[1,32,16,128]{3,2,1,0:T(8,128)S(1)} %collective-permute-done.23.rest_2_, ...), custom_call_target="tpu_custom_call" | custom-call | tf_op jit(solution)/shard_map/pallas_call | solution.py:324
  (59 shorter events, 19.6 us)
Async XLA Ops:
  0.0 26.3 %collective-permute-start.4 = (f32[16,128,128]{2,1,0:T(8,128)}, f32[16,128,128]{2,1,0:T(8,128)S(1)}, u32[]{:S(2)}, u32[]{:S(2)}) collective-permute-start(f32[16,128,128]{2,1,0:T(8,128)} %bitcast.2), channel_id=1, source_target_pairs={{0,16},{8,24},{16,0},{24,8},{1,17},{9,25},{17,1},{25,9},{2,18},{10... | collective-permute-start | bytes 3145736 | tf_op jit(solution)/shard_map/ppermute | solution.py:309
  3.0 24.8 %collective-permute-start.3 = (f32[16,128,128]{2,1,0:T(8,128)}, f32[16,128,128]{2,1,0:T(8,128)S(1)}, u32[]{:S(2)}, u32[]{:S(2)}) collective-permute-start(f32[16,128,128]{2,1,0:T(8,128)} %bitcast.3), channel_id=1, source_target_pairs={{0,8},{8,0},{16,24},{24,16},{1,9},{9,1},{17,25},{25,17},{2,10},{10... | collective-permute-start | bytes 3145736 | tf_op jit(solution)/shard_map/ppermute | solution.py:309
  7.5 22.8 %collective-permute-start = (f32[1,32,16,128]{3,2,1,0:T(8,128)S(1)}, f32[1,32,16,128]{3,2,1,0:T(8,128)S(1)}, u32[]{:S(2)}, u32[]{:S(2)}) collective-permute-start(f32[1,32,16,128]{3,2,1,0:T(8,128)S(1)} %get-tuple-element.47), channel_id=1, source_target_pairs={{0,6},{1,7},{2,4},{3,5},{4,2},{5,3},{6,0},{7,1},{8,14},{9,15},{10,... | collective-permute-start | bytes 786440 | tf_op jit(solution)/shard_map/ppermute | solution.py:309
  11.1 21.8 %collective-permute-start.1 = (f32[1,32,16,128]{3,2,1,0:T(8,128)S(1)}, f32[1,32,16,128]{3,2,1,0:T(8,128)S(1)}, u32[]{:S(2)}, u32[]{:S(2)}) collective-permute-start(f32[1,32,16,128]{3,2,1,0:T(8,128)S(1)} %get-tuple-element.48), channel_id=1, source_target_pairs={{0,4},{1,5},{2,6},{3,7},{4,0},{5,1},{6,2},{7,3},{8,12},{9,13},{10,... | collective-permute-start | bytes 786440 | tf_op jit(solution)/shard_map/ppermute | solution.py:309
  11.1 21.8 %collective-permute-start.2 = (f32[1,32,16,128]{3,2,1,0:T(8,128)S(1)}, f32[1,32,16,128]{3,2,1,0:T(8,128)S(1)}, u32[]{:S(2)}, u32[]{:S(2)}) collective-permute-start(f32[1,32,16,128]{3,2,1,0:T(8,128)S(1)} %get-tuple-element.49), channel_id=1, source_target_pairs={{0,2},{1,3},{2,0},{3,1},{4,6},{5,7},{6,4},{7,5},{8,10},{9,11},{10,... | collective-permute-start | bytes 786440 | tf_op jit(solution)/shard_map/ppermute | solution.py:309
  29.3 12.1 %collective-permute-start.5 = (f32[3,8,16,128]{3,2,1,0:T(8,128)S(1)}, f32[3,8,16,128]{3,2,1,0:T(8,128)S(1)}, u32[]{:S(2)}, u32[]{:S(2)}) collective-permute-start(f32[3,8,16,128]{3,2,1,0:T(8,128)S(1)} %get-tuple-element.51), channel_id=1, source_target_pairs={{0,5},{1,4},{2,7},{3,6},{4,1},{5,0},{6,3},{7,2},{8,13},{9,12},{10,... | collective-permute-start | bytes 589832 | tf_op jit(solution)/shard_map/ppermute | solution.py:309
  45.3 12.9 %collective-permute-start.9 = (f32[3,8,16,128]{3,2,1,0:T(8,128)S(1)}, f32[3,8,16,128]{3,2,1,0:T(8,128)S(1)}, u32[]{:S(2)}, u32[]{:S(2)}) collective-permute-start(f32[3,8,16,128]{3,2,1,0:T(8,128)S(1)} %get-tuple-element.59), channel_id=1, source_target_pairs={{0,1},{1,0},{2,3},{3,2},{4,5},{5,4},{6,7},{7,6},{8,9},{9,8},{10,11... | collective-permute-start | bytes 589832 | tf_op jit(solution)/shard_map/ppermute | solution.py:309
  46.3 29.3 %collective-permute-start.7 = (f32[1,64,16,128]{3,2,1,0:T(8,128)S(1)}, f32[1,64,16,128]{3,2,1,0:T(8,128)S(1)}, u32[]{:S(2)}, u32[]{:S(2)}) collective-permute-start(f32[1,64,16,128]{3,2,1,0:T(8,128)S(1)} %get-tuple-element.57), channel_id=1, source_target_pairs={{0,1},{1,0},{2,3},{3,2},{4,5},{5,4},{6,7},{7,6},{8,9},{9,8},{10,11... | collective-permute-start | bytes 1572872 | tf_op jit(solution)/shard_map/ppermute | solution.py:309
  46.8 11.4 %collective-permute-start.10 = (f32[3,8,16,128]{3,2,1,0:T(8,128)S(1)}, f32[3,8,16,128]{3,2,1,0:T(8,128)S(1)}, u32[]{:S(2)}, u32[]{:S(2)}) collective-permute-start(f32[3,8,16,128]{3,2,1,0:T(8,128)S(1)} %get-tuple-element.60), channel_id=1, source_target_pairs={{0,6},{1,7},{2,4},{3,5},{4,2},{5,3},{6,0},{7,1},{8,14},{9,15},{10,... | collective-permute-start | bytes 589832 | tf_op jit(solution)/shard_map/ppermute | solution.py:309
  48.2 12.1 %collective-permute-start.11 = (f32[3,8,16,128]{3,2,1,0:T(8,128)S(1)}, f32[3,8,16,128]{3,2,1,0:T(8,128)S(1)}, u32[]{:S(2)}, u32[]{:S(2)}) collective-permute-start(f32[3,8,16,128]{3,2,1,0:T(8,128)S(1)} %get-tuple-element.61), channel_id=1, source_target_pairs={{0,2},{1,3},{2,0},{3,1},{4,6},{5,7},{6,4},{7,5},{8,10},{9,11},{10,... | collective-permute-start | bytes 589832 | tf_op jit(solution)/shard_map/ppermute | solution.py:309
  51.4 15.7 %collective-permute-start.12 = (f32[3,8,16,128]{3,2,1,0:T(8,128)S(1)}, f32[3,8,16,128]{3,2,1,0:T(8,128)S(1)}, u32[]{:S(2)}, u32[]{:S(2)}) collective-permute-start(f32[3,8,16,128]{3,2,1,0:T(8,128)S(1)} %get-tuple-element.63), channel_id=1, source_target_pairs={{0,3},{1,2},{2,1},{3,0},{4,7},{5,6},{6,5},{7,4},{8,11},{9,10},{10,... | collective-permute-start | bytes 589832 | tf_op jit(solution)/shard_map/ppermute | solution.py:309
  58.2 12.1 %collective-permute-start.13 = (f32[3,8,16,128]{3,2,1,0:T(8,128)S(1)}, f32[3,8,16,128]{3,2,1,0:T(8,128)S(1)}, u32[]{:S(2)}, u32[]{:S(2)}) collective-permute-start(f32[3,8,16,128]{3,2,1,0:T(8,128)S(1)} %get-tuple-element.64), channel_id=1, source_target_pairs={{0,4},{1,5},{2,6},{3,7},{4,0},{5,1},{6,2},{7,3},{8,12},{9,13},{10,... | collective-permute-start | bytes 589832 | tf_op jit(solution)/shard_map/ppermute | solution.py:309
  71.5 9.2 %collective-permute-start.14 = (f32[3,8,16,128]{3,2,1,0:T(8,128)S(1)}, f32[3,8,16,128]{3,2,1,0:T(8,128)S(1)}, u32[]{:S(2)}, u32[]{:S(2)}) collective-permute-start(f32[3,8,16,128]{3,2,1,0:T(8,128)S(1)} %get-tuple-element.66), channel_id=1, source_target_pairs={{0,7},{1,6},{2,5},{3,4},{4,3},{5,2},{6,1},{7,0},{8,15},{9,14},{10,... | collective-permute-start | bytes 589832 | tf_op jit(solution)/shard_map/ppermute | solution.py:309
  71.8 14.4 %collective-permute-start.15 = (f32[3,8,16,128]{3,2,1,0:T(8,128)S(1)}, f32[3,8,16,128]{3,2,1,0:T(8,128)S(1)}, u32[]{:S(2)}, u32[]{:S(2)}) collective-permute-start(f32[3,8,16,128]{3,2,1,0:T(8,128)S(1)} %get-tuple-element.67), channel_id=1, source_target_pairs={{0,1},{1,0},{2,3},{3,2},{4,5},{5,4},{6,7},{7,6},{8,9},{9,8},{10,11... | collective-permute-start | bytes 589832 | tf_op jit(solution)/shard_map/ppermute | solution.py:309
  73.0 14.2 %collective-permute-start.16 = (f32[3,8,16,128]{3,2,1,0:T(8,128)S(1)}, f32[3,8,16,128]{3,2,1,0:T(8,128)S(1)}, u32[]{:S(2)}, u32[]{:S(2)}) collective-permute-start(f32[3,8,16,128]{3,2,1,0:T(8,128)S(1)} %get-tuple-element.68), channel_id=1, source_target_pairs={{0,6},{1,7},{2,4},{3,5},{4,2},{5,3},{6,0},{7,1},{8,14},{9,15},{10,... | collective-permute-start | bytes 589832 | tf_op jit(solution)/shard_map/ppermute | solution.py:309
  75.5 13.1 %collective-permute-start.17 = (f32[3,8,16,128]{3,2,1,0:T(8,128)S(1)}, f32[3,8,16,128]{3,2,1,0:T(8,128)S(1)}, u32[]{:S(2)}, u32[]{:S(2)}) collective-permute-start(f32[3,8,16,128]{3,2,1,0:T(8,128)S(1)} %get-tuple-element.69), channel_id=1, source_target_pairs={{0,2},{1,3},{2,0},{3,1},{4,6},{5,7},{6,4},{7,5},{8,10},{9,11},{10,... | collective-permute-start | bytes 589832 | tf_op jit(solution)/shard_map/ppermute | solution.py:309
  75.5 26.8 %collective-permute-start.18 = (f32[3,8,16,128]{3,2,1,0:T(8,128)S(1)}, f32[3,8,16,128]{3,2,1,0:T(8,128)S(1)}, u32[]{:S(2)}, u32[]{:S(2)}) collective-permute-start(f32[3,8,16,128]{3,2,1,0:T(8,128)S(1)} %get-tuple-element.70), channel_id=1, source_target_pairs={{0,5},{1,4},{2,7},{3,6},{4,1},{5,0},{6,3},{7,2},{8,13},{9,12},{10,... | collective-permute-start | bytes 589832 | tf_op jit(solution)/shard_map/ppermute | solution.py:309
  80.7 21.7 %collective-permute-start.19 = (f32[3,8,16,128]{3,2,1,0:T(8,128)S(1)}, f32[3,8,16,128]{3,2,1,0:T(8,128)S(1)}, u32[]{:S(2)}, u32[]{:S(2)}) collective-permute-start(f32[3,8,16,128]{3,2,1,0:T(8,128)S(1)} %get-tuple-element.71), channel_id=1, source_target_pairs={{0,3},{1,2},{2,1},{3,0},{4,7},{5,6},{6,5},{7,4},{8,11},{9,10},{10,... | collective-permute-start | bytes 589832 | tf_op jit(solution)/shard_map/ppermute | solution.py:309
  86.1 20.6 %collective-permute-start.20 = (f32[3,8,16,128]{3,2,1,0:T(8,128)S(1)}, f32[3,8,16,128]{3,2,1,0:T(8,128)S(1)}, u32[]{:S(2)}, u32[]{:S(2)}) collective-permute-start(f32[3,8,16,128]{3,2,1,0:T(8,128)S(1)} %get-tuple-element.72), channel_id=1, source_target_pairs={{0,4},{1,5},{2,6},{3,7},{4,0},{5,1},{6,2},{7,3},{8,12},{9,13},{10,... | collective-permute-start | bytes 589832 | tf_op jit(solution)/shard_map/ppermute | solution.py:309
  108.3 25.3 %collective-permute-start.24 = (f32[16,128,128]{2,1,0:T(8,128)S(1)}, f32[16,128,128]{2,1,0:T(8,128)S(1)}, u32[]{:S(2)}, u32[]{:S(2)}) collective-permute-start(f32[16,128,128]{2,1,0:T(8,128)S(1)} %get-tuple-element.87), channel_id=1, source_target_pairs={{0,8},{8,0},{16,24},{24,16},{1,9},{9,1},{17,25},{25,17},{2,10},{10... | collective-permute-start | bytes 3145736 | tf_op jit(solution)/shard_map/ppermute | solution.py:309
  109.9 24.8 %collective-permute-start.25 = (f32[16,128,128]{2,1,0:T(8,128)S(1)}, f32[16,128,128]{2,1,0:T(8,128)S(1)}, u32[]{:S(2)}, u32[]{:S(2)}) collective-permute-start(f32[16,128,128]{2,1,0:T(8,128)S(1)} %get-tuple-element.88), channel_id=1, source_target_pairs={{0,16},{8,24},{16,0},{24,8},{1,17},{9,25},{17,1},{25,9},{2,18},{10... | collective-permute-start | bytes 3145736 | tf_op jit(solution)/shard_map/ppermute | solution.py:309
  110.4 11.1 %collective-permute-start.21 = (f32[1,32,16,128]{3,2,1,0:T(8,128)S(1)}, f32[1,32,16,128]{3,2,1,0:T(8,128)S(1)}, u32[]{:S(2)}, u32[]{:S(2)}) collective-permute-start(f32[1,32,16,128]{3,2,1,0:T(8,128)S(1)} %get-tuple-element.74), channel_id=1, source_target_pairs={{0,6},{1,7},{2,4},{3,5},{4,2},{5,3},{6,0},{7,1},{8,14},{9,15},{10,... | collective-permute-start | bytes 786440 | tf_op jit(solution)/shard_map/ppermute | solution.py:309
  112.0 21.7 %collective-permute-start.22 = (f32[1,32,16,128]{3,2,1,0:T(8,128)S(1)}, f32[1,32,16,128]{3,2,1,0:T(8,128)S(1)}, u32[]{:S(2)}, u32[]{:S(2)}) collective-permute-start(f32[1,32,16,128]{3,2,1,0:T(8,128)S(1)} %get-tuple-element.75), channel_id=1, source_target_pairs={{0,4},{1,5},{2,6},{3,7},{4,0},{5,1},{6,2},{7,3},{8,12},{9,13},{10,... | collective-permute-start | bytes 786440 | tf_op jit(solution)/shard_map/ppermute | solution.py:309
  112.0 21.7 %collective-permute-start.23 = (f32[1,32,16,128]{3,2,1,0:T(8,128)S(1)}, f32[1,32,16,128]{3,2,1,0:T(8,128)S(1)}, u32[]{:S(2)}, u32[]{:S(2)}) collective-permute-start(f32[1,32,16,128]{3,2,1,0:T(8,128)S(1)} %get-tuple-element.76), channel_id=1, source_target_pairs={{0,2},{1,3},{2,0},{3,1},{4,6},{5,7},{6,4},{7,5},{8,10},{9,11},{10,... | collective-permute-start | bytes 786440 | tf_op jit(solution)/shard_map/ppermute | solution.py:309
  (11 other events, 60.6 us)

commit v3 on v1

--- a/solution.py
+++ b/solution.py
@@ -159,12 +159,21 @@
     return [mask for pair in zip(far, near) for mask in pair] if slabs > 1 else [0]
 
 
+def back_masks(slabs):
+    masks = partner_masks(slabs)
+    for n in range(0, slabs - 2, 2):
+        masks[n], masks[n + 1] = masks[n + 1], masks[n]
+    return masks
+
+
 def own_masks(slabs):
     return [chip + core for chip in range(slabs - 2, -1, -2) for core in range(2)]
 
 
-def masks_of(fields, slabs):
-    return own_masks(slabs) if len(fields) == 1 else partner_masks(slabs)
+def masks_of(fields, slabs, back=False):
+    if len(fields) == 1:
+        return own_masks(slabs)
+    return back_masks(slabs) if back else partner_masks(slabs)
 
 
 def partner_rows(table_ref, masks, start, size):
@@ -189,10 +198,10 @@
     return [group * (length // 2) for group in half_groups()]
 
 
-def y_tables(fields, slabs, table_ref):
+def y_tables(fields, slabs, table_ref, back=False):
     starts = group_starts(fields, table_ref.shape[0])
     size = table_ref.shape[0] // slabs // (1 if len(fields) == 1 else 2)
-    masks = masks_of(fields, slabs)
+    masks = masks_of(fields, slabs, back)
     return [partner_rows(table_ref, masks, start, size) for start in starts]
 
 
@@ -235,8 +244,11 @@
     else:
         in_refs, out_refs = rest[:slabs], rest[slabs:]
     _, per_slab, planes, length = in_refs[0].shape
-    back_table = partner_rows(table_ref, masks_of(fields, slabs), 0, planes)
-    x_parts, back_parts = left_table(back_table.T), left_table(back_table)
+    x_table, back_table = (
+        partner_rows(table_ref, masks_of(fields, slabs, back), 0, planes)
+        for back in (False, True)
+    )
+    x_parts, back_parts = left_table(x_table.T), left_table(back_table)
     in_plane = folded_square(
         lax.broadcasted_iota(jnp.int32, (length, length), 0), length
     ) + folded_square(lax.broadcasted_iota(jnp.int32, (length, length), 1), length)
@@ -282,7 +294,7 @@
     term_refs, out_refs, held = rest[arrays + bands : -bands - 1], rest[-bands - 1 : -1], rest[-1]
     _, per_slab, planes, length = spec_refs[0].shape
     z_parts = right_table(table_ref[...])
-    y_parts = [left_table(table.T) for table in y_tables(fields, slabs, table_ref)]
+    y_parts = [left_table(table.T) for table in y_tables(fields, slabs, table_ref, True)]
     rows = per_slab * planes
     for k, ref in enumerate(spec_refs):
         for f in range(len(fields)):
@@ -304,6 +316,10 @@
             store_two(ref, first, total)
 
 
+def sum_kernel(_, first_ref, second_ref, third_ref, out_ref):
+    out_ref[...] = first_ref[...] + second_ref[...] + third_ref[...]
+
+
 def permuted(value, axis, mask):
     count = lax.axis_size(axis)
     return lax.ppermute(value, axis, [(source, source ^ mask) for source in range(count)])
@@ -365,12 +381,13 @@
         for n in range(len(own_chips))
     ]
     cross_spec = middle(cross_pairs, cross_block, slabs, *cross_spec)
-    cross_spec = exchanged(cross_spec, cross_masks)
+    cross_spec = exchanged(cross_spec, back_masks(slabs))
     chips, cross_spec = lax.optimization_barrier((chips, cross_spec))
     chips = exchanged(chips, own_chips)
     own_sum, to_x, to_y = backward(cross_pairs, cross_spec, bands, [], cross_held)
-    sums = [own_sum, permuted(to_x, "band", 1), permuted(to_y, "band", 2)]
-    (total,) = backward(own_pair, chips, [psi], sums, own_held)
+    (total,) = backward(own_pair, chips, [psi], [own_sum], own_held)
+    sums = [total, permuted(to_x, "band", 1), permuted(to_y, "band", 2)]
+    (total,) = call(sum_kernel, psi.shape, 1, None, *sums)
     return total[None]
 
 

time: 137 us -> 136 us (level)
  starting transfers between devices: 45.1 us -> 41.5 us
  waiting for transfers between devices: 80.2 us -> 82.4 us
    ppermute x26, starting transfers between devices: 45.1 us -> 41.5 us  [permuted(): lax.ppermute(value, axis, [(source, source ^ mask) for source in range(co...]
    ppermute x26, waiting for transfers between devices: 80.2 us -> 82.4 us  [permuted(): lax.ppermute(value, axis, [(source, source ^ mask) for source in range(co...]
    pallas_call x6 -> x7, Pallas kernels: 8.2 us -> 8.31 us  [call(): pl.pallas_call(body, out_shape=[jax.ShapeDtypeStruct(shape, jnp.float32)]...]
  transfers between devices with their start and end apart: 26 -> 26, of which waited for: 14 -> 15; matrix products, arithmetic and copies ran while one was open for 0% -> 0% of each run, Pallas kernels for 3% -> 4%
where the time goes in v3:
time: 136 us
  waiting for transfers between devices  82.4 us (61%)
  starting transfers between devices  41.5 us (31%)
  Pallas kernels  8.31 us (6%)
  local copies, waits for them, and re-layouts  3.14 us (2%)
    ppermute x26, waiting for transfers between devices, permuted(): lax.ppermute(value, axis, [(source, source ^ mask) for source in range(co...  82.4 us
    ppermute x26, starting transfers between devices, permuted(): lax.ppermute(value, axis, [(source, source ^ mask) for source in range(co...  41.5 us
    pallas_call x7, Pallas kernels, call(): pl.pallas_call(body, out_shape=[jax.ShapeDtypeStruct(shape, jnp.float32)]...  8.31 us
  transfers between devices with their start and end apart: 26, of which 15 were waited for; matrix products, arithmetic and copies ran while one was open for 0% of the time, Pallas kernels for 4%

profile of v3, /device:TPU:0, one launch (start us, length us, event | category | flops | bytes accessed | tf_op | source)
XLA Modules:
  0.0 135.7 jit_solution(15274916779757615339)
XLA Ops:
  0.0 3.0 %collective-permute-start.4 = (f32[16,128,128]{2,1,0:T(8,128)}, f32[16,128,128]{2,1,0:T(8,128)S(1)}, u32[]{:S(2)}, u32[]{:S(2)}) collective-permute-start(f32[16,128,128]{2,1,0:T(8,128)} %bitcast.2), channel_id=1, source_target_pairs={{0,16},{8,24},{16,0},{24,8},{1,17},{9,25},{17,1},{25,9},{2,18},{10... | collective-permute-start | bytes 3145736 | tf_op jit(solution)/shard_map/ppermute | solution.py:325
  7.5 3.7 %collective-permute-start = (f32[1,32,16,128]{3,2,1,0:T(8,128)S(1)}, f32[1,32,16,128]{3,2,1,0:T(8,128)S(1)}, u32[]{:S(2)}, u32[]{:S(2)}) collective-permute-start(f32[1,32,16,128]{3,2,1,0:T(8,128)S(1)} %get-tuple-element.47), channel_id=1, source_target_pairs={{0,6},{1,7},{2,4},{3,5},{4,2},{5,3},{6,0},{7,1},{8,14},{9,15},{10,... | collective-permute-start | bytes 786440 | tf_op jit(solution)/shard_map/ppermute | solution.py:325
  11.9 14.4 %collective-permute-done.4.rest_2_.rest_10_ = f32[16,128,128]{2,1,0:T(8,128)S(1)} collective-permute-done((f32[16,128,128]{2,1,0:T(8,128)}, f32[16,128,128]{2,1,0:T(8,128)S(1)}, u32[]{:S(2)}, u32[]{:S(2)}) %collective-permute-start.4) | collective-permute-done | bytes 1048608 | tf_op jit(solution)/shard_map/ppermute | solution.py:325
  29.3 1.9 %collective-permute-start.5 = (f32[3,8,16,128]{3,2,1,0:T(8,128)S(1)}, f32[3,8,16,128]{3,2,1,0:T(8,128)S(1)}, u32[]{:S(2)}, u32[]{:S(2)}) collective-permute-start(f32[3,8,16,128]{3,2,1,0:T(8,128)S(1)} %get-tuple-element.51), channel_id=1, source_target_pairs={{0,7},{1,6},{2,5},{3,4},{4,3},{5,2},{6,1},{7,0},{8,15},{9,14},{10,... | collective-permute-start | bytes 589832 | tf_op jit(solution)/shard_map/ppermute | solution.py:325
  31.3 1.6 %collective-permute-done.1.rest_1_ = f32[1,32,16,128]{3,2,1,0:T(8,128)S(1)} collective-permute-done((f32[1,32,16,128]{3,2,1,0:T(8,128)S(1)}, f32[1,32,16,128]{3,2,1,0:T(8,128)S(1)}, u32[]{:S(2)}, u32[]{:S(2)}) %collective-permute-start.1) | collective-permute-done | bytes 262176 | tf_op jit(solution)/shard_map/ppermute | solution.py:325
  32.9 5.4 %collective-permute-done.5.rest_0_ = f32[3,8,16,128]{3,2,1,0:T(8,128)S(1)} collective-permute-done((f32[3,8,16,128]{3,2,1,0:T(8,128)S(1)}, f32[3,8,16,128]{3,2,1,0:T(8,128)S(1)}, u32[]{:S(2)}, u32[]{:S(2)}) %collective-permute-start.5) | collective-permute-done | bytes 196640 | tf_op jit(solution)/shard_map/ppermute | solution.py:325
  39.9 2.7 %collective-permute-start.9 = (f32[3,8,16,128]{3,2,1,0:T(8,128)S(1)}, f32[3,8,16,128]{3,2,1,0:T(8,128)S(1)}, u32[]{:S(2)}, u32[]{:S(2)}) collective-permute-start(f32[3,8,16,128]{3,2,1,0:T(8,128)S(1)} %get-tuple-element.60), channel_id=1, source_target_pairs={{0,6},{1,7},{2,4},{3,5},{4,2},{5,3},{6,0},{7,1},{8,14},{9,15},{10,... | collective-permute-start | bytes 589832 | tf_op jit(solution)/shard_map/ppermute | solution.py:325
  43.6 2.9 %collective-permute-start.10 = (f32[3,8,16,128]{3,2,1,0:T(8,128)S(1)}, f32[3,8,16,128]{3,2,1,0:T(8,128)S(1)}, u32[]{:S(2)}, u32[]{:S(2)}) collective-permute-start(f32[3,8,16,128]{3,2,1,0:T(8,128)S(1)} %get-tuple-element.61), channel_id=1, source_target_pairs={{0,2},{1,3},{2,0},{3,1},{4,6},{5,7},{6,4},{7,5},{8,10},{9,11},{10,... | collective-permute-start | bytes 589832 | tf_op jit(solution)/shard_map/ppermute | solution.py:325
  47.0 1.8 %collective-permute-start.12 = (f32[3,8,16,128]{3,2,1,0:T(8,128)S(1)}, f32[3,8,16,128]{3,2,1,0:T(8,128)S(1)}, u32[]{:S(2)}, u32[]{:S(2)}) collective-permute-start(f32[3,8,16,128]{3,2,1,0:T(8,128)S(1)} %get-tuple-element.63), channel_id=1, source_target_pairs={{0,3},{1,2},{2,1},{3,0},{4,7},{5,6},{6,5},{7,4},{8,11},{9,10},{10,... | collective-permute-start | bytes 589832 | tf_op jit(solution)/shard_map/ppermute | solution.py:325
  48.8 6.3 %collective-permute-start.13 = (f32[3,8,16,128]{3,2,1,0:T(8,128)S(1)}, f32[3,8,16,128]{3,2,1,0:T(8,128)S(1)}, u32[]{:S(2)}, u32[]{:S(2)}) collective-permute-start(f32[3,8,16,128]{3,2,1,0:T(8,128)S(1)} %get-tuple-element.64), channel_id=1, source_target_pairs={{0,4},{1,5},{2,6},{3,7},{4,0},{5,1},{6,2},{7,3},{8,12},{9,13},{10,... | collective-permute-start | bytes 589832 | tf_op jit(solution)/shard_map/ppermute | solution.py:325
  55.1 6.1 %collective-permute-done.11.rest_4_ = f32[3,8,16,128]{3,2,1,0:T(8,128)S(1)} collective-permute-done((f32[3,8,16,128]{3,2,1,0:T(8,128)S(1)}, f32[3,8,16,128]{3,2,1,0:T(8,128)S(1)}, u32[]{:S(2)}, u32[]{:S(2)}) %collective-permute-start.11) | collective-permute-done | bytes 196640 | tf_op jit(solution)/shard_map/ppermute | solution.py:325
  61.2 8.4 %collective-permute-done.13.rest_6_ = f32[3,8,16,128]{3,2,1,0:T(8,128)S(1)} collective-permute-done((f32[3,8,16,128]{3,2,1,0:T(8,128)S(1)}, f32[3,8,16,128]{3,2,1,0:T(8,128)S(1)}, u32[]{:S(2)}, u32[]{:S(2)}) %collective-permute-start.13) | collective-permute-done | bytes 196640 | tf_op jit(solution)/shard_map/ppermute | solution.py:325
  71.0 2.8 %collective-permute-start.15 = (f32[3,8,16,128]{3,2,1,0:T(8,128)S(1)}, f32[3,8,16,128]{3,2,1,0:T(8,128)S(1)}, u32[]{:S(2)}, u32[]{:S(2)}) collective-permute-start(f32[3,8,16,128]{3,2,1,0:T(8,128)S(1)} %get-tuple-element.67), channel_id=1, source_target_pairs={{0,7},{1,6},{2,5},{3,4},{4,3},{5,2},{6,1},{7,0},{8,15},{9,14},{10,... | collective-permute-start | bytes 589832 | tf_op jit(solution)/shard_map/ppermute | solution.py:325
  75.3 2.8 %collective-permute-start.19 = (f32[3,8,16,128]{3,2,1,0:T(8,128)S(1)}, f32[3,8,16,128]{3,2,1,0:T(8,128)S(1)}, u32[]{:S(2)}, u32[]{:S(2)}) collective-permute-start(f32[3,8,16,128]{3,2,1,0:T(8,128)S(1)} %get-tuple-element.71), channel_id=1, source_target_pairs={{0,5},{1,4},{2,7},{3,6},{4,1},{5,0},{6,3},{7,2},{8,13},{9,12},{10,... | collective-permute-start | bytes 589832 | tf_op jit(solution)/shard_map/ppermute | solution.py:325
  79.6 2.2 %collective-permute-start.20 = (f32[3,8,16,128]{3,2,1,0:T(8,128)S(1)}, f32[3,8,16,128]{3,2,1,0:T(8,128)S(1)}, u32[]{:S(2)}, u32[]{:S(2)}) collective-permute-start(f32[3,8,16,128]{3,2,1,0:T(8,128)S(1)} %get-tuple-element.72), channel_id=1, source_target_pairs={{0,4},{1,5},{2,6},{3,7},{4,0},{5,1},{6,2},{7,3},{8,12},{9,13},{10,... | collective-permute-start | bytes 589832 | tf_op jit(solution)/shard_map/ppermute | solution.py:325
  81.9 3.1 %collective-permute-done.16.rest_2_ = f32[3,8,16,128]{3,2,1,0:T(8,128)S(1)} collective-permute-done((f32[3,8,16,128]{3,2,1,0:T(8,128)S(1)}, f32[3,8,16,128]{3,2,1,0:T(8,128)S(1)}, u32[]{:S(2)}, u32[]{:S(2)}) %collective-permute-start.16) | collective-permute-done | bytes 196640 | tf_op jit(solution)/shard_map/ppermute | solution.py:325
  85.0 4.2 %collective-permute-done.17.rest_3_ = f32[3,8,16,128]{3,2,1,0:T(8,128)S(1)} collective-permute-done((f32[3,8,16,128]{3,2,1,0:T(8,128)S(1)}, f32[3,8,16,128]{3,2,1,0:T(8,128)S(1)}, u32[]{:S(2)}, u32[]{:S(2)}) %collective-permute-start.17) | collective-permute-done | bytes 196640 | tf_op jit(solution)/shard_map/ppermute | solution.py:325
  89.1 6.2 %collective-permute-done.18.rest_4_ = f32[3,8,16,128]{3,2,1,0:T(8,128)S(1)} collective-permute-done((f32[3,8,16,128]{3,2,1,0:T(8,128)S(1)}, f32[3,8,16,128]{3,2,1,0:T(8,128)S(1)}, u32[]{:S(2)}, u32[]{:S(2)}) %collective-permute-start.18) | collective-permute-done | bytes 196640 | tf_op jit(solution)/shard_map/ppermute | solution.py:325
  95.4 6.9 %collective-permute-done.19.rest_5_ = f32[3,8,16,128]{3,2,1,0:T(8,128)S(1)} collective-permute-done((f32[3,8,16,128]{3,2,1,0:T(8,128)S(1)}, f32[3,8,16,128]{3,2,1,0:T(8,128)S(1)}, u32[]{:S(2)}, u32[]{:S(2)}) %collective-permute-start.19) | collective-permute-done | bytes 196640 | tf_op jit(solution)/shard_map/ppermute | solution.py:325
  102.3 4.8 %collective-permute-done.20.rest_6_ = f32[3,8,16,128]{3,2,1,0:T(8,128)S(1)} collective-permute-done((f32[3,8,16,128]{3,2,1,0:T(8,128)S(1)}, f32[3,8,16,128]{3,2,1,0:T(8,128)S(1)}, u32[]{:S(2)}, u32[]{:S(2)}) %collective-permute-start.20) | collective-permute-done | bytes 196640 | tf_op jit(solution)/shard_map/ppermute | solution.py:325
  107.1 1.6 %shard_map.32 = (f32[16,128,128]{2,1,0:T(8,128)S(1)}, f32[16,128,128]{2,1,0:T(8,128)S(1)}, f32[16,128,128]{2,1,0:T(8,128)S(1)}) custom-call(f32[128,128]{1,0:T(8,128)S(1)} %copy-done.2, f32[3,8,16,128]{3,2,1,0:T(8,128)S(1)} %collective-permute-done.14.rest_0_, f32[3,8,16,128]{3,2,1,0:T(8,128)S(1)} %collective-permute-done.15.rest_1_, ...), custom_call_target="tpu_custom_call" | custom-call | tf_op jit(solution)/shard_map/pallas_call | solution.py:340
  112.0 3.2 %collective-permute-start.23 = (f32[1,32,16,128]{3,2,1,0:T(8,128)S(1)}, f32[1,32,16,128]{3,2,1,0:T(8,128)S(1)}, u32[]{:S(2)}, u32[]{:S(2)}) collective-permute-start(f32[1,32,16,128]{3,2,1,0:T(8,128)S(1)} %get-tuple-element.76), channel_id=1, source_target_pairs={{0,2},{1,3},{2,0},{3,1},{4,6},{5,7},{6,4},{7,5},{8,10},{9,11},{10,... | collective-permute-start | bytes 786440 | tf_op jit(solution)/shard_map/ppermute | solution.py:325
  115.2 6.8 %collective-permute-done.21.rest_0_ = f32[1,32,16,128]{3,2,1,0:T(8,128)S(1)} collective-permute-done((f32[1,32,16,128]{3,2,1,0:T(8,128)S(1)}, f32[1,32,16,128]{3,2,1,0:T(8,128)S(1)}, u32[]{:S(2)}, u32[]{:S(2)}) %collective-permute-start.21) | collective-permute-done | bytes 262176 | tf_op jit(solution)/shard_map/ppermute | solution.py:325
  122.0 11.2 %collective-permute-done.22.rest_1_ = f32[1,32,16,128]{3,2,1,0:T(8,128)S(1)} collective-permute-done((f32[1,32,16,128]{3,2,1,0:T(8,128)S(1)}, f32[1,32,16,128]{3,2,1,0:T(8,128)S(1)}, u32[]{:S(2)}, u32[]{:S(2)}) %collective-permute-start.22) | collective-permute-done | bytes 262176 | tf_op jit(solution)/shard_map/ppermute | solution.py:325
  (60 shorter events, 21.8 us)
Async XLA Ops:
  0.0 26.3 %collective-permute-start.4 = (f32[16,128,128]{2,1,0:T(8,128)}, f32[16,128,128]{2,1,0:T(8,128)S(1)}, u32[]{:S(2)}, u32[]{:S(2)}) collective-permute-start(f32[16,128,128]{2,1,0:T(8,128)} %bitcast.2), channel_id=1, source_target_pairs={{0,16},{8,24},{16,0},{24,8},{1,17},{9,25},{17,1},{25,9},{2,18},{10... | collective-permute-start | bytes 3145736 | tf_op jit(solution)/shard_map/ppermute | solution.py:325
  3.0 24.8 %collective-permute-start.3 = (f32[16,128,128]{2,1,0:T(8,128)}, f32[16,128,128]{2,1,0:T(8,128)S(1)}, u32[]{:S(2)}, u32[]{:S(2)}) collective-permute-start(f32[16,128,128]{2,1,0:T(8,128)} %bitcast.3), channel_id=1, source_target_pairs={{0,8},{8,0},{16,24},{24,16},{1,9},{9,1},{17,25},{25,17},{2,10},{10... | collective-permute-start | bytes 3145736 | tf_op jit(solution)/shard_map/ppermute | solution.py:325
  7.5 23.8 %collective-permute-start = (f32[1,32,16,128]{3,2,1,0:T(8,128)S(1)}, f32[1,32,16,128]{3,2,1,0:T(8,128)S(1)}, u32[]{:S(2)}, u32[]{:S(2)}) collective-permute-start(f32[1,32,16,128]{3,2,1,0:T(8,128)S(1)} %get-tuple-element.47), channel_id=1, source_target_pairs={{0,6},{1,7},{2,4},{3,5},{4,2},{5,3},{6,0},{7,1},{8,14},{9,15},{10,... | collective-permute-start | bytes 786440 | tf_op jit(solution)/shard_map/ppermute | solution.py:325
  11.1 21.8 %collective-permute-start.1 = (f32[1,32,16,128]{3,2,1,0:T(8,128)S(1)}, f32[1,32,16,128]{3,2,1,0:T(8,128)S(1)}, u32[]{:S(2)}, u32[]{:S(2)}) collective-permute-start(f32[1,32,16,128]{3,2,1,0:T(8,128)S(1)} %get-tuple-element.48), channel_id=1, source_target_pairs={{0,4},{1,5},{2,6},{3,7},{4,0},{5,1},{6,2},{7,3},{8,12},{9,13},{10,... | collective-permute-start | bytes 786440 | tf_op jit(solution)/shard_map/ppermute | solution.py:325
  11.1 21.8 %collective-permute-start.2 = (f32[1,32,16,128]{3,2,1,0:T(8,128)S(1)}, f32[1,32,16,128]{3,2,1,0:T(8,128)S(1)}, u32[]{:S(2)}, u32[]{:S(2)}) collective-permute-start(f32[1,32,16,128]{3,2,1,0:T(8,128)S(1)} %get-tuple-element.49), channel_id=1, source_target_pairs={{0,2},{1,3},{2,0},{3,1},{4,6},{5,7},{6,4},{7,5},{8,10},{9,11},{10,... | collective-permute-start | bytes 786440 | tf_op jit(solution)/shard_map/ppermute | solution.py:325
  29.3 8.9 %collective-permute-start.5 = (f32[3,8,16,128]{3,2,1,0:T(8,128)S(1)}, f32[3,8,16,128]{3,2,1,0:T(8,128)S(1)}, u32[]{:S(2)}, u32[]{:S(2)}) collective-permute-start(f32[3,8,16,128]{3,2,1,0:T(8,128)S(1)} %get-tuple-element.51), channel_id=1, source_target_pairs={{0,7},{1,6},{2,5},{3,4},{4,3},{5,2},{6,1},{7,0},{8,15},{9,14},{10,... | collective-permute-start | bytes 589832 | tf_op jit(solution)/shard_map/ppermute | solution.py:325
  39.4 7.6 %collective-permute-start.8 = (f32[3,8,16,128]{3,2,1,0:T(8,128)S(1)}, f32[3,8,16,128]{3,2,1,0:T(8,128)S(1)}, u32[]{:S(2)}, u32[]{:S(2)}) collective-permute-start(f32[3,8,16,128]{3,2,1,0:T(8,128)S(1)} %get-tuple-element.59), channel_id=1, source_target_pairs={{0,1},{1,0},{2,3},{3,2},{4,5},{5,4},{6,7},{7,6},{8,9},{9,8},{10,11... | collective-permute-start | bytes 589832 | tf_op jit(solution)/shard_map/ppermute | solution.py:325
  39.9 9.0 %collective-permute-start.9 = (f32[3,8,16,128]{3,2,1,0:T(8,128)S(1)}, f32[3,8,16,128]{3,2,1,0:T(8,128)S(1)}, u32[]{:S(2)}, u32[]{:S(2)}) collective-permute-start(f32[3,8,16,128]{3,2,1,0:T(8,128)S(1)} %get-tuple-element.60), channel_id=1, source_target_pairs={{0,6},{1,7},{2,4},{3,5},{4,2},{5,3},{6,0},{7,1},{8,14},{9,15},{10,... | collective-permute-start | bytes 589832 | tf_op jit(solution)/shard_map/ppermute | solution.py:325
  43.5 31.4 %collective-permute-start.7 = (f32[1,64,16,128]{3,2,1,0:T(8,128)S(1)}, f32[1,64,16,128]{3,2,1,0:T(8,128)S(1)}, u32[]{:S(2)}, u32[]{:S(2)}) collective-permute-start(f32[1,64,16,128]{3,2,1,0:T(8,128)S(1)} %get-tuple-element.57), channel_id=1, source_target_pairs={{0,1},{1,0},{2,3},{3,2},{4,5},{5,4},{6,7},{7,6},{8,9},{9,8},{10,11... | collective-permute-start | bytes 1572872 | tf_op jit(solution)/shard_map/ppermute | solution.py:325
  43.6 11.5 %collective-permute-start.10 = (f32[3,8,16,128]{3,2,1,0:T(8,128)S(1)}, f32[3,8,16,128]{3,2,1,0:T(8,128)S(1)}, u32[]{:S(2)}, u32[]{:S(2)}) collective-permute-start(f32[3,8,16,128]{3,2,1,0:T(8,128)S(1)} %get-tuple-element.61), channel_id=1, source_target_pairs={{0,2},{1,3},{2,0},{3,1},{4,6},{5,7},{6,4},{7,5},{8,10},{9,11},{10,... | collective-permute-start | bytes 589832 | tf_op jit(solution)/shard_map/ppermute | solution.py:325
  46.4 14.8 %collective-permute-start.11 = (f32[3,8,16,128]{3,2,1,0:T(8,128)S(1)}, f32[3,8,16,128]{3,2,1,0:T(8,128)S(1)}, u32[]{:S(2)}, u32[]{:S(2)}) collective-permute-start(f32[3,8,16,128]{3,2,1,0:T(8,128)S(1)} %get-tuple-element.62), channel_id=1, source_target_pairs={{0,5},{1,4},{2,7},{3,6},{4,1},{5,0},{6,3},{7,2},{8,13},{9,12},{10,... | collective-permute-start | bytes 589832 | tf_op jit(solution)/shard_map/ppermute | solution.py:325
  47.0 14.2 %collective-permute-start.12 = (f32[3,8,16,128]{3,2,1,0:T(8,128)S(1)}, f32[3,8,16,128]{3,2,1,0:T(8,128)S(1)}, u32[]{:S(2)}, u32[]{:S(2)}) collective-permute-start(f32[3,8,16,128]{3,2,1,0:T(8,128)S(1)} %get-tuple-element.63), channel_id=1, source_target_pairs={{0,3},{1,2},{2,1},{3,0},{4,7},{5,6},{6,5},{7,4},{8,11},{9,10},{10,... | collective-permute-start | bytes 589832 | tf_op jit(solution)/shard_map/ppermute | solution.py:325
  48.8 20.8 %collective-permute-start.13 = (f32[3,8,16,128]{3,2,1,0:T(8,128)S(1)}, f32[3,8,16,128]{3,2,1,0:T(8,128)S(1)}, u32[]{:S(2)}, u32[]{:S(2)}) collective-permute-start(f32[3,8,16,128]{3,2,1,0:T(8,128)S(1)} %get-tuple-element.64), channel_id=1, source_target_pairs={{0,4},{1,5},{2,6},{3,7},{4,0},{5,1},{6,2},{7,3},{8,12},{9,13},{10,... | collective-permute-start | bytes 589832 | tf_op jit(solution)/shard_map/ppermute | solution.py:325
  71.0 8.7 %collective-permute-start.15 = (f32[3,8,16,128]{3,2,1,0:T(8,128)S(1)}, f32[3,8,16,128]{3,2,1,0:T(8,128)S(1)}, u32[]{:S(2)}, u32[]{:S(2)}) collective-permute-start(f32[3,8,16,128]{3,2,1,0:T(8,128)S(1)} %get-tuple-element.67), channel_id=1, source_target_pairs={{0,7},{1,6},{2,5},{3,4},{4,3},{5,2},{6,1},{7,0},{8,15},{9,14},{10,... | collective-permute-start | bytes 589832 | tf_op jit(solution)/shard_map/ppermute | solution.py:325
  73.8 11.2 %collective-permute-start.16 = (f32[3,8,16,128]{3,2,1,0:T(8,128)S(1)}, f32[3,8,16,128]{3,2,1,0:T(8,128)S(1)}, u32[]{:S(2)}, u32[]{:S(2)}) collective-permute-start(f32[3,8,16,128]{3,2,1,0:T(8,128)S(1)} %get-tuple-element.68), channel_id=1, source_target_pairs={{0,2},{1,3},{2,0},{3,1},{4,6},{5,7},{6,4},{7,5},{8,10},{9,11},{10,... | collective-permute-start | bytes 589832 | tf_op jit(solution)/shard_map/ppermute | solution.py:325
  73.8 15.4 %collective-permute-start.17 = (f32[3,8,16,128]{3,2,1,0:T(8,128)S(1)}, f32[3,8,16,128]{3,2,1,0:T(8,128)S(1)}, u32[]{:S(2)}, u32[]{:S(2)}) collective-permute-start(f32[3,8,16,128]{3,2,1,0:T(8,128)S(1)} %get-tuple-element.69), channel_id=1, source_target_pairs={{0,6},{1,7},{2,4},{3,5},{4,2},{5,3},{6,0},{7,1},{8,14},{9,15},{10,... | collective-permute-start | bytes 589832 | tf_op jit(solution)/shard_map/ppermute | solution.py:325
  74.9 20.4 %collective-permute-start.18 = (f32[3,8,16,128]{3,2,1,0:T(8,128)S(1)}, f32[3,8,16,128]{3,2,1,0:T(8,128)S(1)}, u32[]{:S(2)}, u32[]{:S(2)}) collective-permute-start(f32[3,8,16,128]{3,2,1,0:T(8,128)S(1)} %get-tuple-element.70), channel_id=1, source_target_pairs={{0,3},{1,2},{2,1},{3,0},{4,7},{5,6},{6,5},{7,4},{8,11},{9,10},{10,... | collective-permute-start | bytes 589832 | tf_op jit(solution)/shard_map/ppermute | solution.py:325
  75.3 26.9 %collective-permute-start.19 = (f32[3,8,16,128]{3,2,1,0:T(8,128)S(1)}, f32[3,8,16,128]{3,2,1,0:T(8,128)S(1)}, u32[]{:S(2)}, u32[]{:S(2)}) collective-permute-start(f32[3,8,16,128]{3,2,1,0:T(8,128)S(1)} %get-tuple-element.71), channel_id=1, source_target_pairs={{0,5},{1,4},{2,7},{3,6},{4,1},{5,0},{6,3},{7,2},{8,13},{9,12},{10,... | collective-permute-start | bytes 589832 | tf_op jit(solution)/shard_map/ppermute | solution.py:325
  79.6 27.4 %collective-permute-start.20 = (f32[3,8,16,128]{3,2,1,0:T(8,128)S(1)}, f32[3,8,16,128]{3,2,1,0:T(8,128)S(1)}, u32[]{:S(2)}, u32[]{:S(2)}) collective-permute-start(f32[3,8,16,128]{3,2,1,0:T(8,128)S(1)} %get-tuple-element.72), channel_id=1, source_target_pairs={{0,4},{1,5},{2,6},{3,7},{4,0},{5,1},{6,2},{7,3},{8,12},{9,13},{10,... | collective-permute-start | bytes 589832 | tf_op jit(solution)/shard_map/ppermute | solution.py:325
  108.7 25.5 %collective-permute-start.24 = (f32[16,128,128]{2,1,0:T(8,128)S(1)}, f32[16,128,128]{2,1,0:T(8,128)S(1)}, u32[]{:S(2)}, u32[]{:S(2)}) collective-permute-start(f32[16,128,128]{2,1,0:T(8,128)S(1)} %get-tuple-element.87), channel_id=1, source_target_pairs={{0,8},{8,0},{16,24},{24,16},{1,9},{9,1},{17,25},{25,17},{2,10},{10... | collective-permute-start | bytes 3145736 | tf_op jit(solution)/shard_map/ppermute | solution.py:325
  110.2 24.3 %collective-permute-start.25 = (f32[16,128,128]{2,1,0:T(8,128)S(1)}, f32[16,128,128]{2,1,0:T(8,128)S(1)}, u32[]{:S(2)}, u32[]{:S(2)}) collective-permute-start(f32[16,128,128]{2,1,0:T(8,128)S(1)} %get-tuple-element.88), channel_id=1, source_target_pairs={{0,16},{8,24},{16,0},{24,8},{1,17},{9,25},{17,1},{25,9},{2,18},{10... | collective-permute-start | bytes 3145736 | tf_op jit(solution)/shard_map/ppermute | solution.py:325
  110.8 11.1 %collective-permute-start.21 = (f32[1,32,16,128]{3,2,1,0:T(8,128)S(1)}, f32[1,32,16,128]{3,2,1,0:T(8,128)S(1)}, u32[]{:S(2)}, u32[]{:S(2)}) collective-permute-start(f32[1,32,16,128]{3,2,1,0:T(8,128)S(1)} %get-tuple-element.74), channel_id=1, source_target_pairs={{0,6},{1,7},{2,4},{3,5},{4,2},{5,3},{6,0},{7,1},{8,14},{9,15},{10,... | collective-permute-start | bytes 786440 | tf_op jit(solution)/shard_map/ppermute | solution.py:325
  112.0 21.2 %collective-permute-start.22 = (f32[1,32,16,128]{3,2,1,0:T(8,128)S(1)}, f32[1,32,16,128]{3,2,1,0:T(8,128)S(1)}, u32[]{:S(2)}, u32[]{:S(2)}) collective-permute-start(f32[1,32,16,128]{3,2,1,0:T(8,128)S(1)} %get-tuple-element.75), channel_id=1, source_target_pairs={{0,4},{1,5},{2,6},{3,7},{4,0},{5,1},{6,2},{7,3},{8,12},{9,13},{10,... | collective-permute-start | bytes 786440 | tf_op jit(solution)/shard_map/ppermute | solution.py:325
  112.0 21.2 %collective-permute-start.23 = (f32[1,32,16,128]{3,2,1,0:T(8,128)S(1)}, f32[1,32,16,128]{3,2,1,0:T(8,128)S(1)}, u32[]{:S(2)}, u32[]{:S(2)}) collective-permute-start(f32[1,32,16,128]{3,2,1,0:T(8,128)S(1)} %get-tuple-element.76), channel_id=1, source_target_pairs={{0,2},{1,3},{2,0},{3,1},{4,6},{5,7},{6,4},{7,5},{8,10},{9,11},{10,... | collective-permute-start | bytes 786440 | tf_op jit(solution)/shard_map/ppermute | solution.py:325
  (11 other events, 55.9 us)

commit v4 on v3

--- a/solution.py
+++ b/solution.py
@@ -222,9 +222,9 @@
                     :, side * length : (side + 1) * length
                 ]
     for k, ref in enumerate(out_refs):
-        for f in range(len(fields)):
-            spec = right_apply(held[f, k * piece : (k + 1) * piece, :], z_parts)
-            ref[f] = spec.reshape(per_slab, planes, length)
+        rows = [held[f, k * piece : (k + 1) * piece, :] for f in range(len(fields))]
+        spec = right_apply(jnp.concatenate(rows, axis=0), z_parts)
+        ref[...] = spec.reshape(ref.shape)
 
 
 def folded_square(position, length):
@@ -297,10 +297,9 @@
     y_parts = [left_table(table.T) for table in y_tables(fields, slabs, table_ref, True)]
     rows = per_slab * planes
     for k, ref in enumerate(spec_refs):
+        spec = right_apply(ref[...].reshape(len(fields) * rows, length), z_parts)
         for f in range(len(fields)):
-            held[f, k * rows : (k + 1) * rows, :] = right_apply(
-                ref[f].reshape(rows, length), z_parts
-            )
+            held[f, k * rows : (k + 1) * rows, :] = spec[f * rows : (f + 1) * rows]
     for first in range(0, planes, 2):
         psi = [two_planes(ref, first) for ref in psi_refs]
         sums = [None] * bands

time: 136 us -> 136 us (level)
  no operation moved by 1% of the time
where the time goes in v4:
time: 136 us
  waiting for transfers between devices  82.4 us (61%)
  starting transfers between devices  41.5 us (31%)
  Pallas kernels  8.21 us (6%)
  local copies, waits for them, and re-layouts  3.14 us (2%)
    ppermute x26, waiting for transfers between devices, permuted(): lax.ppermute(value, axis, [(source, source ^ mask) for source in range(co...  82.4 us
    ppermute x26, starting transfers between devices, permuted(): lax.ppermute(value, axis, [(source, source ^ mask) for source in range(co...  41.5 us
    pallas_call x7, Pallas kernels, call(): pl.pallas_call(body, out_shape=[jax.ShapeDtypeStruct(shape, jnp.float32)]...  8.21 us
  transfers between devices with their start and end apart: 26, of which 15 were waited for; matrix products, arithmetic and copies ran while one was open for 0% of the time, Pallas kernels for 4%

profile of v4, /device:TPU:0, one launch (start us, length us, event | category | flops | bytes accessed | tf_op | source)
XLA Modules:
  0.0 135.6 jit_solution(13208648382208122712)
XLA Ops:
  0.0 3.0 %collective-permute-start.4 = (f32[16,128,128]{2,1,0:T(8,128)}, f32[16,128,128]{2,1,0:T(8,128)S(1)}, u32[]{:S(2)}, u32[]{:S(2)}) collective-permute-start(f32[16,128,128]{2,1,0:T(8,128)} %bitcast.2), channel_id=1, source_target_pairs={{0,16},{8,24},{16,0},{24,8},{1,17},{9,25},{17,1},{25,9},{2,18},{10... | collective-permute-start | bytes 3145736 | tf_op jit(solution)/shard_map/ppermute | solution.py:324
  7.5 3.7 %collective-permute-start = (f32[1,32,16,128]{3,2,1,0:T(8,128)S(1)}, f32[1,32,16,128]{3,2,1,0:T(8,128)S(1)}, u32[]{:S(2)}, u32[]{:S(2)}) collective-permute-start(f32[1,32,16,128]{3,2,1,0:T(8,128)S(1)} %get-tuple-element.47), channel_id=1, source_target_pairs={{0,6},{1,7},{2,4},{3,5},{4,2},{5,3},{6,0},{7,1},{8,14},{9,15},{10,... | collective-permute-start | bytes 786440 | tf_op jit(solution)/shard_map/ppermute | solution.py:324
  11.9 14.4 %collective-permute-done.4.rest_2_.rest_10_ = f32[16,128,128]{2,1,0:T(8,128)S(1)} collective-permute-done((f32[16,128,128]{2,1,0:T(8,128)}, f32[16,128,128]{2,1,0:T(8,128)S(1)}, u32[]{:S(2)}, u32[]{:S(2)}) %collective-permute-start.4) | collective-permute-done | bytes 1048608 | tf_op jit(solution)/shard_map/ppermute | solution.py:324
  29.3 1.9 %collective-permute-start.5 = (f32[3,8,16,128]{3,2,1,0:T(8,128)S(1)}, f32[3,8,16,128]{3,2,1,0:T(8,128)S(1)}, u32[]{:S(2)}, u32[]{:S(2)}) collective-permute-start(f32[3,8,16,128]{3,2,1,0:T(8,128)S(1)} %get-tuple-element.51), channel_id=1, source_target_pairs={{0,7},{1,6},{2,5},{3,4},{4,3},{5,2},{6,1},{7,0},{8,15},{9,14},{10,... | collective-permute-start | bytes 589832 | tf_op jit(solution)/shard_map/ppermute | solution.py:324
  31.2 1.6 %collective-permute-done.1.rest_1_ = f32[1,32,16,128]{3,2,1,0:T(8,128)S(1)} collective-permute-done((f32[1,32,16,128]{3,2,1,0:T(8,128)S(1)}, f32[1,32,16,128]{3,2,1,0:T(8,128)S(1)}, u32[]{:S(2)}, u32[]{:S(2)}) %collective-permute-start.1) | collective-permute-done | bytes 262176 | tf_op jit(solution)/shard_map/ppermute | solution.py:324
  32.9 5.3 %collective-permute-done.5.rest_0_ = f32[3,8,16,128]{3,2,1,0:T(8,128)S(1)} collective-permute-done((f32[3,8,16,128]{3,2,1,0:T(8,128)S(1)}, f32[3,8,16,128]{3,2,1,0:T(8,128)S(1)}, u32[]{:S(2)}, u32[]{:S(2)}) %collective-permute-start.5) | collective-permute-done | bytes 196640 | tf_op jit(solution)/shard_map/ppermute | solution.py:324
  39.8 2.7 %collective-permute-start.9 = (f32[3,8,16,128]{3,2,1,0:T(8,128)S(1)}, f32[3,8,16,128]{3,2,1,0:T(8,128)S(1)}, u32[]{:S(2)}, u32[]{:S(2)}) collective-permute-start(f32[3,8,16,128]{3,2,1,0:T(8,128)S(1)} %get-tuple-element.60), channel_id=1, source_target_pairs={{0,6},{1,7},{2,4},{3,5},{4,2},{5,3},{6,0},{7,1},{8,14},{9,15},{10,... | collective-permute-start | bytes 589832 | tf_op jit(solution)/shard_map/ppermute | solution.py:324
  43.6 2.9 %collective-permute-start.10 = (f32[3,8,16,128]{3,2,1,0:T(8,128)S(1)}, f32[3,8,16,128]{3,2,1,0:T(8,128)S(1)}, u32[]{:S(2)}, u32[]{:S(2)}) collective-permute-start(f32[3,8,16,128]{3,2,1,0:T(8,128)S(1)} %get-tuple-element.61), channel_id=1, source_target_pairs={{0,2},{1,3},{2,0},{3,1},{4,6},{5,7},{6,4},{7,5},{8,10},{9,11},{10,... | collective-permute-start | bytes 589832 | tf_op jit(solution)/shard_map/ppermute | solution.py:324
  47.0 1.8 %collective-permute-start.12 = (f32[3,8,16,128]{3,2,1,0:T(8,128)S(1)}, f32[3,8,16,128]{3,2,1,0:T(8,128)S(1)}, u32[]{:S(2)}, u32[]{:S(2)}) collective-permute-start(f32[3,8,16,128]{3,2,1,0:T(8,128)S(1)} %get-tuple-element.63), channel_id=1, source_target_pairs={{0,3},{1,2},{2,1},{3,0},{4,7},{5,6},{6,5},{7,4},{8,11},{9,10},{10,... | collective-permute-start | bytes 589832 | tf_op jit(solution)/shard_map/ppermute | solution.py:324
  48.8 6.3 %collective-permute-start.13 = (f32[3,8,16,128]{3,2,1,0:T(8,128)S(1)}, f32[3,8,16,128]{3,2,1,0:T(8,128)S(1)}, u32[]{:S(2)}, u32[]{:S(2)}) collective-permute-start(f32[3,8,16,128]{3,2,1,0:T(8,128)S(1)} %get-tuple-element.64), channel_id=1, source_target_pairs={{0,4},{1,5},{2,6},{3,7},{4,0},{5,1},{6,2},{7,3},{8,12},{9,13},{10,... | collective-permute-start | bytes 589832 | tf_op jit(solution)/shard_map/ppermute | solution.py:324
  55.1 6.1 %collective-permute-done.11.rest_4_ = f32[3,8,16,128]{3,2,1,0:T(8,128)S(1)} collective-permute-done((f32[3,8,16,128]{3,2,1,0:T(8,128)S(1)}, f32[3,8,16,128]{3,2,1,0:T(8,128)S(1)}, u32[]{:S(2)}, u32[]{:S(2)}) %collective-permute-start.11) | collective-permute-done | bytes 196640 | tf_op jit(solution)/shard_map/ppermute | solution.py:324
  61.2 8.4 %collective-permute-done.13.rest_6_ = f32[3,8,16,128]{3,2,1,0:T(8,128)S(1)} collective-permute-done((f32[3,8,16,128]{3,2,1,0:T(8,128)S(1)}, f32[3,8,16,128]{3,2,1,0:T(8,128)S(1)}, u32[]{:S(2)}, u32[]{:S(2)}) %collective-permute-start.13) | collective-permute-done | bytes 196640 | tf_op jit(solution)/shard_map/ppermute | solution.py:324
  70.9 2.8 %collective-permute-start.15 = (f32[3,8,16,128]{3,2,1,0:T(8,128)S(1)}, f32[3,8,16,128]{3,2,1,0:T(8,128)S(1)}, u32[]{:S(2)}, u32[]{:S(2)}) collective-permute-start(f32[3,8,16,128]{3,2,1,0:T(8,128)S(1)} %get-tuple-element.67), channel_id=1, source_target_pairs={{0,7},{1,6},{2,5},{3,4},{4,3},{5,2},{6,1},{7,0},{8,15},{9,14},{10,... | collective-permute-start | bytes 589832 | tf_op jit(solution)/shard_map/ppermute | solution.py:324
  75.3 2.8 %collective-permute-start.19 = (f32[3,8,16,128]{3,2,1,0:T(8,128)S(1)}, f32[3,8,16,128]{3,2,1,0:T(8,128)S(1)}, u32[]{:S(2)}, u32[]{:S(2)}) collective-permute-start(f32[3,8,16,128]{3,2,1,0:T(8,128)S(1)} %get-tuple-element.71), channel_id=1, source_target_pairs={{0,5},{1,4},{2,7},{3,6},{4,1},{5,0},{6,3},{7,2},{8,13},{9,12},{10,... | collective-permute-start | bytes 589832 | tf_op jit(solution)/shard_map/ppermute | solution.py:324
  79.6 2.2 %collective-permute-start.20 = (f32[3,8,16,128]{3,2,1,0:T(8,128)S(1)}, f32[3,8,16,128]{3,2,1,0:T(8,128)S(1)}, u32[]{:S(2)}, u32[]{:S(2)}) collective-permute-start(f32[3,8,16,128]{3,2,1,0:T(8,128)S(1)} %get-tuple-element.72), channel_id=1, source_target_pairs={{0,4},{1,5},{2,6},{3,7},{4,0},{5,1},{6,2},{7,3},{8,12},{9,13},{10,... | collective-permute-start | bytes 589832 | tf_op jit(solution)/shard_map/ppermute | solution.py:324
  81.9 3.1 %collective-permute-done.16.rest_2_ = f32[3,8,16,128]{3,2,1,0:T(8,128)S(1)} collective-permute-done((f32[3,8,16,128]{3,2,1,0:T(8,128)S(1)}, f32[3,8,16,128]{3,2,1,0:T(8,128)S(1)}, u32[]{:S(2)}, u32[]{:S(2)}) %collective-permute-start.16) | collective-permute-done | bytes 196640 | tf_op jit(solution)/shard_map/ppermute | solution.py:324
  85.0 4.2 %collective-permute-done.17.rest_3_ = f32[3,8,16,128]{3,2,1,0:T(8,128)S(1)} collective-permute-done((f32[3,8,16,128]{3,2,1,0:T(8,128)S(1)}, f32[3,8,16,128]{3,2,1,0:T(8,128)S(1)}, u32[]{:S(2)}, u32[]{:S(2)}) %collective-permute-start.17) | collective-permute-done | bytes 196640 | tf_op jit(solution)/shard_map/ppermute | solution.py:324
  89.1 6.2 %collective-permute-done.18.rest_4_ = f32[3,8,16,128]{3,2,1,0:T(8,128)S(1)} collective-permute-done((f32[3,8,16,128]{3,2,1,0:T(8,128)S(1)}, f32[3,8,16,128]{3,2,1,0:T(8,128)S(1)}, u32[]{:S(2)}, u32[]{:S(2)}) %collective-permute-start.18) | collective-permute-done | bytes 196640 | tf_op jit(solution)/shard_map/ppermute | solution.py:324
  95.3 6.9 %collective-permute-done.19.rest_5_ = f32[3,8,16,128]{3,2,1,0:T(8,128)S(1)} collective-permute-done((f32[3,8,16,128]{3,2,1,0:T(8,128)S(1)}, f32[3,8,16,128]{3,2,1,0:T(8,128)S(1)}, u32[]{:S(2)}, u32[]{:S(2)}) %collective-permute-start.19) | collective-permute-done | bytes 196640 | tf_op jit(solution)/shard_map/ppermute | solution.py:324
  102.2 4.8 %collective-permute-done.20.rest_6_ = f32[3,8,16,128]{3,2,1,0:T(8,128)S(1)} collective-permute-done((f32[3,8,16,128]{3,2,1,0:T(8,128)S(1)}, f32[3,8,16,128]{3,2,1,0:T(8,128)S(1)}, u32[]{:S(2)}, u32[]{:S(2)}) %collective-permute-start.20) | collective-permute-done | bytes 196640 | tf_op jit(solution)/shard_map/ppermute | solution.py:324
  108.6 1.6 %collective-permute-start.24 = (f32[16,128,128]{2,1,0:T(8,128)S(1)}, f32[16,128,128]{2,1,0:T(8,128)S(1)}, u32[]{:S(2)}, u32[]{:S(2)}) collective-permute-start(f32[16,128,128]{2,1,0:T(8,128)S(1)} %get-tuple-element.87), channel_id=1, source_target_pairs={{0,8},{8,0},{16,24},{24,16},{1,9},{9,1},{17,25},{25,17},{2,10},{10... | collective-permute-start | bytes 3145736 | tf_op jit(solution)/shard_map/ppermute | solution.py:324
  111.9 3.2 %collective-permute-start.23 = (f32[1,32,16,128]{3,2,1,0:T(8,128)S(1)}, f32[1,32,16,128]{3,2,1,0:T(8,128)S(1)}, u32[]{:S(2)}, u32[]{:S(2)}) collective-permute-start(f32[1,32,16,128]{3,2,1,0:T(8,128)S(1)} %get-tuple-element.76), channel_id=1, source_target_pairs={{0,2},{1,3},{2,0},{3,1},{4,6},{5,7},{6,4},{7,5},{8,10},{9,11},{10,... | collective-permute-start | bytes 786440 | tf_op jit(solution)/shard_map/ppermute | solution.py:324
  115.1 6.8 %collective-permute-done.21.rest_0_ = f32[1,32,16,128]{3,2,1,0:T(8,128)S(1)} collective-permute-done((f32[1,32,16,128]{3,2,1,0:T(8,128)S(1)}, f32[1,32,16,128]{3,2,1,0:T(8,128)S(1)}, u32[]{:S(2)}, u32[]{:S(2)}) %collective-permute-start.21) | collective-permute-done | bytes 262176 | tf_op jit(solution)/shard_map/ppermute | solution.py:324
  121.9 11.2 %collective-permute-done.22.rest_1_ = f32[1,32,16,128]{3,2,1,0:T(8,128)S(1)} collective-permute-done((f32[1,32,16,128]{3,2,1,0:T(8,128)S(1)}, f32[1,32,16,128]{3,2,1,0:T(8,128)S(1)}, u32[]{:S(2)}, u32[]{:S(2)}) %collective-permute-start.22) | collective-permute-done | bytes 262176 | tf_op jit(solution)/shard_map/ppermute | solution.py:324
  (60 shorter events, 21.8 us)
Async XLA Ops:
  0.0 26.3 %collective-permute-start.4 = (f32[16,128,128]{2,1,0:T(8,128)}, f32[16,128,128]{2,1,0:T(8,128)S(1)}, u32[]{:S(2)}, u32[]{:S(2)}) collective-permute-start(f32[16,128,128]{2,1,0:T(8,128)} %bitcast.2), channel_id=1, source_target_pairs={{0,16},{8,24},{16,0},{24,8},{1,17},{9,25},{17,1},{25,9},{2,18},{10... | collective-permute-start | bytes 3145736 | tf_op jit(solution)/shard_map/ppermute | solution.py:324
  3.0 24.8 %collective-permute-start.3 = (f32[16,128,128]{2,1,0:T(8,128)}, f32[16,128,128]{2,1,0:T(8,128)S(1)}, u32[]{:S(2)}, u32[]{:S(2)}) collective-permute-start(f32[16,128,128]{2,1,0:T(8,128)} %bitcast.3), channel_id=1, source_target_pairs={{0,8},{8,0},{16,24},{24,16},{1,9},{9,1},{17,25},{25,17},{2,10},{10... | collective-permute-start | bytes 3145736 | tf_op jit(solution)/shard_map/ppermute | solution.py:324
  7.5 23.8 %collective-permute-start = (f32[1,32,16,128]{3,2,1,0:T(8,128)S(1)}, f32[1,32,16,128]{3,2,1,0:T(8,128)S(1)}, u32[]{:S(2)}, u32[]{:S(2)}) collective-permute-start(f32[1,32,16,128]{3,2,1,0:T(8,128)S(1)} %get-tuple-element.47), channel_id=1, source_target_pairs={{0,6},{1,7},{2,4},{3,5},{4,2},{5,3},{6,0},{7,1},{8,14},{9,15},{10,... | collective-permute-start | bytes 786440 | tf_op jit(solution)/shard_map/ppermute | solution.py:324
  11.1 21.8 %collective-permute-start.1 = (f32[1,32,16,128]{3,2,1,0:T(8,128)S(1)}, f32[1,32,16,128]{3,2,1,0:T(8,128)S(1)}, u32[]{:S(2)}, u32[]{:S(2)}) collective-permute-start(f32[1,32,16,128]{3,2,1,0:T(8,128)S(1)} %get-tuple-element.48), channel_id=1, source_target_pairs={{0,4},{1,5},{2,6},{3,7},{4,0},{5,1},{6,2},{7,3},{8,12},{9,13},{10,... | collective-permute-start | bytes 786440 | tf_op jit(solution)/shard_map/ppermute | solution.py:324
  11.1 21.8 %collective-permute-start.2 = (f32[1,32,16,128]{3,2,1,0:T(8,128)S(1)}, f32[1,32,16,128]{3,2,1,0:T(8,128)S(1)}, u32[]{:S(2)}, u32[]{:S(2)}) collective-permute-start(f32[1,32,16,128]{3,2,1,0:T(8,128)S(1)} %get-tuple-element.49), channel_id=1, source_target_pairs={{0,2},{1,3},{2,0},{3,1},{4,6},{5,7},{6,4},{7,5},{8,10},{9,11},{10,... | collective-permute-start | bytes 786440 | tf_op jit(solution)/shard_map/ppermute | solution.py:324
  29.3 8.9 %collective-permute-start.5 = (f32[3,8,16,128]{3,2,1,0:T(8,128)S(1)}, f32[3,8,16,128]{3,2,1,0:T(8,128)S(1)}, u32[]{:S(2)}, u32[]{:S(2)}) collective-permute-start(f32[3,8,16,128]{3,2,1,0:T(8,128)S(1)} %get-tuple-element.51), channel_id=1, source_target_pairs={{0,7},{1,6},{2,5},{3,4},{4,3},{5,2},{6,1},{7,0},{8,15},{9,14},{10,... | collective-permute-start | bytes 589832 | tf_op jit(solution)/shard_map/ppermute | solution.py:324
  39.4 7.6 %collective-permute-start.8 = (f32[3,8,16,128]{3,2,1,0:T(8,128)S(1)}, f32[3,8,16,128]{3,2,1,0:T(8,128)S(1)}, u32[]{:S(2)}, u32[]{:S(2)}) collective-permute-start(f32[3,8,16,128]{3,2,1,0:T(8,128)S(1)} %get-tuple-element.59), channel_id=1, source_target_pairs={{0,1},{1,0},{2,3},{3,2},{4,5},{5,4},{6,7},{7,6},{8,9},{9,8},{10,11... | collective-permute-start | bytes 589832 | tf_op jit(solution)/shard_map/ppermute | solution.py:324
  39.8 9.0 %collective-permute-start.9 = (f32[3,8,16,128]{3,2,1,0:T(8,128)S(1)}, f32[3,8,16,128]{3,2,1,0:T(8,128)S(1)}, u32[]{:S(2)}, u32[]{:S(2)}) collective-permute-start(f32[3,8,16,128]{3,2,1,0:T(8,128)S(1)} %get-tuple-element.60), channel_id=1, source_target_pairs={{0,6},{1,7},{2,4},{3,5},{4,2},{5,3},{6,0},{7,1},{8,14},{9,15},{10,... | collective-permute-start | bytes 589832 | tf_op jit(solution)/shard_map/ppermute | solution.py:324
  43.5 31.4 %collective-permute-start.7 = (f32[1,64,16,128]{3,2,1,0:T(8,128)S(1)}, f32[1,64,16,128]{3,2,1,0:T(8,128)S(1)}, u32[]{:S(2)}, u32[]{:S(2)}) collective-permute-start(f32[1,64,16,128]{3,2,1,0:T(8,128)S(1)} %get-tuple-element.57), channel_id=1, source_target_pairs={{0,1},{1,0},{2,3},{3,2},{4,5},{5,4},{6,7},{7,6},{8,9},{9,8},{10,11... | collective-permute-start | bytes 1572872 | tf_op jit(solution)/shard_map/ppermute | solution.py:324
  43.6 11.5 %collective-permute-start.10 = (f32[3,8,16,128]{3,2,1,0:T(8,128)S(1)}, f32[3,8,16,128]{3,2,1,0:T(8,128)S(1)}, u32[]{:S(2)}, u32[]{:S(2)}) collective-permute-start(f32[3,8,16,128]{3,2,1,0:T(8,128)S(1)} %get-tuple-element.61), channel_id=1, source_target_pairs={{0,2},{1,3},{2,0},{3,1},{4,6},{5,7},{6,4},{7,5},{8,10},{9,11},{10,... | collective-permute-start | bytes 589832 | tf_op jit(solution)/shard_map/ppermute | solution.py:324
  46.4 14.8 %collective-permute-start.11 = (f32[3,8,16,128]{3,2,1,0:T(8,128)S(1)}, f32[3,8,16,128]{3,2,1,0:T(8,128)S(1)}, u32[]{:S(2)}, u32[]{:S(2)}) collective-permute-start(f32[3,8,16,128]{3,2,1,0:T(8,128)S(1)} %get-tuple-element.62), channel_id=1, source_target_pairs={{0,5},{1,4},{2,7},{3,6},{4,1},{5,0},{6,3},{7,2},{8,13},{9,12},{10,... | collective-permute-start | bytes 589832 | tf_op jit(solution)/shard_map/ppermute | solution.py:324
  47.0 14.2 %collective-permute-start.12 = (f32[3,8,16,128]{3,2,1,0:T(8,128)S(1)}, f32[3,8,16,128]{3,2,1,0:T(8,128)S(1)}, u32[]{:S(2)}, u32[]{:S(2)}) collective-permute-start(f32[3,8,16,128]{3,2,1,0:T(8,128)S(1)} %get-tuple-element.63), channel_id=1, source_target_pairs={{0,3},{1,2},{2,1},{3,0},{4,7},{5,6},{6,5},{7,4},{8,11},{9,10},{10,... | collective-permute-start | bytes 589832 | tf_op jit(solution)/shard_map/ppermute | solution.py:324
  48.8 20.8 %collective-permute-start.13 = (f32[3,8,16,128]{3,2,1,0:T(8,128)S(1)}, f32[3,8,16,128]{3,2,1,0:T(8,128)S(1)}, u32[]{:S(2)}, u32[]{:S(2)}) collective-permute-start(f32[3,8,16,128]{3,2,1,0:T(8,128)S(1)} %get-tuple-element.64), channel_id=1, source_target_pairs={{0,4},{1,5},{2,6},{3,7},{4,0},{5,1},{6,2},{7,3},{8,12},{9,13},{10,... | collective-permute-start | bytes 589832 | tf_op jit(solution)/shard_map/ppermute | solution.py:324
  70.9 8.7 %collective-permute-start.15 = (f32[3,8,16,128]{3,2,1,0:T(8,128)S(1)}, f32[3,8,16,128]{3,2,1,0:T(8,128)S(1)}, u32[]{:S(2)}, u32[]{:S(2)}) collective-permute-start(f32[3,8,16,128]{3,2,1,0:T(8,128)S(1)} %get-tuple-element.67), channel_id=1, source_target_pairs={{0,7},{1,6},{2,5},{3,4},{4,3},{5,2},{6,1},{7,0},{8,15},{9,14},{10,... | collective-permute-start | bytes 589832 | tf_op jit(solution)/shard_map/ppermute | solution.py:324
  73.7 11.2 %collective-permute-start.16 = (f32[3,8,16,128]{3,2,1,0:T(8,128)S(1)}, f32[3,8,16,128]{3,2,1,0:T(8,128)S(1)}, u32[]{:S(2)}, u32[]{:S(2)}) collective-permute-start(f32[3,8,16,128]{3,2,1,0:T(8,128)S(1)} %get-tuple-element.68), channel_id=1, source_target_pairs={{0,2},{1,3},{2,0},{3,1},{4,6},{5,7},{6,4},{7,5},{8,10},{9,11},{10,... | collective-permute-start | bytes 589832 | tf_op jit(solution)/shard_map/ppermute | solution.py:324
  73.7 15.4 %collective-permute-start.17 = (f32[3,8,16,128]{3,2,1,0:T(8,128)S(1)}, f32[3,8,16,128]{3,2,1,0:T(8,128)S(1)}, u32[]{:S(2)}, u32[]{:S(2)}) collective-permute-start(f32[3,8,16,128]{3,2,1,0:T(8,128)S(1)} %get-tuple-element.69), channel_id=1, source_target_pairs={{0,6},{1,7},{2,4},{3,5},{4,2},{5,3},{6,0},{7,1},{8,14},{9,15},{10,... | collective-permute-start | bytes 589832 | tf_op jit(solution)/shard_map/ppermute | solution.py:324
  74.9 20.4 %collective-permute-start.18 = (f32[3,8,16,128]{3,2,1,0:T(8,128)S(1)}, f32[3,8,16,128]{3,2,1,0:T(8,128)S(1)}, u32[]{:S(2)}, u32[]{:S(2)}) collective-permute-start(f32[3,8,16,128]{3,2,1,0:T(8,128)S(1)} %get-tuple-element.70), channel_id=1, source_target_pairs={{0,3},{1,2},{2,1},{3,0},{4,7},{5,6},{6,5},{7,4},{8,11},{9,10},{10,... | collective-permute-start | bytes 589832 | tf_op jit(solution)/shard_map/ppermute | solution.py:324
  75.3 26.9 %collective-permute-start.19 = (f32[3,8,16,128]{3,2,1,0:T(8,128)S(1)}, f32[3,8,16,128]{3,2,1,0:T(8,128)S(1)}, u32[]{:S(2)}, u32[]{:S(2)}) collective-permute-start(f32[3,8,16,128]{3,2,1,0:T(8,128)S(1)} %get-tuple-element.71), channel_id=1, source_target_pairs={{0,5},{1,4},{2,7},{3,6},{4,1},{5,0},{6,3},{7,2},{8,13},{9,12},{10,... | collective-permute-start | bytes 589832 | tf_op jit(solution)/shard_map/ppermute | solution.py:324
  79.6 27.4 %collective-permute-start.20 = (f32[3,8,16,128]{3,2,1,0:T(8,128)S(1)}, f32[3,8,16,128]{3,2,1,0:T(8,128)S(1)}, u32[]{:S(2)}, u32[]{:S(2)}) collective-permute-start(f32[3,8,16,128]{3,2,1,0:T(8,128)S(1)} %get-tuple-element.72), channel_id=1, source_target_pairs={{0,4},{1,5},{2,6},{3,7},{4,0},{5,1},{6,2},{7,3},{8,12},{9,13},{10,... | collective-permute-start | bytes 589832 | tf_op jit(solution)/shard_map/ppermute | solution.py:324
  108.6 25.5 %collective-permute-start.24 = (f32[16,128,128]{2,1,0:T(8,128)S(1)}, f32[16,128,128]{2,1,0:T(8,128)S(1)}, u32[]{:S(2)}, u32[]{:S(2)}) collective-permute-start(f32[16,128,128]{2,1,0:T(8,128)S(1)} %get-tuple-element.87), channel_id=1, source_target_pairs={{0,8},{8,0},{16,24},{24,16},{1,9},{9,1},{17,25},{25,17},{2,10},{10... | collective-permute-start | bytes 3145736 | tf_op jit(solution)/shard_map/ppermute | solution.py:324
  110.1 24.3 %collective-permute-start.25 = (f32[16,128,128]{2,1,0:T(8,128)S(1)}, f32[16,128,128]{2,1,0:T(8,128)S(1)}, u32[]{:S(2)}, u32[]{:S(2)}) collective-permute-start(f32[16,128,128]{2,1,0:T(8,128)S(1)} %get-tuple-element.88), channel_id=1, source_target_pairs={{0,16},{8,24},{16,0},{24,8},{1,17},{9,25},{17,1},{25,9},{2,18},{10... | collective-permute-start | bytes 3145736 | tf_op jit(solution)/shard_map/ppermute | solution.py:324
  110.7 11.1 %collective-permute-start.21 = (f32[1,32,16,128]{3,2,1,0:T(8,128)S(1)}, f32[1,32,16,128]{3,2,1,0:T(8,128)S(1)}, u32[]{:S(2)}, u32[]{:S(2)}) collective-permute-start(f32[1,32,16,128]{3,2,1,0:T(8,128)S(1)} %get-tuple-element.74), channel_id=1, source_target_pairs={{0,6},{1,7},{2,4},{3,5},{4,2},{5,3},{6,0},{7,1},{8,14},{9,15},{10,... | collective-permute-start | bytes 786440 | tf_op jit(solution)/shard_map/ppermute | solution.py:324
  111.9 21.2 %collective-permute-start.22 = (f32[1,32,16,128]{3,2,1,0:T(8,128)S(1)}, f32[1,32,16,128]{3,2,1,0:T(8,128)S(1)}, u32[]{:S(2)}, u32[]{:S(2)}) collective-permute-start(f32[1,32,16,128]{3,2,1,0:T(8,128)S(1)} %get-tuple-element.75), channel_id=1, source_target_pairs={{0,4},{1,5},{2,6},{3,7},{4,0},{5,1},{6,2},{7,3},{8,12},{9,13},{10,... | collective-permute-start | bytes 786440 | tf_op jit(solution)/shard_map/ppermute | solution.py:324
  111.9 21.2 %collective-permute-start.23 = (f32[1,32,16,128]{3,2,1,0:T(8,128)S(1)}, f32[1,32,16,128]{3,2,1,0:T(8,128)S(1)}, u32[]{:S(2)}, u32[]{:S(2)}) collective-permute-start(f32[1,32,16,128]{3,2,1,0:T(8,128)S(1)} %get-tuple-element.76), channel_id=1, source_target_pairs={{0,2},{1,3},{2,0},{3,1},{4,6},{5,7},{6,4},{7,5},{8,10},{9,11},{10,... | collective-permute-start | bytes 786440 | tf_op jit(solution)/shard_map/ppermute | solution.py:324
  (11 other events, 55.9 us)

commit v5 on v3

--- a/solution.py
+++ b/solution.py
@@ -167,7 +167,10 @@
 
 
 def own_masks(slabs):
-    return [chip + core for chip in range(slabs - 2, -1, -2) for core in range(2)]
+    chips = list(range(slabs - 2, -1, -2))
+    middle = slabs // 2 // 2 - 1
+    chips.insert(0, chips.pop(middle))
+    return [chip + core for chip in chips for core in range(2)]
 
 
 def masks_of(fields, slabs, back=False):

time: 136 us -> 136 us (level)
  waiting for transfers between devices: 82.4 us -> 84 us
  starting transfers between devices: 41.5 us -> 40 us
    ppermute x26, starting transfers between devices: 41.5 us -> 40 us  [permuted(): lax.ppermute(value, axis, [(source, source ^ mask) for source in range(co...]
    ppermute x26, waiting for transfers between devices: 82.4 us -> 84 us  [permuted(): lax.ppermute(value, axis, [(source, source ^ mask) for source in range(co...]
where the time goes in v5:
time: 136 us
  waiting for transfers between devices  84 us (62%)
  starting transfers between devices  40 us (29%)
  Pallas kernels  8.31 us (6%)
  local copies, waits for them, and re-layouts  3.14 us (2%)
    ppermute x26, waiting for transfers between devices, permuted(): lax.ppermute(value, axis, [(source, source ^ mask) for source in range(co...  84 us
    ppermute x26, starting transfers between devices, permuted(): lax.ppermute(value, axis, [(source, source ^ mask) for source in range(co...  40 us
    pallas_call x7, Pallas kernels, call(): pl.pallas_call(body, out_shape=[jax.ShapeDtypeStruct(shape, jnp.float32)]...  8.31 us
  transfers between devices with their start and end apart: 26, of which 15 were waited for; matrix products, arithmetic and copies ran while one was open for 0% of the time, Pallas kernels for 4%

profile of v5, /device:TPU:0, one launch (start us, length us, event | category | flops | bytes accessed | tf_op | source)
XLA Modules:
  0.0 135.7 jit_solution(6141120950745826254)
XLA Ops:
  0.0 3.0 %collective-permute-start.4 = (f32[16,128,128]{2,1,0:T(8,128)}, f32[16,128,128]{2,1,0:T(8,128)S(1)}, u32[]{:S(2)}, u32[]{:S(2)}) collective-permute-start(f32[16,128,128]{2,1,0:T(8,128)} %bitcast.2), channel_id=1, source_target_pairs={{0,16},{8,24},{16,0},{24,8},{1,17},{9,25},{17,1},{25,9},{2,18},{10... | collective-permute-start | bytes 3145736 | tf_op jit(solution)/shard_map/ppermute | solution.py:328
  7.5 2.7 %collective-permute-start = (f32[1,32,16,128]{3,2,1,0:T(8,128)S(1)}, f32[1,32,16,128]{3,2,1,0:T(8,128)S(1)}, u32[]{:S(2)}, u32[]{:S(2)}) collective-permute-start(f32[1,32,16,128]{3,2,1,0:T(8,128)S(1)} %get-tuple-element.47), channel_id=1, source_target_pairs={{0,4},{1,5},{2,6},{3,7},{4,0},{5,1},{6,2},{7,3},{8,12},{9,13},{10,... | collective-permute-start | bytes 786440 | tf_op jit(solution)/shard_map/ppermute | solution.py:328
  11.7 14.7 %collective-permute-done.4.rest_2_.rest_10_ = f32[16,128,128]{2,1,0:T(8,128)S(1)} collective-permute-done((f32[16,128,128]{2,1,0:T(8,128)}, f32[16,128,128]{2,1,0:T(8,128)S(1)}, u32[]{:S(2)}, u32[]{:S(2)}) %collective-permute-start.4) | collective-permute-done | bytes 1048608 | tf_op jit(solution)/shard_map/ppermute | solution.py:328
  29.3 1.9 %collective-permute-start.5 = (f32[3,8,16,128]{3,2,1,0:T(8,128)S(1)}, f32[3,8,16,128]{3,2,1,0:T(8,128)S(1)}, u32[]{:S(2)}, u32[]{:S(2)}) collective-permute-start(f32[3,8,16,128]{3,2,1,0:T(8,128)S(1)} %get-tuple-element.51), channel_id=1, source_target_pairs={{0,7},{1,6},{2,5},{3,4},{4,3},{5,2},{6,1},{7,0},{8,15},{9,14},{10,... | collective-permute-start | bytes 589832 | tf_op jit(solution)/shard_map/ppermute | solution.py:328
  31.3 6.9 %collective-permute-done.5.rest_0_ = f32[3,8,16,128]{3,2,1,0:T(8,128)S(1)} collective-permute-done((f32[3,8,16,128]{3,2,1,0:T(8,128)S(1)}, f32[3,8,16,128]{3,2,1,0:T(8,128)S(1)}, u32[]{:S(2)}, u32[]{:S(2)}) %collective-permute-start.5) | collective-permute-done | bytes 196640 | tf_op jit(solution)/shard_map/ppermute | solution.py:328
  39.9 2.7 %collective-permute-start.9 = (f32[3,8,16,128]{3,2,1,0:T(8,128)S(1)}, f32[3,8,16,128]{3,2,1,0:T(8,128)S(1)}, u32[]{:S(2)}, u32[]{:S(2)}) collective-permute-start(f32[3,8,16,128]{3,2,1,0:T(8,128)S(1)} %get-tuple-element.60), channel_id=1, source_target_pairs={{0,6},{1,7},{2,4},{3,5},{4,2},{5,3},{6,0},{7,1},{8,14},{9,15},{10,... | collective-permute-start | bytes 589832 | tf_op jit(solution)/shard_map/ppermute | solution.py:328
  43.6 3.4 %collective-permute-start.10 = (f32[3,8,16,128]{3,2,1,0:T(8,128)S(1)}, f32[3,8,16,128]{3,2,1,0:T(8,128)S(1)}, u32[]{:S(2)}, u32[]{:S(2)}) collective-permute-start(f32[3,8,16,128]{3,2,1,0:T(8,128)S(1)} %get-tuple-element.61), channel_id=1, source_target_pairs={{0,2},{1,3},{2,0},{3,1},{4,6},{5,7},{6,4},{7,5},{8,10},{9,11},{10,... | collective-permute-start | bytes 589832 | tf_op jit(solution)/shard_map/ppermute | solution.py:328
  47.9 1.8 %collective-permute-start.12 = (f32[3,8,16,128]{3,2,1,0:T(8,128)S(1)}, f32[3,8,16,128]{3,2,1,0:T(8,128)S(1)}, u32[]{:S(2)}, u32[]{:S(2)}) collective-permute-start(f32[3,8,16,128]{3,2,1,0:T(8,128)S(1)} %get-tuple-element.63), channel_id=1, source_target_pairs={{0,3},{1,2},{2,1},{3,0},{4,7},{5,6},{6,5},{7,4},{8,11},{9,10},{10,... | collective-permute-start | bytes 589832 | tf_op jit(solution)/shard_map/ppermute | solution.py:328
  49.7 5.0 %collective-permute-start.13 = (f32[3,8,16,128]{3,2,1,0:T(8,128)S(1)}, f32[3,8,16,128]{3,2,1,0:T(8,128)S(1)}, u32[]{:S(2)}, u32[]{:S(2)}) collective-permute-start(f32[3,8,16,128]{3,2,1,0:T(8,128)S(1)} %get-tuple-element.64), channel_id=1, source_target_pairs={{0,4},{1,5},{2,6},{3,7},{4,0},{5,1},{6,2},{7,3},{8,12},{9,13},{10,... | collective-permute-start | bytes 589832 | tf_op jit(solution)/shard_map/ppermute | solution.py:328
  54.6 6.6 %collective-permute-done.11.rest_4_ = f32[3,8,16,128]{3,2,1,0:T(8,128)S(1)} collective-permute-done((f32[3,8,16,128]{3,2,1,0:T(8,128)S(1)}, f32[3,8,16,128]{3,2,1,0:T(8,128)S(1)}, u32[]{:S(2)}, u32[]{:S(2)}) %collective-permute-start.11) | collective-permute-done | bytes 196640 | tf_op jit(solution)/shard_map/ppermute | solution.py:328
  61.2 8.4 %collective-permute-done.13.rest_6_ = f32[3,8,16,128]{3,2,1,0:T(8,128)S(1)} collective-permute-done((f32[3,8,16,128]{3,2,1,0:T(8,128)S(1)}, f32[3,8,16,128]{3,2,1,0:T(8,128)S(1)}, u32[]{:S(2)}, u32[]{:S(2)}) %collective-permute-start.13) | collective-permute-done | bytes 196640 | tf_op jit(solution)/shard_map/ppermute | solution.py:328
  71.0 2.8 %collective-permute-start.15 = (f32[3,8,16,128]{3,2,1,0:T(8,128)S(1)}, f32[3,8,16,128]{3,2,1,0:T(8,128)S(1)}, u32[]{:S(2)}, u32[]{:S(2)}) collective-permute-start(f32[3,8,16,128]{3,2,1,0:T(8,128)S(1)} %get-tuple-element.67), channel_id=1, source_target_pairs={{0,7},{1,6},{2,5},{3,4},{4,3},{5,2},{6,1},{7,0},{8,15},{9,14},{10,... | collective-permute-start | bytes 589832 | tf_op jit(solution)/shard_map/ppermute | solution.py:328
  75.3 2.8 %collective-permute-start.19 = (f32[3,8,16,128]{3,2,1,0:T(8,128)S(1)}, f32[3,8,16,128]{3,2,1,0:T(8,128)S(1)}, u32[]{:S(2)}, u32[]{:S(2)}) collective-permute-start(f32[3,8,16,128]{3,2,1,0:T(8,128)S(1)} %get-tuple-element.71), channel_id=1, source_target_pairs={{0,5},{1,4},{2,7},{3,6},{4,1},{5,0},{6,3},{7,2},{8,13},{9,12},{10,... | collective-permute-start | bytes 589832 | tf_op jit(solution)/shard_map/ppermute | solution.py:328
  78.1 1.5 %collective-permute-done.15.rest_1_ = f32[3,8,16,128]{3,2,1,0:T(8,128)S(1)} collective-permute-done((f32[3,8,16,128]{3,2,1,0:T(8,128)S(1)}, f32[3,8,16,128]{3,2,1,0:T(8,128)S(1)}, u32[]{:S(2)}, u32[]{:S(2)}) %collective-permute-start.15) | collective-permute-done | bytes 196640 | tf_op jit(solution)/shard_map/ppermute | solution.py:328
  79.6 2.2 %collective-permute-start.20 = (f32[3,8,16,128]{3,2,1,0:T(8,128)S(1)}, f32[3,8,16,128]{3,2,1,0:T(8,128)S(1)}, u32[]{:S(2)}, u32[]{:S(2)}) collective-permute-start(f32[3,8,16,128]{3,2,1,0:T(8,128)S(1)} %get-tuple-element.72), channel_id=1, source_target_pairs={{0,4},{1,5},{2,6},{3,7},{4,0},{5,1},{6,2},{7,3},{8,12},{9,13},{10,... | collective-permute-start | bytes 589832 | tf_op jit(solution)/shard_map/ppermute | solution.py:328
  81.9 3.1 %collective-permute-done.16.rest_2_ = f32[3,8,16,128]{3,2,1,0:T(8,128)S(1)} collective-permute-done((f32[3,8,16,128]{3,2,1,0:T(8,128)S(1)}, f32[3,8,16,128]{3,2,1,0:T(8,128)S(1)}, u32[]{:S(2)}, u32[]{:S(2)}) %collective-permute-start.16) | collective-permute-done | bytes 196640 | tf_op jit(solution)/shard_map/ppermute | solution.py:328
  85.0 4.2 %collective-permute-done.17.rest_3_ = f32[3,8,16,128]{3,2,1,0:T(8,128)S(1)} collective-permute-done((f32[3,8,16,128]{3,2,1,0:T(8,128)S(1)}, f32[3,8,16,128]{3,2,1,0:T(8,128)S(1)}, u32[]{:S(2)}, u32[]{:S(2)}) %collective-permute-start.17) | collective-permute-done | bytes 196640 | tf_op jit(solution)/shard_map/ppermute | solution.py:328
  89.1 6.2 %collective-permute-done.18.rest_4_ = f32[3,8,16,128]{3,2,1,0:T(8,128)S(1)} collective-permute-done((f32[3,8,16,128]{3,2,1,0:T(8,128)S(1)}, f32[3,8,16,128]{3,2,1,0:T(8,128)S(1)}, u32[]{:S(2)}, u32[]{:S(2)}) %collective-permute-start.18) | collective-permute-done | bytes 196640 | tf_op jit(solution)/shard_map/ppermute | solution.py:328
  95.3 6.9 %collective-permute-done.19.rest_5_ = f32[3,8,16,128]{3,2,1,0:T(8,128)S(1)} collective-permute-done((f32[3,8,16,128]{3,2,1,0:T(8,128)S(1)}, f32[3,8,16,128]{3,2,1,0:T(8,128)S(1)}, u32[]{:S(2)}, u32[]{:S(2)}) %collective-permute-start.19) | collective-permute-done | bytes 196640 | tf_op jit(solution)/shard_map/ppermute | solution.py:328
  102.3 4.8 %collective-permute-done.20.rest_6_ = f32[3,8,16,128]{3,2,1,0:T(8,128)S(1)} collective-permute-done((f32[3,8,16,128]{3,2,1,0:T(8,128)S(1)}, f32[3,8,16,128]{3,2,1,0:T(8,128)S(1)}, u32[]{:S(2)}, u32[]{:S(2)}) %collective-permute-start.20) | collective-permute-done | bytes 196640 | tf_op jit(solution)/shard_map/ppermute | solution.py:328
  107.1 1.6 %shard_map.32 = (f32[16,128,128]{2,1,0:T(8,128)S(1)}, f32[16,128,128]{2,1,0:T(8,128)S(1)}, f32[16,128,128]{2,1,0:T(8,128)S(1)}) custom-call(f32[128,128]{1,0:T(8,128)S(1)} %copy-done.2, f32[3,8,16,128]{3,2,1,0:T(8,128)S(1)} %collective-permute-done.14.rest_0_, f32[3,8,16,128]{3,2,1,0:T(8,128)S(1)} %collective-permute-done.15.rest_1_, ...), custom_call_target="tpu_custom_call" | custom-call | tf_op jit(solution)/shard_map/pallas_call | solution.py:343
  112.0 2.3 %collective-permute-start.23 = (f32[1,32,16,128]{3,2,1,0:T(8,128)S(1)}, f32[1,32,16,128]{3,2,1,0:T(8,128)S(1)}, u32[]{:S(2)}, u32[]{:S(2)}) collective-permute-start(f32[1,32,16,128]{3,2,1,0:T(8,128)S(1)} %get-tuple-element.76), channel_id=1, source_target_pairs={{0,2},{1,3},{2,0},{3,1},{4,6},{5,7},{6,4},{7,5},{8,10},{9,11},{10,... | collective-permute-start | bytes 786440 | tf_op jit(solution)/shard_map/ppermute | solution.py:328
  114.3 15.0 %collective-permute-done.21.rest_0_ = f32[1,32,16,128]{3,2,1,0:T(8,128)S(1)} collective-permute-done((f32[1,32,16,128]{3,2,1,0:T(8,128)S(1)}, f32[1,32,16,128]{3,2,1,0:T(8,128)S(1)}, u32[]{:S(2)}, u32[]{:S(2)}) %collective-permute-start.21) | collective-permute-done | bytes 262176 | tf_op jit(solution)/shard_map/ppermute | solution.py:328
  131.6 1.7 %collective-permute-done.24.second_ref = f32[16,128,128]{2,1,0:T(8,128)S(1)} collective-permute-done((f32[16,128,128]{2,1,0:T(8,128)S(1)}, f32[16,128,128]{2,1,0:T(8,128)S(1)}, u32[]{:S(2)}, u32[]{:S(2)}) %collective-permute-start.24) | collective-permute-done | bytes 1048608 | tf_op jit(solution)/shard_map/ppermute | solution.py:328
  (60 shorter events, 23.5 us)
Async XLA Ops:
  0.0 26.3 %collective-permute-start.4 = (f32[16,128,128]{2,1,0:T(8,128)}, f32[16,128,128]{2,1,0:T(8,128)S(1)}, u32[]{:S(2)}, u32[]{:S(2)}) collective-permute-start(f32[16,128,128]{2,1,0:T(8,128)} %bitcast.2), channel_id=1, source_target_pairs={{0,16},{8,24},{16,0},{24,8},{1,17},{9,25},{17,1},{25,9},{2,18},{10... | collective-permute-start | bytes 3145736 | tf_op jit(solution)/shard_map/ppermute | solution.py:328
  3.0 24.8 %collective-permute-start.3 = (f32[16,128,128]{2,1,0:T(8,128)}, f32[16,128,128]{2,1,0:T(8,128)S(1)}, u32[]{:S(2)}, u32[]{:S(2)}) collective-permute-start(f32[16,128,128]{2,1,0:T(8,128)} %bitcast.3), channel_id=1, source_target_pairs={{0,8},{8,0},{16,24},{24,16},{1,9},{9,1},{17,25},{25,17},{2,10},{10... | collective-permute-start | bytes 3145736 | tf_op jit(solution)/shard_map/ppermute | solution.py:328
  7.5 23.8 %collective-permute-start = (f32[1,32,16,128]{3,2,1,0:T(8,128)S(1)}, f32[1,32,16,128]{3,2,1,0:T(8,128)S(1)}, u32[]{:S(2)}, u32[]{:S(2)}) collective-permute-start(f32[1,32,16,128]{3,2,1,0:T(8,128)S(1)} %get-tuple-element.47), channel_id=1, source_target_pairs={{0,4},{1,5},{2,6},{3,7},{4,0},{5,1},{6,2},{7,3},{8,12},{9,13},{10,... | collective-permute-start | bytes 786440 | tf_op jit(solution)/shard_map/ppermute | solution.py:328
  10.1 21.2 %collective-permute-start.1 = (f32[1,32,16,128]{3,2,1,0:T(8,128)S(1)}, f32[1,32,16,128]{3,2,1,0:T(8,128)S(1)}, u32[]{:S(2)}, u32[]{:S(2)}) collective-permute-start(f32[1,32,16,128]{3,2,1,0:T(8,128)S(1)} %get-tuple-element.48), channel_id=1, source_target_pairs={{0,6},{1,7},{2,4},{3,5},{4,2},{5,3},{6,0},{7,1},{8,14},{9,15},{10,... | collective-permute-start | bytes 786440 | tf_op jit(solution)/shard_map/ppermute | solution.py:328
  11.5 19.8 %collective-permute-start.2 = (f32[1,32,16,128]{3,2,1,0:T(8,128)S(1)}, f32[1,32,16,128]{3,2,1,0:T(8,128)S(1)}, u32[]{:S(2)}, u32[]{:S(2)}) collective-permute-start(f32[1,32,16,128]{3,2,1,0:T(8,128)S(1)} %get-tuple-element.49), channel_id=1, source_target_pairs={{0,2},{1,3},{2,0},{3,1},{4,6},{5,7},{6,4},{7,5},{8,10},{9,11},{10,... | collective-permute-start | bytes 786440 | tf_op jit(solution)/shard_map/ppermute | solution.py:328
  29.3 8.9 %collective-permute-start.5 = (f32[3,8,16,128]{3,2,1,0:T(8,128)S(1)}, f32[3,8,16,128]{3,2,1,0:T(8,128)S(1)}, u32[]{:S(2)}, u32[]{:S(2)}) collective-permute-start(f32[3,8,16,128]{3,2,1,0:T(8,128)S(1)} %get-tuple-element.51), channel_id=1, source_target_pairs={{0,7},{1,6},{2,5},{3,4},{4,3},{5,2},{6,1},{7,0},{8,15},{9,14},{10,... | collective-permute-start | bytes 589832 | tf_op jit(solution)/shard_map/ppermute | solution.py:328
  39.4 8.4 %collective-permute-start.8 = (f32[3,8,16,128]{3,2,1,0:T(8,128)S(1)}, f32[3,8,16,128]{3,2,1,0:T(8,128)S(1)}, u32[]{:S(2)}, u32[]{:S(2)}) collective-permute-start(f32[3,8,16,128]{3,2,1,0:T(8,128)S(1)} %get-tuple-element.59), channel_id=1, source_target_pairs={{0,1},{1,0},{2,3},{3,2},{4,5},{5,4},{6,7},{7,6},{8,9},{9,8},{10,11... | collective-permute-start | bytes 589832 | tf_op jit(solution)/shard_map/ppermute | solution.py:328
  39.9 9.8 %collective-permute-start.9 = (f32[3,8,16,128]{3,2,1,0:T(8,128)S(1)}, f32[3,8,16,128]{3,2,1,0:T(8,128)S(1)}, u32[]{:S(2)}, u32[]{:S(2)}) collective-permute-start(f32[3,8,16,128]{3,2,1,0:T(8,128)S(1)} %get-tuple-element.60), channel_id=1, source_target_pairs={{0,6},{1,7},{2,4},{3,5},{4,2},{5,3},{6,0},{7,1},{8,14},{9,15},{10,... | collective-permute-start | bytes 589832 | tf_op jit(solution)/shard_map/ppermute | solution.py:328
  43.5 31.4 %collective-permute-start.7 = (f32[1,64,16,128]{3,2,1,0:T(8,128)S(1)}, f32[1,64,16,128]{3,2,1,0:T(8,128)S(1)}, u32[]{:S(2)}, u32[]{:S(2)}) collective-permute-start(f32[1,64,16,128]{3,2,1,0:T(8,128)S(1)} %get-tuple-element.57), channel_id=1, source_target_pairs={{0,1},{1,0},{2,3},{3,2},{4,5},{5,4},{6,7},{7,6},{8,9},{9,8},{10,11... | collective-permute-start | bytes 1572872 | tf_op jit(solution)/shard_map/ppermute | solution.py:328
  43.6 11.0 %collective-permute-start.10 = (f32[3,8,16,128]{3,2,1,0:T(8,128)S(1)}, f32[3,8,16,128]{3,2,1,0:T(8,128)S(1)}, u32[]{:S(2)}, u32[]{:S(2)}) collective-permute-start(f32[3,8,16,128]{3,2,1,0:T(8,128)S(1)} %get-tuple-element.61), channel_id=1, source_target_pairs={{0,2},{1,3},{2,0},{3,1},{4,6},{5,7},{6,4},{7,5},{8,10},{9,11},{10,... | collective-permute-start | bytes 589832 | tf_op jit(solution)/shard_map/ppermute | solution.py:328
  47.0 14.2 %collective-permute-start.11 = (f32[3,8,16,128]{3,2,1,0:T(8,128)S(1)}, f32[3,8,16,128]{3,2,1,0:T(8,128)S(1)}, u32[]{:S(2)}, u32[]{:S(2)}) collective-permute-start(f32[3,8,16,128]{3,2,1,0:T(8,128)S(1)} %get-tuple-element.62), channel_id=1, source_target_pairs={{0,5},{1,4},{2,7},{3,6},{4,1},{5,0},{6,3},{7,2},{8,13},{9,12},{10,... | collective-permute-start | bytes 589832 | tf_op jit(solution)/shard_map/ppermute | solution.py:328
  47.9 13.4 %collective-permute-start.12 = (f32[3,8,16,128]{3,2,1,0:T(8,128)S(1)}, f32[3,8,16,128]{3,2,1,0:T(8,128)S(1)}, u32[]{:S(2)}, u32[]{:S(2)}) collective-permute-start(f32[3,8,16,128]{3,2,1,0:T(8,128)S(1)} %get-tuple-element.63), channel_id=1, source_target_pairs={{0,3},{1,2},{2,1},{3,0},{4,7},{5,6},{6,5},{7,4},{8,11},{9,10},{10,... | collective-permute-start | bytes 589832 | tf_op jit(solution)/shard_map/ppermute | solution.py:328
  49.7 20.0 %collective-permute-start.13 = (f32[3,8,16,128]{3,2,1,0:T(8,128)S(1)}, f32[3,8,16,128]{3,2,1,0:T(8,128)S(1)}, u32[]{:S(2)}, u32[]{:S(2)}) collective-permute-start(f32[3,8,16,128]{3,2,1,0:T(8,128)S(1)} %get-tuple-element.64), channel_id=1, source_target_pairs={{0,4},{1,5},{2,6},{3,7},{4,0},{5,1},{6,2},{7,3},{8,12},{9,13},{10,... | collective-permute-start | bytes 589832 | tf_op jit(solution)/shard_map/ppermute | solution.py:328
  71.0 8.6 %collective-permute-start.15 = (f32[3,8,16,128]{3,2,1,0:T(8,128)S(1)}, f32[3,8,16,128]{3,2,1,0:T(8,128)S(1)}, u32[]{:S(2)}, u32[]{:S(2)}) collective-permute-start(f32[3,8,16,128]{3,2,1,0:T(8,128)S(1)} %get-tuple-element.67), channel_id=1, source_target_pairs={{0,7},{1,6},{2,5},{3,4},{4,3},{5,2},{6,1},{7,0},{8,15},{9,14},{10,... | collective-permute-start | bytes 589832 | tf_op jit(solution)/shard_map/ppermute | solution.py:328
  73.8 11.2 %collective-permute-start.16 = (f32[3,8,16,128]{3,2,1,0:T(8,128)S(1)}, f32[3,8,16,128]{3,2,1,0:T(8,128)S(1)}, u32[]{:S(2)}, u32[]{:S(2)}) collective-permute-start(f32[3,8,16,128]{3,2,1,0:T(8,128)S(1)} %get-tuple-element.68), channel_id=1, source_target_pairs={{0,2},{1,3},{2,0},{3,1},{4,6},{5,7},{6,4},{7,5},{8,10},{9,11},{10,... | collective-permute-start | bytes 589832 | tf_op jit(solution)/shard_map/ppermute | solution.py:328
  73.8 15.4 %collective-permute-start.17 = (f32[3,8,16,128]{3,2,1,0:T(8,128)S(1)}, f32[3,8,16,128]{3,2,1,0:T(8,128)S(1)}, u32[]{:S(2)}, u32[]{:S(2)}) collective-permute-start(f32[3,8,16,128]{3,2,1,0:T(8,128)S(1)} %get-tuple-element.69), channel_id=1, source_target_pairs={{0,6},{1,7},{2,4},{3,5},{4,2},{5,3},{6,0},{7,1},{8,14},{9,15},{10,... | collective-permute-start | bytes 589832 | tf_op jit(solution)/shard_map/ppermute | solution.py:328
  74.9 20.4 %collective-permute-start.18 = (f32[3,8,16,128]{3,2,1,0:T(8,128)S(1)}, f32[3,8,16,128]{3,2,1,0:T(8,128)S(1)}, u32[]{:S(2)}, u32[]{:S(2)}) collective-permute-start(f32[3,8,16,128]{3,2,1,0:T(8,128)S(1)} %get-tuple-element.70), channel_id=1, source_target_pairs={{0,3},{1,2},{2,1},{3,0},{4,7},{5,6},{6,5},{7,4},{8,11},{9,10},{10,... | collective-permute-start | bytes 589832 | tf_op jit(solution)/shard_map/ppermute | solution.py:328
  75.3 26.9 %collective-permute-start.19 = (f32[3,8,16,128]{3,2,1,0:T(8,128)S(1)}, f32[3,8,16,128]{3,2,1,0:T(8,128)S(1)}, u32[]{:S(2)}, u32[]{:S(2)}) collective-permute-start(f32[3,8,16,128]{3,2,1,0:T(8,128)S(1)} %get-tuple-element.71), channel_id=1, source_target_pairs={{0,5},{1,4},{2,7},{3,6},{4,1},{5,0},{6,3},{7,2},{8,13},{9,12},{10,... | collective-permute-start | bytes 589832 | tf_op jit(solution)/shard_map/ppermute | solution.py:328
  79.6 27.4 %collective-permute-start.20 = (f32[3,8,16,128]{3,2,1,0:T(8,128)S(1)}, f32[3,8,16,128]{3,2,1,0:T(8,128)S(1)}, u32[]{:S(2)}, u32[]{:S(2)}) collective-permute-start(f32[3,8,16,128]{3,2,1,0:T(8,128)S(1)} %get-tuple-element.72), channel_id=1, source_target_pairs={{0,4},{1,5},{2,6},{3,7},{4,0},{5,1},{6,2},{7,3},{8,12},{9,13},{10,... | collective-permute-start | bytes 589832 | tf_op jit(solution)/shard_map/ppermute | solution.py:328
  108.7 24.7 %collective-permute-start.24 = (f32[16,128,128]{2,1,0:T(8,128)S(1)}, f32[16,128,128]{2,1,0:T(8,128)S(1)}, u32[]{:S(2)}, u32[]{:S(2)}) collective-permute-start(f32[16,128,128]{2,1,0:T(8,128)S(1)} %get-tuple-element.87), channel_id=1, source_target_pairs={{0,8},{8,0},{16,24},{24,16},{1,9},{9,1},{17,25},{25,17},{2,10},{10... | collective-permute-start | bytes 3145736 | tf_op jit(solution)/shard_map/ppermute | solution.py:328
  110.2 24.3 %collective-permute-start.25 = (f32[16,128,128]{2,1,0:T(8,128)S(1)}, f32[16,128,128]{2,1,0:T(8,128)S(1)}, u32[]{:S(2)}, u32[]{:S(2)}) collective-permute-start(f32[16,128,128]{2,1,0:T(8,128)S(1)} %get-tuple-element.88), channel_id=1, source_target_pairs={{0,16},{8,24},{16,0},{24,8},{1,17},{9,25},{17,1},{25,9},{2,18},{10... | collective-permute-start | bytes 3145736 | tf_op jit(solution)/shard_map/ppermute | solution.py:328
  110.8 18.5 %collective-permute-start.21 = (f32[1,32,16,128]{3,2,1,0:T(8,128)S(1)}, f32[1,32,16,128]{3,2,1,0:T(8,128)S(1)}, u32[]{:S(2)}, u32[]{:S(2)}) collective-permute-start(f32[1,32,16,128]{3,2,1,0:T(8,128)S(1)} %get-tuple-element.74), channel_id=1, source_target_pairs={{0,4},{1,5},{2,6},{3,7},{4,0},{5,1},{6,2},{7,3},{8,12},{9,13},{10,... | collective-permute-start | bytes 786440 | tf_op jit(solution)/shard_map/ppermute | solution.py:328
  110.8 18.5 %collective-permute-start.22 = (f32[1,32,16,128]{3,2,1,0:T(8,128)S(1)}, f32[1,32,16,128]{3,2,1,0:T(8,128)S(1)}, u32[]{:S(2)}, u32[]{:S(2)}) collective-permute-start(f32[1,32,16,128]{3,2,1,0:T(8,128)S(1)} %get-tuple-element.75), channel_id=1, source_target_pairs={{0,6},{1,7},{2,4},{3,5},{4,2},{5,3},{6,0},{7,1},{8,14},{9,15},{10,... | collective-permute-start | bytes 786440 | tf_op jit(solution)/shard_map/ppermute | solution.py:328
  112.0 18.6 %collective-permute-start.23 = (f32[1,32,16,128]{3,2,1,0:T(8,128)S(1)}, f32[1,32,16,128]{3,2,1,0:T(8,128)S(1)}, u32[]{:S(2)}, u32[]{:S(2)}) collective-permute-start(f32[1,32,16,128]{3,2,1,0:T(8,128)S(1)} %get-tuple-element.76), channel_id=1, source_target_pairs={{0,2},{1,3},{2,0},{3,1},{4,6},{5,7},{6,4},{7,5},{8,10},{9,11},{10,... | collective-permute-start | bytes 786440 | tf_op jit(solution)/shard_map/ppermute | solution.py:328
  (11 other events, 57.5 us)
